TPU v7x, 32 devices: a whole 2x2x4 slice. The times are simulated.
32 devices in a mesh: dp: 2 (over x), context: 4 (over z), experts: 4 (over y, core).
Axes of the slice: x: 2, y: 2, z: 4, core: 2. Of those that a mesh axis runs over, the one named last changes fastest.
Arguments:
- tokens: bfloat16 [2, 4, 2, 4, 384, 768], P('dp', 'experts', None, 'context'), may hold values from -6 to 6
- cotangent: bfloat16 [2, 4, 2, 4, 384, 768], P('dp', 'experts', None, 'context'), may hold values from -6 to 6
- gates: float32 [2, 4, 2, 4, 384, 2], P('dp', 'experts', None, 'context'), may hold values from 0.3 to 1
- routes: int32 [2, 4, 2, 4, 384, 2], P('dp', 'experts', None, 'context'), may hold values from 0 to 7, all different within a row; in each aligned block of 384 rows (0 to 383, 384 to 767, ..., all dimensions but the last counted through in order) at most 128 rows name the same one
- qkv_weight: bfloat16 [768, 2304], P(None, ('context', 'experts')), may hold values from -0.21875 to 0.21875
- out_weight: bfloat16 [768, 768], P(('context', 'experts')), may hold values from -0.875 to 0.875
- shared_gate: bfloat16 [768, 2048], P(None, ('context', 'experts')), may hold values from -0.21875 to 0.21875
- shared_up: bfloat16 [768, 2048], P(None, ('context', 'experts')), may hold values from -0.21875 to 0.21875
- shared_down: bfloat16 [2048, 768], P(('context', 'experts')), may hold values from -0.1875 to 0.1875
- gains: bfloat16 [2, 768], P(None, ('context', 'experts')), may hold values from 0.5 to 1.5
- expert_gate: bfloat16 [8, 768, 2048], P('experts', None, ('dp', 'context')), may hold values from -0.21875 to 0.21875
- expert_up: bfloat16 [8, 768, 2048], P('experts', None, ('dp', 'context')), may hold values from -0.21875 to 0.21875
- expert_down: bfloat16 [8, 2048, 768], P('experts', ('dp', 'context')), may hold values from -0.1875 to 0.1875
Outputs:
- mixed: bfloat16 [2, 4, 2, 4, 384, 768], P('dp', 'experts', None, 'context')
- input_grad: bfloat16 [2, 4, 2, 4, 384, 768], P('dp', 'experts', None, 'context')
- grad_qkv: float32 [768, 2304], P(None, ('context', 'experts'))
- grad_out: float32 [768, 768], P(('context', 'experts'))
- grad_shared_gate: float32 [768, 2048], P(None, ('context', 'experts'))
- grad_shared_up: float32 [768, 2048], P(None, ('context', 'experts'))
- grad_shared_down: float32 [2048, 768], P(('context', 'experts'))
- grad_gains: float32 [2, 768], P(None, ('context', 'experts'))
- grad_expert_gate: float32 [8, 768, 2048], P('experts', None, ('dp', 'context'))
- grad_expert_up: float32 [8, 768, 2048], P('experts', None, ('dp', 'context'))
- grad_expert_down: float32 [8, 2048, 768], P('experts', ('dp', 'context'))
Inputs may be any that keep to these rules, and one draw needn't show every extreme that they name: `routes`: in each aligned block of 384 rows (one block of one group and micro-batch) no expert is named more than 128 times, a bound that some block reaches; a row's 2 experts differ.
All inputs are finite; a program needn't handle non-finite values.
Results may differ from a plain program's by a relative error of at most 0.019.
Values may be sent and summed in bfloat16 or wider, within the bound.
A program may use at most 384 MiB of HBM per device.

v0:
```python
import jax
import jax.numpy as jnp
from jax import lax
from jax.sharding import PartitionSpec as P

H = 12
HD = 64
PB = 128
CONT = 256


EPSILON = 1e-06


def mdot(former, latter):
    return jnp.dot(former, latter, preferred_element_type=jnp.float32)


def tdot(former, latter):
    return lax.dot_general(
        former, latter, (((0,), (0,)), ((), ())), preferred_element_type=jnp.float32
    )


def ndot(former, latter):
    return lax.dot_general(
        former, latter, (((1,), (1,)), ((), ())), preferred_element_type=jnp.float32
    )


def rotate(values, cosine, sine_part):
    half_size = HD // 2
    shaped = values.reshape(values.shape[0], H, HD)
    former = shaped[..., :half_size]
    latter = shaped[..., half_size:]
    turned = jnp.concatenate(
        [former * cosine - latter * sine_part, latter * cosine + former * sine_part], -1
    )
    return turned.reshape(values.shape)


def slot_table(routes_block, expert_count):
    flat_routes = routes_block.reshape(-1)
    onehot = (flat_routes[:, None] == jnp.arange(expert_count, dtype=jnp.int32)[None, :]).astype(
        jnp.int32
    )
    before = jnp.cumsum(onehot, 0) - onehot
    return jnp.sum(before * onehot, 1).reshape(routes_block.shape)


def silu_parts(values):
    sigma = jax.nn.sigmoid(values)
    return (values * sigma, sigma * (1.0 + values * (1.0 - sigma)))


def on_device(
    tokens,
    cotangent,
    gates,
    routes,
    qkv_weight,
    out_weight,
    shared_gate,
    shared_up,
    shared_down,
    gains,
    expert_gate,
    expert_up,
    expert_down,
):
    micro_count = tokens.shape[2]
    row_count = tokens.shape[4]
    feature_count = tokens.shape[5]
    owners = lax.axis_size("experts")
    local_experts = expert_gate.shape[0]
    total_experts = owners * local_experts
    capacity = row_count * 8 // (3 * total_experts)
    blocks = lax.axis_size("context")
    prompt = blocks * PB
    scaling = HD ** (-0.5)
    w_qkv, w_out, w_sgate, w_sup, w_sdown, w_gains = (
        lax.all_gather(qkv_weight, ("context", "experts"), axis=1, tiled=True),
        lax.all_gather(out_weight, ("context", "experts"), axis=0, tiled=True),
        lax.all_gather(shared_gate, ("context", "experts"), axis=1, tiled=True),
        lax.all_gather(shared_up, ("context", "experts"), axis=1, tiled=True),
        lax.all_gather(shared_down, ("context", "experts"), axis=0, tiled=True),
        lax.all_gather(gains, ("context", "experts"), axis=1, tiled=True),
    )
    e_gate, expert_up_weight, e_down = (
        lax.all_gather(expert_gate, ("dp", "context"), axis=2, tiled=True),
        lax.all_gather(expert_up, ("dp", "context"), axis=2, tiled=True),
        lax.all_gather(expert_down, ("dp", "context"), axis=1, tiled=True),
    )
    gain_one = w_gains[0].astype(jnp.float32)
    gain_two = w_gains[1].astype(jnp.float32)
    here_index = lax.axis_index("context")
    row_ids = jnp.arange(row_count, dtype=jnp.int32)
    query_pos = jnp.where(row_ids < PB, here_index * PB + row_ids, prompt + row_ids - PB)
    key_pos = jnp.arange(prompt + CONT, dtype=jnp.int32)
    allowed = key_pos[None, None, :] <= query_pos[None, :, None]
    half_size = HD // 2
    frequency = 10000.0 ** (-2.0 * jnp.arange(half_size, dtype=jnp.float32) / HD)
    angles = query_pos.astype(jnp.float32)[:, None] * frequency
    cosine = jnp.cos(angles)[:, None, :]
    sine_part = jnp.sin(angles)[:, None, :]
    kept_list = []
    mixed_list = []
    for step_index in range(micro_count):
        inputs = tokens[0, 0, step_index, 0].astype(jnp.float32)
        root_one = lax.rsqrt(jnp.mean(inputs * inputs, -1, keepdims=True) + EPSILON)
        normed_one = (inputs * root_one * gain_one).astype(jnp.bfloat16)
        projected = mdot(normed_one, w_qkv)
        query = rotate(projected[:, :feature_count], cosine, sine_part).astype(jnp.bfloat16)
        key_rows = rotate(
            projected[:, feature_count : 2 * feature_count], cosine, sine_part
        ).astype(jnp.bfloat16)
        value_rows = projected[:, 2 * feature_count :].astype(jnp.bfloat16)
        prompt_key, prompt_value = (
            lax.all_gather(key_rows[:PB], "context", axis=0, tiled=True),
            lax.all_gather(value_rows[:PB], "context", axis=0, tiled=True),
        )
        key_heads = jnp.concatenate([prompt_key, key_rows[PB:]], 0).reshape(prompt + CONT, H, HD)
        value_heads = jnp.concatenate([prompt_value, value_rows[PB:]], 0).reshape(
            prompt + CONT, H, HD
        )
        query_heads = query.reshape(row_count, H, HD)
        scores = (
            jnp.einsum("qhd,khd->hqk", query_heads, key_heads, preferred_element_type=jnp.float32)
            * scaling
        )
        scores = jnp.where(allowed, scores, -1000000000.0)
        highest = jnp.max(scores, -1, keepdims=True)
        weights = jnp.exp(scores - highest)
        total = jnp.sum(weights, -1, keepdims=True)
        log_total = highest + jnp.log(total)
        probs = (weights / total).astype(jnp.bfloat16)
        attended = (
            jnp.einsum("hqk,khd->qhd", probs, value_heads, preferred_element_type=jnp.float32)
            .reshape(row_count, feature_count)
            .astype(jnp.bfloat16)
        )
        hidden = inputs + mdot(attended, w_out)
        root_two = lax.rsqrt(jnp.mean(hidden * hidden, -1, keepdims=True) + EPSILON)
        normed_two = (hidden * root_two * gain_two).astype(jnp.bfloat16)
        side_gate = mdot(normed_two, w_sgate)
        side_up = mdot(normed_two, w_sup)
        side_act = (jax.nn.silu(side_gate) * side_up).astype(jnp.bfloat16)
        side = mdot(side_act, w_sdown)
        route_rows = routes[0, 0, step_index, 0]
        slots = slot_table(route_rows, total_experts)
        flat_dest = (route_rows * capacity + slots).reshape(-1)
        source = (
            jnp.full((total_experts * capacity,), 2 * row_count, jnp.int32)
            .at[flat_dest]
            .set(jnp.arange(2 * row_count, dtype=jnp.int32))
        )
        padded = jnp.concatenate([normed_two, jnp.zeros((1, feature_count), jnp.bfloat16)], 0)
        send = padded[source // 2].reshape(total_experts, capacity, feature_count)
        received = lax.all_to_all(send, "experts", split_axis=0, concat_axis=0, tiled=True)
        count = received.shape[1]
        expert_grouped = received.reshape(owners, local_experts, count, feature_count)
        expert_gate_act = jnp.einsum(
            "send,edf->senf", expert_grouped, e_gate, preferred_element_type=jnp.float32
        )
        expert_up_act = jnp.einsum(
            "send,edf->senf", expert_grouped, expert_up_weight, preferred_element_type=jnp.float32
        )
        expert_hidden_act = (jax.nn.silu(expert_gate_act) * expert_up_act).astype(jnp.bfloat16)
        result = jnp.einsum(
            "senf,efd->send", expert_hidden_act, e_down, preferred_element_type=jnp.float32
        ).astype(jnp.bfloat16)
        expert_out = result.reshape(owners * local_experts, count, feature_count)
        expert_in = received
        returned = lax.all_to_all(
            expert_out, "experts", split_axis=0, concat_axis=0, tiled=True
        ).reshape(-1, feature_count)
        gate_rows = gates[0, 0, step_index, 0]
        picked = returned[flat_dest].reshape(row_count, 2, feature_count).astype(jnp.float32)
        routed = jnp.sum(gate_rows[:, :, None] * picked, 1)
        mixed_list.append((hidden + routed + side).astype(jnp.bfloat16))
        cached = (prompt_key, prompt_value)
        kept_list.append(
            (
                inputs,
                root_one,
                normed_one,
                query,
                key_rows,
                value_rows,
                cached,
                log_total,
                attended,
                hidden,
                root_two,
                normed_two,
                side_gate,
                side_up,
                side_act,
                flat_dest,
                source,
                expert_in,
                gate_rows,
            )
        )
    acc_qkv = jnp.zeros(w_qkv.shape, jnp.float32)
    acc_out = jnp.zeros(w_out.shape, jnp.float32)
    acc_sgate = jnp.zeros(w_sgate.shape, jnp.float32)
    acc_sup = jnp.zeros(w_sup.shape, jnp.float32)
    acc_sdown = jnp.zeros(w_sdown.shape, jnp.float32)
    acc_gain_one = jnp.zeros((feature_count,), jnp.float32)
    acc_gain_two = jnp.zeros((feature_count,), jnp.float32)
    local_egate = jnp.zeros(e_gate.shape, jnp.float32)
    local_expert_up_weight = jnp.zeros(expert_up_weight.shape, jnp.float32)
    local_edown = jnp.zeros(e_down.shape, jnp.float32)
    input_list = []
    for step_index in range(micro_count):
        (
            inputs,
            root_one,
            normed_one,
            query,
            key_rows,
            value_rows,
            cached,
            log_total,
            attended,
            hidden,
            root_two,
            normed_two,
            side_gate,
            side_up,
            side_act,
            flat_dest,
            source,
            expert_in,
            gate_rows,
        ) = kept_list[step_index]
        grad_rows = cotangent[0, 0, step_index, 0].astype(jnp.float32)
        grad_low = grad_rows.astype(jnp.bfloat16)
        acc_sdown = acc_sdown + tdot(side_act, grad_low)
        d_side_act = ndot(grad_low, w_sdown).astype(jnp.bfloat16).astype(jnp.float32)
        silu_side, slope_side = silu_parts(side_gate)
        d_side_gate = (d_side_act * side_up * slope_side).astype(jnp.bfloat16)
        d_side_up = (d_side_act * silu_side).astype(jnp.bfloat16)
        acc_sgate = acc_sgate + tdot(normed_two, d_side_gate)
        acc_sup = acc_sup + tdot(normed_two, d_side_up)
        d_normed_two = ndot(d_side_gate, w_sgate) + ndot(d_side_up, w_sup)
        d_pairs = (
            (gate_rows[:, :, None] * grad_rows[:, None, :])
            .astype(jnp.bfloat16)
            .reshape(2 * row_count, feature_count)
        )
        padded_grad = jnp.concatenate([d_pairs, jnp.zeros((1, feature_count), jnp.bfloat16)], 0)
        grad_send = padded_grad[source].reshape(total_experts, capacity, feature_count)
        grad_in = lax.all_to_all(grad_send, "experts", split_axis=0, concat_axis=0, tiled=True)
        grouped_grad = grad_in.reshape(owners, local_experts, capacity, feature_count)
        grouped = expert_in.reshape(owners, local_experts, capacity, feature_count)
        gate_act = jnp.einsum("send,edf->senf", grouped, e_gate, preferred_element_type=jnp.float32)
        up_act = jnp.einsum(
            "send,edf->senf", grouped, expert_up_weight, preferred_element_type=jnp.float32
        )
        silu_gate, slope_gate = silu_parts(gate_act)
        hidden_act = (silu_gate * up_act).astype(jnp.bfloat16)
        d_hidden_act = (
            jnp.einsum("send,efd->senf", grouped_grad, e_down, preferred_element_type=jnp.float32)
            .astype(jnp.bfloat16)
            .astype(jnp.float32)
        )
        d_gate_act = (d_hidden_act * up_act * slope_gate).astype(jnp.bfloat16)
        d_up_act = (d_hidden_act * silu_gate).astype(jnp.bfloat16)
        step_edown = jnp.einsum(
            "senf,send->efd", hidden_act, grouped_grad, preferred_element_type=jnp.float32
        )
        step_egate = jnp.einsum(
            "send,senf->edf", grouped, d_gate_act, preferred_element_type=jnp.float32
        )
        stepwise_expert_up = jnp.einsum(
            "send,senf->edf", grouped, d_up_act, preferred_element_type=jnp.float32
        )
        local_egate = local_egate + step_egate
        local_expert_up_weight = local_expert_up_weight + stepwise_expert_up
        local_edown = local_edown + step_edown
        d_expert_in = jnp.einsum(
            "senf,edf->send", d_gate_act, e_gate, preferred_element_type=jnp.float32
        ) + jnp.einsum(
            "senf,edf->send", d_up_act, expert_up_weight, preferred_element_type=jnp.float32
        )
        d_expert_in = d_expert_in.astype(jnp.bfloat16).reshape(
            total_experts, capacity, feature_count
        )
        back = lax.all_to_all(
            d_expert_in, "experts", split_axis=0, concat_axis=0, tiled=True
        ).reshape(-1, feature_count)
        d_normed_two = d_normed_two + jnp.sum(
            back[flat_dest].reshape(row_count, 2, feature_count).astype(jnp.float32), 1
        )
        scaled_two = gain_two * d_normed_two
        d_hidden = (
            grad_rows
            + root_two * scaled_two
            - hidden * root_two**3 * jnp.mean(hidden * scaled_two, -1, keepdims=True)
        )
        acc_gain_two = acc_gain_two + jnp.sum(d_normed_two * hidden * root_two, 0)
        d_attn = d_hidden.astype(jnp.bfloat16)
        acc_out = acc_out + tdot(attended, d_attn)
        d_attended = ndot(d_attn, w_out).astype(jnp.bfloat16)
        prompt_key, prompt_value = cached
        key_heads = jnp.concatenate([prompt_key, key_rows[PB:]], 0).reshape(prompt + CONT, H, HD)
        value_heads = jnp.concatenate([prompt_value, value_rows[PB:]], 0).reshape(
            prompt + CONT, H, HD
        )
        query_heads = query.reshape(row_count, H, HD)
        scores = (
            jnp.einsum("qhd,khd->hqk", query_heads, key_heads, preferred_element_type=jnp.float32)
            * scaling
        )
        scores = jnp.where(allowed, scores, -1000000000.0)
        probs = jnp.exp(scores - log_total)
        d_heads = d_attended.reshape(row_count, H, HD)
        d_probs = jnp.einsum(
            "qhd,khd->hqk", d_heads, value_heads, preferred_element_type=jnp.float32
        )
        centre = jnp.sum(probs * d_probs, -1, keepdims=True)
        d_scores = (probs * (d_probs - centre)).astype(jnp.bfloat16)
        d_query = (
            jnp.einsum(
                "hqk,khd->qhd", d_scores, key_heads, preferred_element_type=jnp.float32
            ).reshape(row_count, feature_count)
            * scaling
        )
        d_keys = (
            jnp.einsum(
                "hqk,qhd->khd", d_scores, query_heads, preferred_element_type=jnp.float32
            ).reshape(prompt + CONT, feature_count)
            * scaling
        )
        d_values = jnp.einsum(
            "hqk,qhd->khd", probs.astype(jnp.bfloat16), d_heads, preferred_element_type=jnp.float32
        ).reshape(prompt + CONT, feature_count)
        own_dkey, own_dvalue = (
            lax.psum_scatter(
                d_keys[:prompt].astype(jnp.bfloat16), "context", scatter_dimension=0, tiled=True
            ).astype(jnp.float32),
            lax.psum_scatter(
                d_values[:prompt].astype(jnp.bfloat16), "context", scatter_dimension=0, tiled=True
            ).astype(jnp.float32),
        )
        d_key_rows = jnp.concatenate([own_dkey, d_keys[prompt:]], 0)
        d_value_rows = jnp.concatenate([own_dvalue, d_values[prompt:]], 0)
        d_projected = jnp.concatenate(
            [
                rotate(d_query, cosine, -sine_part).astype(jnp.bfloat16),
                rotate(d_key_rows, cosine, -sine_part).astype(jnp.bfloat16),
                d_value_rows.astype(jnp.bfloat16),
            ],
            1,
        )
        acc_qkv = acc_qkv + tdot(normed_one, d_projected)
        d_normed_one = ndot(d_projected, w_qkv)
        scaled_one = gain_one * d_normed_one
        d_inputs = (
            d_hidden
            + root_one * scaled_one
            - inputs * root_one**3 * jnp.mean(inputs * scaled_one, -1, keepdims=True)
        )
        acc_gain_one = acc_gain_one + jnp.sum(d_normed_one * inputs * root_one, 0)
        input_list.append(d_inputs.astype(jnp.bfloat16))
    sharded_expert_gate, sharded_expert_up, sharded_expert_down = (
        lax.psum_scatter(
            local_egate.astype(jnp.bfloat16), ("dp", "context"), scatter_dimension=2, tiled=True
        ).astype(jnp.float32),
        lax.psum_scatter(
            local_expert_up_weight.astype(jnp.bfloat16),
            ("dp", "context"),
            scatter_dimension=2,
            tiled=True,
        ).astype(jnp.float32),
        lax.psum_scatter(
            local_edown.astype(jnp.bfloat16), ("dp", "context"), scatter_dimension=1, tiled=True
        ).astype(jnp.float32),
    )
    acc_gains = jnp.stack([acc_gain_one, acc_gain_two], 0)
    dense_shards = (
        lax.psum_scatter(acc_qkv, ("context", "experts"), scatter_dimension=1, tiled=True),
        lax.psum_scatter(acc_out, ("context", "experts"), scatter_dimension=0, tiled=True),
        lax.psum_scatter(acc_sgate, ("context", "experts"), scatter_dimension=1, tiled=True),
        lax.psum_scatter(acc_sup, ("context", "experts"), scatter_dimension=1, tiled=True),
        lax.psum_scatter(acc_sdown, ("context", "experts"), scatter_dimension=0, tiled=True),
        lax.psum_scatter(acc_gains, ("context", "experts"), scatter_dimension=1, tiled=True),
    )
    grad_qkv, grad_out, grad_sgate, grad_sup, grad_sdown, grad_gains = (
        lax.psum(dense_shards[0].astype(jnp.bfloat16), "dp").astype(jnp.float32),
        lax.psum(dense_shards[1].astype(jnp.bfloat16), "dp").astype(jnp.float32),
        lax.psum(dense_shards[2].astype(jnp.bfloat16), "dp").astype(jnp.float32),
        lax.psum(dense_shards[3].astype(jnp.bfloat16), "dp").astype(jnp.float32),
        lax.psum(dense_shards[4].astype(jnp.bfloat16), "dp").astype(jnp.float32),
        lax.psum(dense_shards[5].astype(jnp.bfloat16), "dp").astype(jnp.float32),
    )
    mixed = jnp.stack(mixed_list, 0).reshape(tokens.shape)
    input_grad = jnp.stack(input_list, 0).reshape(tokens.shape)
    return (
        mixed,
        input_grad,
        grad_qkv,
        grad_out,
        grad_sgate,
        grad_sup,
        grad_sdown,
        grad_gains,
        sharded_expert_gate,
        sharded_expert_up,
        sharded_expert_down,
    )


def solution(mesh):
    return jax.shard_map(
        on_device,
        mesh=mesh,
        in_specs=(
            P("dp", "experts", None, "context", None, None),
            P("dp", "experts", None, "context", None, None),
            P("dp", "experts", None, "context", None, None),
            P("dp", "experts", None, "context", None, None),
            P(None, ("context", "experts")),
            P(("context", "experts"), None),
            P(None, ("context", "experts")),
            P(None, ("context", "experts")),
            P(("context", "experts"), None),
            P(None, ("context", "experts")),
            P("experts", None, ("dp", "context")),
            P("experts", None, ("dp", "context")),
            P("experts", ("dp", "context"), None),
        ),
        out_specs=(
            P("dp", "experts", None, "context", None, None),
            P("dp", "experts", None, "context", None, None),
            P(None, ("context", "experts")),
            P(("context", "experts"), None),
            P(None, ("context", "experts")),
            P(None, ("context", "experts")),
            P(("context", "experts"), None),
            P(None, ("context", "experts")),
            P("experts", None, ("dp", "context")),
            P("experts", None, ("dp", "context")),
            P("experts", ("dp", "context"), None),
        ),
        check_vma=False,
    )
```

profile of v0, /device:TPU:0, one launch (start us, length us, event | category | flops | bytes accessed | tf_op | source)
XLA Modules:
  0.0 1778.9 jit_solution(18386080788179844725)
XLA Ops:
  15.3 23.0 %all-gather = bf16[16,48,2]{1,2,0:T(2,128)(2,1)S(1)} all-gather(bf16[1,48,2]{1,2,0:T(2,128)(2,1)S(1)} %bitcast.476), channel_id=1, replica_groups=mesh['dp'=2,'context'=4,'experts'=4] {'context','experts'}, dimensions={0}, use_global_device_ids=true | all-gather | bytes 3264 | tf_op jit(solution)/shard_map/all_gather | solution.py:87
  135.5 19.8 %all_gather.41 = bf16[512,768]{1,0:T(8,128)(2,1)S(1)} all-gather(bf16[128,768]{1,0:T(8,128)(2,1)S(1)} %copy-done.79), channel_id=1, replica_groups=mesh['dp'=2,'context'=4,'experts'=4] {'context'}, dimensions={0}, use_global_device_ids=true | all-gather | bytes 983040 | tf_op jit(solution)/shard_map/all_gather | solution.py:120
  158.0 22.3 %all_gather.42 = bf16[512,768]{0,1:T(8,128)(2,1)S(1)} all-gather(bf16[128,768]{0,1:T(8,128)(2,1)} %bitcast.459), channel_id=1, replica_groups=mesh['dp'=2,'context'=4,'experts'=4] {'context'}, dimensions={0}, use_global_device_ids=true | all-gather | bytes 983040 | tf_op jit(solution)/shard_map/all_gather | solution.py:119
  196.9 17.7 all_gather.50
  216.1 33.7 %all_gather.51 = bf16[512,768]{0,1:T(8,128)(2,1)} all-gather(bf16[128,768]{0,1:T(8,128)(2,1)S(1)} %bitcast.458), channel_id=1, replica_groups=mesh['dp'=2,'context'=4,'experts'=4] {'context'}, dimensions={0}, use_global_device_ids=true | all-gather | bytes 983040 | tf_op jit(solution)/shard_map/all_gather | solution.py:119
  287.5 28.6 %all-gather.16.cloned.1.call-done = bf16[2,768,2048]{2,1,0:T(8,128)(2,1)} async-done(((bf16[2,768,256]{2,1,0:T(8,128)(2,1)}), bf16[2,768,2048]{2,1,0:T(8,128)(2,1)}) %all-gather.16.cloned.1.call-update) | async-done | bytes 6291472 | tf_op jit(solution)/shard_map/all_gather | solution.py:91
  324.6 91.6 %all-gather.14.cloned.1.call-done = bf16[2,768,2048]{2,1,0:T(8,128)(2,1)} async-done(((bf16[2,768,256]{2,1,0:T(8,128)(2,1)}), bf16[2,768,2048]{2,1,0:T(8,128)(2,1)}) %all-gather.14.cloned.1.call-update) | async-done | bytes 6291472 | tf_op jit(solution)/shard_map/all_gather | solution.py:90
  424.6 90.9 %all-gather.18.cloned.1.call-done = bf16[2,2048,768]{2,1,0:T(8,128)(2,1)} async-done(((bf16[2,256,768]{2,1,0:T(8,128)(2,1)}), bf16[2,2048,768]{2,1,0:T(8,128)(2,1)}) %all-gather.18.cloned.1.call-update) | async-done | bytes 6291472 | tf_op jit(solution)/shard_map/all_gather | solution.py:92
  515.5 13.5 fusion.11
  545.0 23.2 %all-gather.22.cloned.1.call-done = bf16[768,2048]{1,0:T(8,128)(2,1)} async-done(((bf16[768,128]{1,0:T(8,128)(2,1)}), bf16[768,2048]{1,0:T(8,128)(2,1)}) %all-gather.22.cloned.1.call-update) | async-done | bytes 3145744 | tf_op jit(solution)/shard_map/all_gather | solution.py:85
  648.6 13.9 fusion.8
  728.5 14.4 multiply_reduce_fusion.1
  757.3 14.4 multiply_reduce_fusion
  889.8 12.7 fusion.2
  931.4 13.2 fusion
  967.4 27.3 %all-to-all-done.1 = bf16[8,128,768]{2,1,0:T(8,128)(2,1)S(1)} async-done(((bf16[8,128,768]{2,1,0:T(8,128)(2,1)}), bf16[8,128,768]{2,1,0:T(8,128)(2,1)S(1)}, u32[]{:S(2)}, u32[]{:S(2)}) %all-to-all-start.1) | async-done | bytes 1572896 | tf_op jit(solution)/shard_map/all_to_all | solution.py:174
  1038.6 82.0 %reduce-scatter.30.cloned.1.call-done = f32[768,128]{1,0:T(8,128)} async-done(((f32[768,2048]{1,0:T(8,128)}), f32[768,128]{1,0:T(8,128)}) %reduce-scatter.30.cloned.1.call-update) | async-done | bytes 393232 | tf_op jit(solution)/shard_map/reduce_scatter | solution.py:387
  1122.3 87.2 %reduce-scatter.32.cloned.1.call-done = f32[128,768]{1,0:T(8,128)} async-done(((f32[2048,768]{1,0:T(8,128)}), f32[128,768]{1,0:T(8,128)}) %reduce-scatter.32.cloned.1.call-update) | async-done | bytes 393232 | tf_op jit(solution)/shard_map/reduce_scatter | solution.py:388
  1211.1 91.4 %reduce-scatter.24.cloned.1.call-done = f32[768,144]{0,1:T(8,128)} async-done(((f32[768,2304]{0,1:T(8,128)}), f32[768,144]{0,1:T(8,128)}) %reduce-scatter.24.cloned.1.call-update) | async-done | bytes 442384 | tf_op jit(solution)/shard_map/reduce_scatter | solution.py:384
  1309.1 52.9 %reduce-scatter.48.cloned.1.call-done = f32[48,2]{1,0:T(8,128)} async-done(((f32[768,2]{1,0:T(8,128)}), f32[48,2]{1,0:T(8,128)}) %reduce-scatter.48.cloned.1.call-update) | async-done | bytes 400
  1368.3 114.7 %reduce-scatter.34.cloned.1.call-done = bf16[2,768,256]{2,1,0:T(8,128)(2,1)} async-done(((bf16[2,768,2048]{2,1,0:T(8,128)(2,1)}), bf16[2,768,256]{2,1,0:T(8,128)(2,1)}) %reduce-scatter.34.cloned.1.call-update) | async-done | bytes 786448 | tf_op jit(solution)/shard_map/reduce_scatter | solution.py:369
  1485.5 118.6 %reduce-scatter.36.cloned.1.call-done = bf16[2,768,256]{2,1,0:T(8,128)(2,1)} async-done(((bf16[2,768,2048]{2,1,0:T(8,128)(2,1)}), bf16[2,768,256]{2,1,0:T(8,128)(2,1)}) %reduce-scatter.36.cloned.1.call-update) | async-done | bytes 786448 | tf_op jit(solution)/shard_map/reduce_scatter | solution.py:372
  1606.5 118.3 %reduce-scatter.38.cloned.1.call-done = bf16[2,256,768]{2,1,0:T(8,128)(2,1)} async-done(((bf16[2,2048,768]{2,1,0:T(8,128)(2,1)}), bf16[2,256,768]{2,1,0:T(8,128)(2,1)}) %reduce-scatter.38.cloned.1.call-update) | async-done | bytes 786448 | tf_op jit(solution)/shard_map/reduce_scatter | solution.py:378
  1727.2 37.1 %all-reduce.7.cloned.1.call-done = (bf16[768,144]{0,1:T(8,128)(2,1)}, bf16[48,768]{1,0:T(8,128)(2,1)}, bf16[768,128]{1,0:T(8,128)(2,1)}, bf16[768,128]{1,0:T(8,128)(2,1)}, bf16[128,768]{1,0:T(8,128)(2,1)}) async-done(((bf16[768,144]{0,1:T(8,128)(2,1)}, bf16[48,768]{1,0:T(8,128)(2,1)}, bf16[768,128]{1,0:T(8,128)(2,1)}, bf16[768,128]{1,0:T(8,128)(2,1)}, bf16[128,768]{1,0:T(8,128)(2,1)}), ...) | async-done | bytes 884752 | tf_op jit(solution)/shard_map/psum | solution.py:392
  (606 shorter events, 599.7 us)
Async XLA Ops:
  7.2 88.2 %all-gather.24.cloned.1.call-start = ((), (), s32[]{:S(2)}) async-start(), calls=%async_computation.28 | async-start | bytes 3342336 | tf_op jit(solution)/shard_map/all_gather | solution.py:86
  7.9 98.9 %all-gather.10.cloned.1.call-start = ((), (), s32[]{:S(2)}) async-start(), calls=%async_computation.21 | async-start | bytes 3760128 | tf_op jit(solution)/shard_map/all_gather | solution.py:82
  8.7 184.5 %all-gather.12.cloned.1.call-start = ((), (), s32[]{:S(2)}) async-start(), calls=%async_computation.22 | async-start | bytes 1253376 | tf_op jit(solution)/shard_map/all_gather | solution.py:83
  9.4 268.5 %all-gather.20.cloned.1.call-start = ((), (), s32[]{:S(2)}) async-start(), calls=%async_computation.26 | async-start | bytes 3342336 | tf_op jit(solution)/shard_map/all_gather | solution.py:84
  10.0 306.1 %all-gather.16.cloned.1.call-start = ((), (), s32[]{:S(2)}) async-start(), calls=%async_computation.24 | async-start | bytes 7077888 | tf_op jit(solution)/shard_map/all_gather | solution.py:91
  10.6 405.6 %all-gather.14.cloned.1.call-start = ((), (), s32[]{:S(2)}) async-start(), calls=%async_computation.23 | async-start | bytes 7077888 | tf_op jit(solution)/shard_map/all_gather | solution.py:90
  11.2 504.4 %all-gather.18.cloned.1.call-start = ((), (), s32[]{:S(2)}) async-start(), calls=%async_computation.25 | async-start | bytes 7077888 | tf_op jit(solution)/shard_map/all_gather | solution.py:92
  11.9 556.3 %all-gather.22.cloned.1.call-start = ((), (), s32[]{:S(2)}) async-start(), calls=%async_computation.27 | async-start | bytes 3342336 | tf_op jit(solution)/shard_map/all_gather | solution.py:85
  283.4 141.2 %all-to-all-start.4 = ((bf16[8,128,768]{2,1,0:T(8,128)(2,1)}), bf16[8,128,768]{2,1,0:T(8,128)(2,1)S(1)}, u32[]{:S(2)}, u32[]{:S(2)}) async-start(bf16[8,128,768]{2,1,0:T(8,128)(2,1)} %bitcast.428), calls=%async_computation.4 | async-start | bytes 3145728 | tf_op jit(solution)/shard_map/all_to_all | solution.py:255
  680.9 172.0 %reduce-scatter.40.cloned.1.call-start = ((), (), s32[]{:S(2)}) async-start(), calls=%async_computation.37 | async-start | bytes 983040
  757.2 96.9 %reduce-scatter.44.cloned.1.call-start = ((), (), s32[]{:S(2)}) async-start(), calls=%async_computation.39 | async-start | bytes 983040
  785.7 71.2 %reduce-scatter.46.cloned.1.call-start = ((), (), s32[]{:S(2)}) async-start(), calls=%async_computation.40 | async-start | bytes 983040
  797.6 61.9 %reduce-scatter.42.cloned.1.call-start = ((), (), s32[]{:S(2)}) async-start(), calls=%async_computation.38 | async-start | bytes 983040
  809.9 225.3 %reduce-scatter.26.cloned.1.call-start = ((), (), s32[]{:S(2)}) async-start(), calls=%async_computation.30 | async-start | bytes 2506752 | tf_op jit(solution)/shard_map/reduce_scatter | solution.py:385
  814.1 222.8 %reduce-scatter.28.cloned.1.call-start = ((), (), s32[]{:S(2)}) async-start(), calls=%async_computation.31 | async-start | bytes 6684672 | tf_op jit(solution)/shard_map/reduce_scatter | solution.py:386
  823.1 297.5 %reduce-scatter.30.cloned.1.call-start = ((), (), s32[]{:S(2)}) async-start(), calls=%async_computation.32 | async-start | bytes 6684672 | tf_op jit(solution)/shard_map/reduce_scatter | solution.py:387
  832.4 377.0 %reduce-scatter.32.cloned.1.call-start = ((), (), s32[]{:S(2)}) async-start(), calls=%async_computation.33 | async-start | bytes 6684672 | tf_op jit(solution)/shard_map/reduce_scatter | solution.py:388
  840.4 462.1 %reduce-scatter.24.cloned.1.call-start = ((), (), s32[]{:S(2)}) async-start(), calls=%async_computation.29 | async-start | bytes 7520256 | tf_op jit(solution)/shard_map/reduce_scatter | solution.py:384
  872.9 489.1 %reduce-scatter.48.cloned.1.call-start = ((), (), s32[]{:S(2)}) async-start(), calls=%async_computation.41 | async-start | bytes 417792
  889.7 593.4 %reduce-scatter.34.cloned.1.call-start = ((), (), s32[]{:S(2)}) async-start(), calls=%async_computation.34 | async-start | bytes 7077888 | tf_op jit(solution)/shard_map/reduce_scatter | solution.py:369
  902.4 701.6 %reduce-scatter.36.cloned.1.call-start = ((), (), s32[]{:S(2)}) async-start(), calls=%async_computation.35 | async-start | bytes 7077888 | tf_op jit(solution)/shard_map/reduce_scatter | solution.py:372
  919.8 805.0 %reduce-scatter.38.cloned.1.call-start = ((), (), s32[]{:S(2)}) async-start(), calls=%async_computation.36 | async-start | bytes 7077888 | tf_op jit(solution)/shard_map/reduce_scatter | solution.py:378
  954.1 40.7 %all-to-all-start.1 = ((bf16[8,128,768]{2,1,0:T(8,128)(2,1)}), bf16[8,128,768]{2,1,0:T(8,128)(2,1)S(1)}, u32[]{:S(2)}, u32[]{:S(2)}) async-start(bf16[8,128,768]{2,1,0:T(8,128)(2,1)} %bitcast.28), calls=%async_computation.1 | async-start | bytes 3145728 | tf_op jit(solution)/shard_map/all_to_all | solution.py:174
  998.5 765.8 %all-reduce.7.cloned.1.call-start = ((), (), s32[]{:S(2)}) async-start(), calls=%async_computation.42 | async-start | bytes 1769472 | tf_op jit(solution)/shard_map/psum | solution.py:392
  (162 other events, 3298.5 us)
Sparse Core Ops, SparseCore 0:
  10.3 48.1 all-gather.23
  60.7 46.0 all-gather.9
  109.1 38.4 all-gather.11
  149.7 55.4 all-gather.19
  207.0 109.0 all-gather.15
  318.0 98.1 all-gather.13
  418.3 97.2 all-gather.17
  517.7 50.5 all-gather.21
  757.3 24.0 reduce-scatter.39
  785.8 24.0 reduce-scatter.43
  812.2 22.4 reduce-scatter.45
  836.9 22.5 reduce-scatter.41
  863.3 62.2 reduce-scatter.25
  929.8 101.9 reduce-scatter.27
  1035.6 84.9 reduce-scatter.29
  1124.9 84.4 reduce-scatter.31
  1213.3 89.2 reduce-scatter.23
  1306.9 55.0 reduce-scatter.47
  1365.6 117.4 reduce-scatter.33
  1486.5 117.5 reduce-scatter.35
  1607.7 117.0 reduce-scatter.37
  1728.0 36.3 all-reduce.6
where the time goes:
time: 1790 us; the launch traced here: 1780 us
  waiting for transfers between devices  1010 us (56%)
  matrix products  350 us (20%)
  local copies, waits for them, and re-layouts  153 us (9%)
  blocking collectives  122 us (7%)
  other arithmetic  98.5 us (6%)
  starting transfers between devices  33.2 us (2%)
    reduce_scatter x1, waiting for transfers between devices, on_device(): lax.psum_scatter(local_expert_up_weight.astype(jnp.bfloat16), ('dp', 'con...  119 us
    reduce_scatter x1, waiting for transfers between devices, on_device(): lax.psum_scatter(local_edown.astype(jnp.bfloat16), ('dp', 'context'), sca...  118 us
    reduce_scatter x1, waiting for transfers between devices, on_device(): lax.psum_scatter(local_egate.astype(jnp.bfloat16), ('dp', 'context'), sca...  115 us
    all_gather x1, waiting for transfers between devices, on_device(): lax.all_gather(expert_gate, ('dp', 'context'), axis=2, tiled=True)  91.6 us
    reduce_scatter x1, waiting for transfers between devices, on_device(): lax.psum_scatter(acc_qkv, ('context', 'experts'), scatter_dimension=1, ti...  91.4 us
    all_gather x1, waiting for transfers between devices, on_device(): lax.all_gather(expert_down, ('dp', 'context'), axis=1, tiled=True)  90.9 us
    reduce_scatter x1, waiting for transfers between devices, on_device(): lax.psum_scatter(acc_sdown, ('context', 'experts'), scatter_dimension=0,...  87.2 us
    reduce_scatter x1, waiting for transfers between devices, on_device(): lax.psum_scatter(acc_sup, ('context', 'experts'), scatter_dimension=1, ti...  82 us
  transfers between devices with their start and end apart: 30, of which 19 were waited for; matrix products, arithmetic and copies ran while one was open for 26% of the time, Pallas kernels for 0%

commit v1 on v0

--- a/solution.py
+++ b/solution.py
@@ -1,7 +1,14 @@
+import functools
+
 import jax
 import jax.numpy as jnp
+import numpy as np
 from jax import lax
+from jax.experimental import pallas as pl
+from jax.experimental.pallas import tpu as pltpu
 from jax.sharding import PartitionSpec as P
+
+DP, CONTEXT, EXPERTS = "dp", "context", "experts"
 
 H = 12
 HD = 64
@@ -53,7 +60,1376 @@
     return (values * sigma, sigma * (1.0 + values * (1.0 - sigma)))
 
 
-def on_device(
+MESH = pl.DeviceIdType.MESH
+MIB = 1024 * 1024
+BF = jnp.bfloat16
+F32 = jnp.float32
+
+
+def remote(source, target, send_sem, recv_sem, **device):
+    return pltpu.make_async_remote_copy(
+        src_ref=source,
+        dst_ref=target,
+        send_sem=send_sem,
+        recv_sem=recv_sem,
+        device_id=device,
+        device_id_type=MESH,
+    )
+
+
+def arrived(slot, recv_sem):
+    remote(slot, slot, recv_sem, recv_sem, context=0).wait_recv()
+
+
+def either(first, second):
+    return jnp.logical_and(first, second)
+
+
+class Place:
+    def __init__(self, sizes):
+        self.depth, self.high_count = sizes
+        self.owners = self.high_count * 2
+        self.x = lax.axis_index(DP)
+        self.z = lax.axis_index(CONTEXT)
+        self.e = lax.axis_index(EXPERTS)
+        self.high = self.e // 2
+        self.low = self.e % 2
+
+    def shard(self, z):
+        return self.x * self.depth + z
+
+    def other_shard(self, z):
+        return (1 - self.x) * self.depth + z
+
+    def peer_high(self, step):
+        return lax.rem(self.high + step, self.high_count)
+
+    def peer_owner(self, step):
+        return lax.rem(self.e + step, self.owners)
+
+    def on_line(self, z):
+        return (z >= 0) & (z < self.depth)
+
+    def greet(self):
+        barrier = pltpu.get_barrier_semaphore()
+
+        def signal(**device):
+            pl.semaphore_signal(barrier, inc=1, device_id=device, device_id_type=MESH)
+
+        signal(dp=1 - self.x)
+        for step in range(1, self.owners):
+            signal(experts=self.peer_owner(step))
+        pl.when(self.z > 0)(lambda: signal(context=self.z - 1))
+        pl.when(self.z < self.depth - 1)(lambda: signal(context=self.z + 1))
+        count = 1 + self.owners - 1
+        count += jnp.where(self.z > 0, 1, 0) + jnp.where(self.z < self.depth - 1, 1, 0)
+        pl.semaphore_wait(barrier, count)
+
+
+class Line:
+    def __init__(self, place, own, slot, send_sem, recv_sem):
+        self.place, self.own, self.slot = place, own, slot
+        self.send_sem, self.recv_sem = send_sem, recv_sem
+
+    def _copy(self, direction, step):
+        place = self.place
+        z = place.z - direction * step
+        source = self.own if step == 0 else self.slot(z)
+        return remote(
+            source,
+            self.slot(z),
+            self.send_sem.at[(direction + 1) // 2, step],
+            self.recv_sem.at[z],
+            context=place.z + direction,
+        )
+
+    def _valid(self, direction, step):
+        place = self.place
+        return place.on_line(place.z - direction * step) & place.on_line(place.z + direction)
+
+    def send(self, direction, step):
+        if step < self.place.depth - 1:
+            pl.when(self._valid(direction, step))(lambda: self._copy(direction, step).start())
+
+    def start(self):
+        self.send(1, 0)
+        self.send(-1, 0)
+
+    def hop(self, step, then=None):
+        for direction in (1, -1):
+            z = self.place.z - direction * (step + 1)
+
+            def body(direction=direction, z=z):
+                arrived(self.slot(z), self.recv_sem.at[z])
+                self.send(direction, step + 1)
+                if then is not None:
+                    then(z)
+
+            pl.when(self.place.on_line(z))(body)
+
+    def drain(self):
+        for direction in (1, -1):
+            for step in range(self.place.depth - 1):
+                pl.when(self._valid(direction, step))(
+                    lambda d=direction, s=step: self._copy(d, s).wait_send()
+                )
+
+
+class DenseGather:
+    def __init__(self, place, own, slot, sems):
+        self.place, self.own, self.slot_of = place, own, slot
+        zs, zr, self.h_send, self.h_recv, self.l_send, self.l_recv = sems
+        self.line = Line(place, own, lambda z: self.slot(z, place.high, place.low), zs, zr)
+
+    @staticmethod
+    def semaphores(count, depth, high_count):
+        dma = pltpu.SemaphoreType.DMA
+        cross = dma((count, high_count, depth))
+        return [dma((count, 2, depth)), dma((count, depth)), cross, cross, cross, cross]
+
+    def slot(self, z, high, low):
+        return self.slot_of((z * self.place.high_count + high) * 2 + low)
+
+    def _to_high(self, z, step, own):
+        place = self.place
+        target = self.slot(z, place.high, place.low)
+        return remote(
+            self.own if own else target,
+            target,
+            self.h_send.at[step, z],
+            self.h_recv.at[place.high, z],
+            experts=place.peer_high(step) * 2 + place.low,
+        )
+
+    def _to_low(self, z, high, own):
+        place = self.place
+        target = self.slot(z, high, place.low)
+        return remote(
+            self.own if own else target,
+            target,
+            self.l_send.at[high, z],
+            self.l_recv.at[high, z],
+            experts=place.e + 1 - 2 * place.low,
+        )
+
+    def _spread(self, z, own=False):
+        for step in range(1, self.place.high_count):
+            self._to_high(z, step, own).start()
+        self._to_low(z, self.place.high, own).start()
+
+    def start(self):
+        self.line.start()
+        self._spread(self.place.z, True)
+
+    def hop(self, step):
+        self.line.hop(step, self._spread)
+
+    def cross(self, z):
+        place = self.place
+        for step in range(1, place.high_count):
+            high = place.peer_high(step)
+            arrived(self.slot(z, high, place.low), self.h_recv.at[high, z])
+            self._to_low(z, high, False).start()
+
+    def finish(self):
+        place = self.place
+        for z in range(place.depth):
+            for high in range(place.high_count):
+                arrived(self.slot(z, high, 1 - place.low), self.l_recv.at[high, z])
+
+    def drain(self):
+        place = self.place
+        self.line.drain()
+        for z in range(place.depth):
+            for step in range(1, place.high_count):
+                self._to_high(z, step, False).wait_send()
+            for high in range(place.high_count):
+                self._to_low(z, high, False).wait_send()
+
+
+def expert_slab(ref, kind, local, shard, width):
+    start = pl.multiple_of(shard * width, 128)
+    if kind == 2:
+        return ref.at[local, pl.ds(start, width)]
+    return ref.at[local, :, pl.ds(start, width)]
+
+
+class ExpertGather:
+    def __init__(self, place, own, out, sems):
+        self.place, self.own, self.out = place, own, out
+        self.z_send, self.z_recv, self.x_send, self.x_recv = sems
+        self.local_count, self.width = own[0].shape[0], own[0].shape[2]
+
+    @staticmethod
+    def semaphores(depth, local_count):
+        dma = pltpu.SemaphoreType.DMA
+        return [
+            dma((local_count, 3, 2, depth)),
+            dma((local_count, 3, depth)),
+            dma((local_count, 3, depth)),
+            dma((local_count, 3, depth)),
+        ]
+
+    def slot(self, local, kind, shard):
+        return expert_slab(self.out[kind], kind, local, shard, self.width)
+
+    def _line(self, local, kind):
+        return Line(
+            self.place,
+            self.own[kind].at[local],
+            lambda z: self.slot(local, kind, self.place.shard(z)),
+            self.z_send.at[local, kind],
+            self.z_recv.at[local, kind],
+        )
+
+    def _across(self, local, kind, z, own=False):
+        target = self.slot(local, kind, self.place.shard(z))
+        return remote(
+            self.own[kind].at[local] if own else target,
+            target,
+            self.x_send.at[local, kind, z],
+            self.x_recv.at[local, kind, z],
+            dp=1 - self.place.x,
+        )
+
+    def start_x(self):
+        for local in range(self.local_count):
+            for kind in range(3):
+                self._across(local, kind, self.place.z, True).start()
+
+    def start_z(self):
+        for local in range(self.local_count):
+            for kind in range(3):
+                self._line(local, kind).start()
+
+    def hop(self, local, step):
+        for kind in range(3):
+            self._line(local, kind).hop(
+                step, lambda z, kind=kind: self._across(local, kind, z).start()
+            )
+
+    def wait_x(self, local, z):
+        for kind in range(3):
+            arrived(
+                self.slot(local, kind, self.place.other_shard(z)), self.x_recv.at[local, kind, z]
+            )
+
+    def drain(self):
+        for local in range(self.local_count):
+            for kind in range(3):
+                self._line(local, kind).drain()
+                for z in range(self.place.depth):
+                    self._across(local, kind, z).wait_send()
+
+
+def rope(values, cosine, sine_part):
+    lane = lax.broadcasted_iota(jnp.int32, cosine.shape, 1)
+    first = lax.rem(lane, HD) < HD // 2
+    turned = []
+    for start in range(0, values.shape[1], 2 * HD):
+        part = values[:, start : start + 2 * HD]
+        partner = jnp.where(
+            first, pltpu.roll(part, 2 * HD - HD // 2, 1), pltpu.roll(part, HD // 2, 1)
+        )
+        turned.append(part * cosine + partner * sine_part)
+    return jnp.concatenate(turned, 1)
+
+
+def norm_rows(values, gain):
+    root = lax.rsqrt(jnp.mean(values * values, -1, keepdims=True) + EPSILON)
+    return (values * root * gain).astype(BF)
+
+
+def tiles(total, size, body):
+    def run(i, carry):
+        body(pl.ds(pl.multiple_of(i * size, size), size))
+        return carry
+
+    lax.fori_loop(0, total // size, run, 0)
+
+
+def one_hots(routes, gates, me, local_count, total):
+    rows = routes.shape[1]
+    capacity = rows * 8 // (3 * total)
+    first, second = routes[0:1, :], routes[1:2, :]
+    ids = lax.rem(
+        lax.broadcasted_iota(jnp.int32, (total, rows), 0) + me * local_count, total
+    )
+    named = (first == ids) | (second == ids)
+    earlier = (
+        lax.broadcasted_iota(jnp.int32, (rows, rows), 0)
+        < lax.broadcasted_iota(jnp.int32, (rows, rows), 1)
+    ).astype(F32).astype(BF)
+    counts = mdot(named.astype(F32).astype(BF), earlier).astype(jnp.int32)
+    places = jnp.where(named, counts, -1)
+    weights = jnp.where(first == ids, gates[0:1, :], 0.0) + jnp.where(
+        second == ids, gates[1:2, :], 0.0
+    )
+    slot = lax.broadcasted_iota(jnp.int32, (capacity, rows), 0)
+    for i in range(total):
+        yield i, slot == places[i : i + 1, :], weights[i : i + 1, :]
+
+
+def ffn_chunk(x, g, weights, saved, sums, grads, tile):
+    gate_w, up_w, down_w = weights
+    act_s, d_gate_s, d_up_s = saved
+    out_sum, in_sum = sums
+
+    def forward(here):
+        x_rows, g_rows = x[here, :], g[here, :]
+        gate = mdot(x_rows, gate_w[...])
+        up = mdot(x_rows, up_w[...])
+        d_act = ndot(g_rows, down_w[...]).astype(BF).astype(F32)
+        sigma = jax.nn.sigmoid(gate)
+        silu = gate * sigma
+        act = (silu * up).astype(BF)
+        d_gate = (d_act * up * (sigma * (1.0 + gate * (1.0 - sigma)))).astype(BF)
+        d_up = (d_act * silu).astype(BF)
+        act_s[here, :] = act
+        d_gate_s[here, :] = d_gate
+        d_up_s[here, :] = d_up
+        out_sum[here, :] += mdot(act, down_w[...])
+        in_sum[here, :] += ndot(d_gate, gate_w[...]) + ndot(d_up, up_w[...])
+
+    rows = x.shape[0]
+    tiles(rows, tile, forward)
+    used = pl.ds(0, rows)
+
+    def weight_grads(here):
+        grads[0][here, :] = tdot(x[:, here], d_gate_s[used, :]).astype(BF)
+        grads[1][here, :] = tdot(x[:, here], d_up_s[used, :]).astype(BF)
+        grads[2][:, here] = tdot(act_s[used, :], g[:, here]).astype(BF)
+
+    tiles(x.shape[1], 256, weight_grads)
+
+
+def forward_kernel(sizes, *refs):
+    place = Place(sizes)
+    depth, high_count = sizes
+    owners = place.owners
+    (
+        tokens, cot, gates, routes, cosine, sine_part,
+        qkv_in, out_in, gain_in, sg_in, su_in, sd_in, eg_in, eu_in, ed_in,
+        qkv_o, out_o, gain_o, sg_o, su_o, sd_o, eg_o, eu_o, ed_o,
+        n1_o, k_o, v_o, q_o, att_o, hid_o, lse_o, side_o, dn2_o,
+        gsg_o, gsu_o, gsd_o, geg_o, geu_o, ged_o, outs_o, dins_o,
+        xk, wq, wo, gain_land, gain_v, g_all, n2, in_s, do_s, send_in, send_do,
+        wg, wu, wd, act_s, dg_s, du_s, stage_g, stage_u, stage_d,
+        *sems,
+    ) = refs
+    dense_sems, sems = sems[:6], sems[6:]
+    expert_sems, sems = sems[:4], sems[4:]
+    (
+        line_send, line_recv, load_sem, ai_send, ai_recv, ad_send, ad_recv,
+        chunk_sem, store_sem, out_sem,
+    ) = sems
+    micro_count, rows, features = tokens.shape
+    prompt = depth * PB
+    length = prompt + CONT
+    local_count, _, width = eg_in.shape
+    total = owners * local_count
+    capacity = rows * 8 // (3 * total)
+    slots = in_s.shape[1]
+    me = place.e
+
+    def dense(i, own, slot):
+        return DenseGather(place, own, slot, [s.at[i] for s in dense_sems])
+
+    def rows_of(ref, count):
+        return lambda s: ref.at[pl.ds(pl.multiple_of(s * count, 16), count)]
+
+    def columns_of(ref, count):
+        return lambda s: ref.at[:, pl.ds(pl.multiple_of(s * count, 128), count)]
+
+    early = [
+        dense(0, qkv_in, rows_of(wq, qkv_in.shape[0])),
+        dense(1, out_in, rows_of(wo, out_in.shape[0])),
+        dense(2, gain_in, rows_of(gain_land, gain_in.shape[0])),
+    ]
+    late = [
+        dense(3, sg_in, columns_of(sg_o, sg_in.shape[1])),
+        dense(4, su_in, columns_of(su_o, su_in.shape[1])),
+        dense(5, sd_in, rows_of(sd_o, sd_in.shape[0])),
+    ]
+    experts = ExpertGather(place, (eg_in, eu_in, ed_in), (eg_o, eu_o, ed_o), expert_sems)
+    own_prompt = pl.ds(pl.multiple_of(place.z * PB, PB), PB)
+    prompts = Line(
+        place,
+        tokens.at[:, pl.ds(0, PB)],
+        lambda z: xk.at[:, pl.ds(pl.multiple_of(z * PB, PB), PB)],
+        line_send,
+        line_recv,
+    )
+    own_at = (place.z * high_count + place.high) * 2 + place.low
+    loads = [
+        (tokens.at[:, pl.ds(0, PB)], xk.at[:, own_prompt]),
+        (tokens.at[:, pl.ds(PB, CONT)], xk.at[:, pl.ds(prompt, CONT)]),
+    ]
+    loads += [(cot.at[m], g_all.at[pl.ds(m * rows, rows)]) for m in range(micro_count)]
+    loads += [(d.own, d.slot_of(own_at)) for d in early]
+    bounce = [
+        (sg_in, wg.at[0, :, pl.ds(0, sg_in.shape[1])], late[0].slot_of(own_at)),
+        (su_in, wu.at[0, :, pl.ds(0, su_in.shape[1])], late[1].slot_of(own_at)),
+        (sd_in, wd.at[0, pl.ds(0, sd_in.shape[0])], late[2].slot_of(own_at)),
+    ]
+    loads += [(source, middle) for source, middle, _ in bounce]
+    load_copies = [
+        pltpu.make_async_copy(source, target, load_sem.at[i])
+        for i, (source, target) in enumerate(loads)
+    ]
+    bounce_copies = [
+        pltpu.make_async_copy(middle, target, load_sem.at[i])
+        for i, (_, middle, target) in enumerate(bounce)
+    ]
+    for copy in load_copies:
+        copy.start()
+    place.greet()
+    prompts.start()
+    for d in early:
+        d.start()
+    experts.start_x()
+    for copy in load_copies:
+        copy.wait()
+    for copy in bounce_copies:
+        copy.start()
+    stores = []
+
+    def store(source, target):
+        copy = pltpu.make_async_copy(source, target, out_sem.at[len(stores)])
+        copy.start()
+        stores.append(copy)
+
+    def slot_rows(m, sender):
+        return pl.ds(pl.multiple_of((m * owners + sender) * capacity, 16), capacity)
+
+    def exchange(buffer, land, send_sem, recv_sem, m, step):
+        return remote(
+            buffer.at[step - 1, m],
+            land.at[:, slot_rows(m, me)],
+            send_sem.at[step - 1, m],
+            recv_sem.at[step - 1, m],
+            experts=place.peer_owner(step),
+        )
+
+    def exchanged(land, recv_sem, m, step):
+        sender = lax.rem(me - step + owners, owners)
+        arrived(land.at[:, slot_rows(m, sender)], recv_sem.at[step - 1, m])
+
+    def put(buffer, land, m, i, value):
+        if i < local_count:
+            land[i, slot_rows(m, me), :] = value
+        else:
+            buffer[i // local_count - 1, m, i % local_count] = value
+
+    for m in range(micro_count):
+        g_rows = g_all[pl.ds(m * rows, rows), :]
+        for i, hit, weight in one_hots(routes.at[m], gates.at[m], me, local_count, total):
+            gate = jnp.sum(jnp.where(hit, weight, 0.0), -1, keepdims=True)
+            value = mdot(hit.astype(F32).astype(BF), g_rows)
+            put(send_do, do_s, m, i, (gate * value).astype(BF))
+    prompts.hop(0)
+    for step in range(depth - 1):
+        for d in early:
+            d.hop(step)
+        if step + 1 < depth - 1:
+            prompts.hop(step + 1)
+    for copy in bounce_copies:
+        copy.wait()
+    for d in late:
+        d.start()
+    experts.start_z()
+    for z in range(depth):
+        for d in early:
+            d.cross(z)
+    for d in early:
+        d.finish()
+    for m in range(micro_count):
+        for step in range(1, owners):
+            exchange(send_do, do_s, ad_send, ad_recv, m, step).start()
+    store(wq, qkv_o)
+    store(wo, out_o)
+    shards = depth * owners
+    gain_rows = gain_in.shape[0]
+    gain_sum = jnp.zeros((8, features), F32)
+    for s in range(shards):
+        gain_sum += gain_land[pl.ds(s * gain_rows, gain_rows), :].astype(F32)[:8]
+    gain_v[...] = gain_sum
+    store(gain_v, gain_o)
+
+    def own_rows(i):
+        start = place.z * PB if i == 0 else prompt + (i - 1) * PB
+        return start, pl.ds(start if i else pl.multiple_of(start, PB), PB)
+
+    def front(n1, k, v, q, att, hid, lse):
+        lse[...] = jnp.zeros_like(lse)
+        for m in range(micro_count):
+
+            def project(here):
+                normed = norm_rows(xk[m, here, :].astype(F32), gain_v[0:1, :])
+                n1[m, here, :] = normed
+                key = ndot(normed, wq[pl.ds(features, features), :])
+                k[m, here, :] = rope(key, cosine[here, :], sine_part[here, :]).astype(BF)
+                v[m, here, :] = ndot(normed, wq[pl.ds(2 * features, features), :]).astype(BF)
+
+            tiles(length, 256, project)
+            for i in range(rows // PB):
+                _, here = own_rows(i)
+                query = ndot(n1[m, here, :], wq[pl.ds(0, features), :])
+                query = rope(query, cosine[here, :], sine_part[here, :]).astype(BF)
+                q[m, pl.ds(i * PB, PB), :] = query * jnp.asarray(HD**-0.5, BF)
+            for d in late:
+                d.hop(m)
+        store(n1, n1_o)
+        store(k, k_o)
+        store(v, v_o)
+        store(q, q_o)
+        lane = lax.broadcasted_iota(jnp.int32, (PB, 2 * HD), 1)
+        column = lax.broadcasted_iota(jnp.int32, (PB, length), 1)
+        row = lax.broadcasted_iota(jnp.int32, (PB, length), 0)
+        for m in range(micro_count):
+
+            def pair(index, carry):
+                lanes = pl.ds(pl.multiple_of(index * 2 * HD, 2 * HD), 2 * HD)
+                keys, values = k[m, :, lanes], v[m, :, lanes]
+                for i in range(rows // PB):
+                    here = pl.ds(i * PB, PB)
+                    query = q[m, here, lanes]
+                    allowed = column <= row + own_rows(i)[0]
+                    parts = []
+                    logs = lse[m, here, :]
+                    for sub in range(2):
+                        only = jnp.where(lane // HD == sub, query, jnp.zeros_like(query))
+                        scores = jnp.where(allowed, ndot(only, keys), -1000000000.0)
+                        highest = jnp.max(scores, -1, keepdims=True)
+                        weights = jnp.exp(scores - highest)
+                        sums = jnp.sum(weights, -1, keepdims=True)
+                        parts.append(mdot((weights * (1.0 / sums)).astype(BF), values))
+                        logs = jnp.where(lane == 2 * index + sub, highest + jnp.log(sums), logs)
+                    lse[m, here, :] = logs
+                    att[m, here, lanes] = jnp.where(lane < HD, parts[0], parts[1]).astype(BF)
+                return carry
+
+            lax.fori_loop(0, features // (2 * HD), pair, 0)
+            for i in range(rows // PB):
+                here = pl.ds(i * PB, PB)
+                hidden = xk[m, own_rows(i)[1], :].astype(F32) + mdot(att[m, here, :], wo[...])
+                hid[m, here, :] = hidden
+                n2[pl.ds(m * rows + i * PB, PB), :] = norm_rows(hidden, gain_v[1:2, :])
+            normed = n2[pl.ds(m * rows, rows), :]
+            for i, hit, _ in one_hots(routes.at[m], gates.at[m], me, local_count, total):
+                value = mdot(hit.astype(F32).astype(BF), normed)
+                put(send_in, in_s, m, i, value.astype(BF))
+            for step in range(1, owners):
+                exchange(send_in, in_s, ai_send, ai_recv, m, step).start()
+            if m == 0:
+                for step in range(micro_count, depth - 1):
+                    for d in late:
+                        d.hop(step)
+        store(att, att_o)
+        store(hid, hid_o)
+        store(lse, lse_o)
+        for z in range(depth):
+            for d in late:
+                d.cross(z)
+        for d in late:
+            d.finish()
+        for copy in stores:
+            copy.wait()
+
+    pl.run_scoped(
+        front,
+        pltpu.VMEM((micro_count, length, features), BF),
+        pltpu.VMEM((micro_count, length, features), BF),
+        pltpu.VMEM((micro_count, length, features), BF),
+        pltpu.VMEM((micro_count, rows, features), BF),
+        pltpu.VMEM((micro_count, rows, features), BF),
+        pltpu.VMEM((micro_count, rows, features), F32),
+        pltpu.VMEM((micro_count, rows, 2 * HD), F32),
+    )
+    saved = (act_s, dg_s, du_s)
+    staged = (stage_g, stage_u, stage_d)
+
+    def chunk_loads(sources, slot):
+        return [
+            pltpu.make_async_copy(source, buffer.at[slot], chunk_sem.at[slot, kind])
+            for kind, (source, buffer) in enumerate(zip(sources, (wg, wu, wd)))
+        ]
+
+    def chunk_stores(targets, slot):
+        return [
+            pltpu.make_async_copy(buffer.at[slot], target, store_sem.at[slot, kind])
+            for kind, (target, buffer) in enumerate(zip(targets, staged))
+        ]
+
+    def shared(out_sum, in_sum):
+        out_sum[...] = jnp.zeros_like(out_sum)
+        in_sum[...] = jnp.zeros_like(in_sum)
+        count = sg_o.shape[1] // width
+
+        def part(refs, c):
+            here = pl.ds(pl.multiple_of(c * width, 128), width)
+            return [refs[0].at[:, here], refs[1].at[:, here], refs[2].at[here]]
+
+        for copy in chunk_loads(part((sg_o, su_o, sd_o), 0), 0):
+            copy.start()
+
+        def run(c, carry):
+            slot = lax.rem(c, 2)
+
+            def prefetch():
+                for copy in chunk_loads(part((sg_o, su_o, sd_o), c + 1), 1 - slot):
+                    copy.start()
+
+            pl.when(c + 1 < count)(prefetch)
+            for copy in chunk_loads(part((sg_o, su_o, sd_o), c), slot):
+                copy.wait()
+            targets = part((gsg_o, gsu_o, gsd_o), c)
+
+            def previous():
+                for copy in chunk_stores(targets, slot):
+                    copy.wait()
+
+            pl.when(c >= 2)(previous)
+            ffn_chunk(
+                n2,
+                g_all,
+                (wg.at[slot], wu.at[slot], wd.at[slot]),
+                saved,
+                (out_sum, in_sum),
+                [buffer.at[slot] for buffer in staged],
+                384,
+            )
+            for copy in chunk_stores(targets, slot):
+                copy.start()
+            for local in range(local_count):
+                pl.when(c == count // 2 + local)(lambda local=local: experts.hop(local, 0))
+            return carry
+
+        lax.fori_loop(0, count, run, 0)
+        for slot in range(2):
+            for copy in chunk_stores(part((gsg_o, gsu_o, gsd_o), slot), slot):
+                copy.wait()
+        ends = [
+            pltpu.make_async_copy(out_sum, side_o, out_sem.at[0]),
+            pltpu.make_async_copy(in_sum, dn2_o, out_sem.at[1]),
+        ]
+        for copy in ends:
+            copy.start()
+        for copy in ends:
+            copy.wait()
+
+    pl.run_scoped(
+        shared,
+        pltpu.VMEM((micro_count * rows, features), F32),
+        pltpu.VMEM((micro_count * rows, features), F32),
+    )
+    for m in range(micro_count):
+        for step in range(1, owners):
+            exchanged(in_s, ai_recv, m, step)
+            exchanged(do_s, ad_recv, m, step)
+
+    def routed(out_sum, in_sum):
+        out_sum[...] = jnp.zeros_like(out_sum)
+        in_sum[...] = jnp.zeros_like(in_sum)
+
+        def item(w, carry):
+            after = jnp.maximum(w - 2, 0)
+            step, kind = after // 4, lax.rem(after, 4)
+            side = lax.rem(kind, 2)
+            z = jnp.where(w < 2, place.z, place.z + (2 * side - 1) * (1 + step))
+            crossed = jnp.where(w < 2, w, kind // 2)
+            valid = place.on_line(z)
+            shard = jnp.where(crossed == 1, place.other_shard(z), place.shard(z))
+
+            def load(local):
+                sources = [
+                    expert_slab(ref, kind, local, shard, width)
+                    for kind, ref in enumerate((eg_o, eu_o, ed_o))
+                ]
+                return chunk_loads(sources, local)
+
+            def begin():
+                def own():
+                    for local in range(local_count):
+                        mine = [ref.at[local] for ref in (eg_in, eu_in, ed_in)]
+                        for copy in chunk_loads(mine, local):
+                            copy.start()
+
+                def landed():
+                    def wait_x():
+                        for local in range(local_count):
+                            experts.wait_x(local, z)
+
+                    pl.when(crossed == 1)(wait_x)
+                    for local in range(local_count):
+                        for copy in load(local):
+                            copy.start()
+
+                pl.when(w == 0)(own)
+                pl.when(w > 0)(landed)
+
+            pl.when(valid)(begin)
+
+            def one(local, carry):
+                targets = [
+                    expert_slab(ref, kind, local, shard, width)
+                    for kind, ref in enumerate((geg_o, geu_o, ged_o))
+                ]
+
+                def compute():
+                    for copy in load(local):
+                        copy.wait()
+
+                    def previous():
+                        for copy in chunk_stores(targets, local):
+                            copy.wait()
+
+                    pl.when(w > 0)(previous)
+                    ffn_chunk(
+                        in_s.at[local],
+                        do_s.at[local],
+                        (wg.at[local], wu.at[local], wd.at[local]),
+                        saved,
+                        (out_sum.at[local], in_sum.at[local]),
+                        [buffer.at[local] for buffer in staged],
+                        512,
+                    )
+                    for copy in chunk_stores(targets, local):
+                        copy.start()
+
+                pl.when(valid)(compute)
+                for later in range(1, depth - 1):
+                    at = 0 if later == 1 else 2 + 4 * (later - 2)
+                    pl.when(w == at)(lambda later=later: experts.hop(local, later))
+                return carry
+
+            lax.fori_loop(0, local_count, one, 0)
+            return carry
+
+        lax.fori_loop(0, 2 + 4 * (depth - 1), item, 0)
+        for local in range(local_count):
+            targets = [
+                expert_slab(ref, kind, local, 0, width)
+                for kind, ref in enumerate((geg_o, geu_o, ged_o))
+            ]
+            for copy in chunk_stores(targets, local):
+                copy.wait()
+
+            def finish(here, local=local):
+                in_s[local, here, :] = out_sum[local, here, :].astype(BF)
+                do_s[local, here, :] = in_sum[local, here, :].astype(BF)
+
+            tiles(slots, 256, finish)
+
+    pl.run_scoped(
+        routed,
+        pltpu.VMEM((local_count, slots, features), F32),
+        pltpu.VMEM((local_count, slots, features), F32),
+    )
+    ends = [
+        pltpu.make_async_copy(in_s, outs_o, out_sem.at[0]),
+        pltpu.make_async_copy(do_s, dins_o, out_sem.at[1]),
+    ]
+    for copy in ends:
+        copy.start()
+    for copy in ends:
+        copy.wait()
+    prompts.drain()
+    for d in early + late:
+        d.drain()
+    experts.drain()
+    for m in range(micro_count):
+        for step in range(1, owners):
+            exchange(send_do, do_s, ad_send, ad_recv, m, step).wait_send()
+            exchange(send_in, in_s, ai_send, ai_recv, m, step).wait_send()
+
+
+def rope_tables(prompt):
+    positions = np.arange(prompt + CONT, dtype=np.float64)
+    frequency = 10000.0 ** (-2.0 * np.arange(HD // 2) / HD)
+    angles = positions[:, None] * frequency
+    cosine, sine_part = np.cos(angles), np.sin(angles)
+    return (
+        np.concatenate([cosine] * 4, 1).astype(np.float32),
+        np.concatenate([-sine_part, sine_part] * 2, 1).astype(np.float32),
+    )
+
+
+def run_forward(sizes, tokens, cot, gates, routes, dense, experts):
+    depth, high_count = sizes
+    micro_count, rows, features = tokens.shape
+    owners = high_count * 2
+    line = depth * owners
+    prompt = depth * PB
+    length = prompt + CONT
+    local_count, _, width = experts[0].shape
+    hidden_units = dense[3].shape[1] * line
+    capacity = rows * 8 // (3 * owners * local_count)
+    slots = micro_count * owners * capacity
+    cosine, sine_part = rope_tables(prompt)
+    hbm, vmem = pl.BlockSpec(memory_space=pltpu.HBM), pl.BlockSpec(memory_space=pltpu.VMEM)
+
+    def shape(dtype, *dims):
+        return jax.ShapeDtypeStruct(dims, dtype)
+
+    token_rows = micro_count * rows
+    wide, tall = (features, hidden_units), (hidden_units, features)
+    out_shape = [
+        shape(BF, dense[0].shape[0] * line, features),
+        shape(BF, dense[1].shape[0] * line, features),
+        shape(F32, 8, features),
+        shape(BF, *wide), shape(BF, *wide), shape(BF, *tall),
+        shape(BF, local_count, *wide), shape(BF, local_count, *wide), shape(BF, local_count, *tall),
+        shape(BF, micro_count, length, features),
+        shape(BF, micro_count, length, features),
+        shape(BF, micro_count, length, features),
+        shape(BF, micro_count, rows, features),
+        shape(BF, micro_count, rows, features),
+        shape(F32, micro_count, rows, features),
+        shape(F32, micro_count, rows, 2 * HD),
+        shape(F32, token_rows, features),
+        shape(F32, token_rows, features),
+        shape(BF, *wide), shape(BF, *wide), shape(BF, *tall),
+        shape(BF, local_count, *wide), shape(BF, local_count, *wide), shape(BF, local_count, *tall),
+        shape(BF, local_count, slots, features),
+        shape(BF, local_count, slots, features),
+    ]
+    dma = pltpu.SemaphoreType.DMA
+    buffers = max(2, local_count)
+    send = pltpu.VMEM((owners - 1, micro_count, local_count, capacity, features), BF)
+    scratch = [
+        pltpu.VMEM((micro_count, length, features), BF),
+        pltpu.VMEM(out_shape[0].shape, BF),
+        pltpu.VMEM(out_shape[1].shape, BF),
+        pltpu.VMEM((dense[2].shape[0] * line, features), BF),
+        pltpu.VMEM((8, features), F32),
+        pltpu.VMEM((token_rows, features), BF),
+        pltpu.VMEM((token_rows, features), BF),
+        pltpu.VMEM((local_count, slots, features), BF),
+        pltpu.VMEM((local_count, slots, features), BF),
+        send,
+        send,
+        pltpu.VMEM((buffers, features, width), BF),
+        pltpu.VMEM((buffers, features, width), BF),
+        pltpu.VMEM((buffers, width, features), BF),
+        pltpu.VMEM((max(slots, token_rows), width), BF),
+        pltpu.VMEM((max(slots, token_rows), width), BF),
+        pltpu.VMEM((max(slots, token_rows), width), BF),
+        pltpu.VMEM((buffers, features, width), BF),
+        pltpu.VMEM((buffers, features, width), BF),
+        pltpu.VMEM((buffers, width, features), BF),
+    ]
+    scratch += DenseGather.semaphores(len(dense), depth, high_count)
+    scratch += ExpertGather.semaphores(depth, local_count)
+    scratch += [
+        dma((2, depth)),
+        dma((depth,)),
+        dma((10 + micro_count,)),
+        dma((owners - 1, micro_count)),
+        dma((owners - 1, micro_count)),
+        dma((owners - 1, micro_count)),
+        dma((owners - 1, micro_count)),
+        dma((buffers, 3)),
+        dma((buffers, 3)),
+        dma((12,)),
+    ]
+    return pl.pallas_call(
+        functools.partial(forward_kernel, sizes),
+        out_shape=out_shape,
+        in_specs=[hbm] * 2 + [vmem] * 4 + [hbm] * 9,
+        out_specs=[hbm] * len(out_shape),
+        scratch_shapes=scratch,
+        compiler_params=pltpu.CompilerParams(
+            collective_id=0, has_side_effects=True, vmem_limit_bytes=60 * MIB
+        ),
+        name="gather_and_forward",
+    )(tokens, cot, gates, routes, cosine, sine_part, *dense, *experts)
+
+
+class PlaceS:
+    def __init__(self, sizes):
+        self.depth, self.high_count = sizes
+        self.x = lax.axis_index(DP)
+        self.z = lax.axis_index(CONTEXT)
+        self.e = lax.axis_index(EXPERTS)
+        self.high = self.e // 2
+        self.low = self.e % 2
+
+    def shard(self, z):
+        return self.x * self.depth + z
+
+    def other_shard(self, z):
+        return (1 - self.x) * self.depth + z
+
+    def peer_high(self, step):
+        return lax.rem(self.high + step, self.high_count)
+
+    def greet(self, everyone=False):
+        barrier = pltpu.get_barrier_semaphore()
+
+        def signal(**device):
+            pl.semaphore_signal(barrier, inc=1, device_id=device, device_id_type=MESH)
+
+        signal(dp=1 - self.x)
+        signal(experts=self.e + 1 - 2 * self.low)
+        count = 2
+        for step in range(1, self.high_count):
+            signal(experts=self.peer_high(step) * 2 + self.low)
+            count += 1
+            if everyone:
+                signal(experts=self.peer_high(step) * 2 + 1 - self.low)
+                count += 1
+        if everyone:
+            for step in range(1, self.depth):
+                signal(context=lax.rem(self.z + step, self.depth))
+                count += 1
+            pl.semaphore_wait(barrier, count)
+        else:
+            pl.when(self.z > 0)(lambda: signal(context=self.z - 1))
+            pl.when(self.z < self.depth - 1)(lambda: signal(context=self.z + 1))
+            count += jnp.where(self.z > 0, 1, 0) + jnp.where(self.z < self.depth - 1, 1, 0)
+            pl.semaphore_wait(barrier, count)
+
+
+def slab(ref, index, rows):
+    return ref.at[pl.ds(pl.multiple_of(index * rows, 16), rows)]
+
+
+def add_into(target, sources, rows):
+    total = target.shape[0]
+
+    def body(i, carry):
+        here = pl.ds(pl.multiple_of(i * rows, rows), rows)
+        value = target[here, :].astype(jnp.float32)
+        for source in sources:
+            value = value + source[here, :].astype(jnp.float32)
+        target[here, :] = value.astype(target.dtype)
+        return carry
+
+    lax.fori_loop(0, total // rows, body, 0)
+
+
+class ScatterAll:
+    def __init__(self, place, dense, expert, dense_outs, expert_outs, gain, gain_out, buffers, sems):
+        self.place = place
+        self.dense, self.expert = dense, expert
+        self.dense_outs, self.expert_outs = dense_outs, expert_outs
+        self.gain, self.gain_out = gain, gain_out
+        count = len(dense)
+        self.count = count
+        self.dlow = buffers[:count]
+        self.dhigh = buffers[count : 2 * count]
+        self.dline = buffers[2 * count : 3 * count]
+        self.dcross = buffers[3 * count : 4 * count]
+        rest = buffers[4 * count :]
+        self.dense_own, self.ecross, self.eline, self.eown = rest[0], rest[1:4], rest[4:7], rest[7:10]
+        self.gmine, self.glow, self.ghigh, self.gline, self.gcross = rest[10:15]
+        (
+            self.sl_send,
+            self.sl_recv,
+            self.sh_send,
+            self.sh_recv,
+            self.sz_send,
+            self.sz_recv,
+            self.sx_send,
+            self.sx_recv,
+            self.ez_send,
+            self.ez_recv,
+            self.ex_send,
+            self.ex_recv,
+            self.own_sem,
+            self.eown_sem,
+            self.out_sem,
+            self.eout_sem,
+            self.g_send,
+            self.g_recv,
+        ) = sems
+        self.local_count = self.ecross[0].shape[1]
+        self.pieces = [(a, e) for e in range(self.local_count) for a in range(3)]
+        self.width = self.ecross[0].shape[3]
+
+    @staticmethod
+    def scratch(sizes, rows, features, local_count, width):
+        depth, high_count = sizes
+        bf = jnp.bfloat16
+        buffers = [pltpu.VMEM((depth, high_count, r, features), bf) for r in rows]
+        buffers += [pltpu.VMEM((high_count - 1, depth, r, features), bf) for r in rows]
+        buffers += [pltpu.VMEM((depth + 1, r, features), bf) for r in rows]
+        buffers += [pltpu.VMEM((r, features), bf) for r in rows]
+        buffers += [pltpu.VMEM((depth, high_count, max(rows), features), bf)]
+        for lead in (depth, depth + 1, None):
+            for a in range(3):
+                shape = (local_count,) + ((features, width) if a < 2 else (width, features))
+                buffers.append(pltpu.VMEM(shape if lead is None else (lead,) + shape, bf))
+        gain = (8, features)
+        buffers += [
+            pltpu.VMEM(gain, jnp.float32),
+            pltpu.VMEM(gain, jnp.float32),
+            pltpu.VMEM((high_count - 1,) + gain, jnp.float32),
+            pltpu.VMEM((depth - 1,) + gain, jnp.float32),
+            pltpu.VMEM(gain, jnp.float32),
+        ]
+        dma = pltpu.SemaphoreType.DMA
+        count, pieces = len(rows), 3 * local_count
+        sems = [
+            dma((count,)),
+            dma((count,)),
+            dma((count, high_count)),
+            dma((count, high_count)),
+            dma((count, depth)),
+            dma((count, depth + 1)),
+            dma((count,)),
+            dma((count,)),
+            dma((pieces, depth)),
+            dma((pieces, depth + 1)),
+            dma((pieces, depth)),
+            dma((pieces, depth)),
+            dma((1,)),
+            dma((pieces,)),
+            dma((count,)),
+            dma((pieces,)),
+            dma((3 + depth + high_count,)),
+            dma((3 + depth + high_count,)),
+        ]
+        return buffers, sems
+
+    def _x_copy(self, p, z):
+        a, local = self.pieces[p]
+        return remote(
+            expert_slab(self.expert[a], a, local, self.place.other_shard(z), self.width),
+            self.ecross[a].at[z, local],
+            self.ex_send.at[p, z],
+            self.ex_recv.at[p, z],
+            dp=1 - self.place.x,
+        )
+
+    def _order(self, do):
+        place = self.place
+        for step in range(place.depth - 1, 0, -1):
+            for direction in (1, -1):
+                z = place.z + direction * step
+                pl.when((z >= 0) & (z < place.depth))(
+                    lambda z=z, d=direction, s=step: do(z, d, s)
+                )
+        do(place.z, 0, 0)
+
+    def expert_start(self):
+        def start(z, direction, step):
+            for p in range(len(self.pieces)):
+                self._x_copy(p, z).start()
+
+        self._order(start)
+
+    def _own_load(self, p, z):
+        a, local = self.pieces[p]
+        return pltpu.make_async_copy(
+            expert_slab(self.expert[a], a, local, self.place.shard(z), self.width),
+            self.eown[a].at[local],
+            self.eown_sem.at[p],
+        )
+
+    def _line_copy(self, p, z, direction):
+        a, local = self.pieces[p]
+        place = self.place
+        if direction > 0:
+            slot = z
+        else:
+            slot = jnp.where(z == place.z - 1, place.depth, z)
+        return remote(
+            self.ecross[a].at[z, local],
+            self.eline[a].at[slot, local],
+            self.ez_send.at[p, z],
+            self.ez_recv.at[p, slot],
+            context=place.z + direction,
+        )
+
+    def _line_wait(self, p, slot):
+        a, local = self.pieces[p]
+        here = self.eline[a].at[slot, local]
+        remote(here, here, self.ez_send.at[p, 0], self.ez_recv.at[p, slot], context=0).wait_recv()
+
+    def expert_loads(self, z):
+        for p in range(len(self.pieces)):
+            self._own_load(p, z).start()
+
+    def expert_piece(self, p, z, direction):
+        a, local = self.pieces[p]
+        place = self.place
+        rows = 64
+        self._x_copy(p, z).wait_recv()
+        self._own_load(p, z).wait()
+        target, own = self.ecross[a].at[z, local], self.eown[a].at[local]
+        if direction:
+            upstream = place.z > 0 if direction > 0 else place.z < place.depth - 1
+
+            def with_line():
+                self._line_wait(p, z)
+                add_into(target, [own, self.eline[a].at[z, local]], rows)
+
+            pl.when(upstream)(with_line)
+            pl.when(jnp.logical_not(upstream))(lambda: add_into(target, [own], rows))
+            self._line_copy(p, z, direction).start()
+        else:
+            left, right = place.z > 0, place.z < place.depth - 1
+
+            def both():
+                self._line_wait(p, z)
+                self._line_wait(p, place.depth)
+                add_into(
+                    target, [own, self.eline[a].at[z, local], self.eline[a].at[place.depth, local]], rows
+                )
+
+            def one(slot):
+                self._line_wait(p, slot)
+                add_into(target, [own, self.eline[a].at[slot, local]], rows)
+
+            pl.when(left & right)(both)
+            pl.when(left & jnp.logical_not(right))(lambda: one(z))
+            pl.when(jnp.logical_not(left) & right)(lambda: one(place.depth))
+            pltpu.make_async_copy(
+                target, self.expert_outs[a].at[local], self.eout_sem.at[p]
+            ).start()
+
+    def expert_all(self):
+        def run(z, direction, step):
+            self.expert_loads(z)
+            for p in range(len(self.pieces)):
+                self.expert_piece(p, z, direction)
+
+        self._order(run)
+
+    def expert_drain(self):
+        def drain(z, direction, step):
+            for p, (a, local) in enumerate(self.pieces):
+                self._x_copy(p, z).wait_send()
+                if direction:
+                    self._line_copy(p, z, direction).wait_send()
+                else:
+                    pltpu.make_async_copy(
+                        self.ecross[a].at[z, local], self.expert_outs[a].at[local], self.eout_sem.at[p]
+                    ).wait()
+
+        self._order(drain)
+
+    def _low_copy(self, a):
+        place = self.place
+        return remote(
+            self.dense[a].at[:, :, 1 - place.low],
+            self.dlow[a],
+            self.sl_send.at[a],
+            self.sl_recv.at[a],
+            experts=place.e + 1 - 2 * place.low,
+        )
+
+    def dense_start(self, a):
+        self._low_copy(a).start()
+
+    def _high_copy(self, a, step):
+        place = self.place
+        peer = place.peer_high(step)
+        return remote(
+            self.dlow[a].at[:, peer],
+            self.dhigh[a].at[step - 1],
+            self.sh_send.at[a, step],
+            self.sh_recv.at[a, step],
+            experts=peer * 2 + place.low,
+        )
+
+    def dense_low(self, a):
+        place = self.place
+        rows = self.dlow[a].shape[2]
+        own = self.dense_own.at[:, :, pl.ds(0, rows)]
+        copy = pltpu.make_async_copy(self.dense[a].at[:, :, place.low], own, self.own_sem.at[0])
+        copy.start()
+        self._low_copy(a).wait_recv()
+        copy.wait()
+        for z in range(place.depth):
+            for high in range(place.high_count):
+                add_into(self.dlow[a].at[z, high], [self.dense_own.at[z, high, pl.ds(0, rows)]], 16)
+        for step in range(1, place.high_count):
+            self._high_copy(a, step).start()
+
+    def dense_high(self, a):
+        place = self.place
+        for step in range(1, place.high_count):
+            self._high_copy(a, step).wait_recv()
+        for z in range(place.depth):
+            add_into(
+                self.dlow[a].at[z, place.high],
+                [self.dhigh[a].at[step - 1, z] for step in range(1, place.high_count)],
+                16,
+            )
+
+    def _dline_copy(self, a, z, direction):
+        place = self.place
+        if direction > 0:
+            slot = z
+        else:
+            slot = jnp.where(z == place.z - 1, place.depth, z)
+        return remote(
+            self.dlow[a].at[z, place.high],
+            self.dline[a].at[slot],
+            self.sz_send.at[a, z],
+            self.sz_recv.at[a, slot],
+            context=place.z + direction,
+        )
+
+    def _dline_wait(self, a, slot):
+        here = self.dline[a].at[slot]
+        remote(here, here, self.sz_send.at[a, 0], self.sz_recv.at[a, slot], context=0).wait_recv()
+
+    def _dcross_copy(self, a):
+        place = self.place
+        return remote(
+            self.dlow[a].at[place.z, place.high],
+            self.dcross[a],
+            self.sx_send.at[a],
+            self.sx_recv.at[a],
+            dp=1 - place.x,
+        )
+
+    def dense_line(self, which):
+        place = self.place
+
+        def run(z, direction, step):
+            for a in which:
+                target = self.dlow[a].at[z, place.high]
+                if direction:
+                    upstream = place.z > 0 if direction > 0 else place.z < place.depth - 1
+
+                    def with_line(a=a, target=target):
+                        self._dline_wait(a, z)
+                        add_into(target, [self.dline[a].at[z]], 16)
+
+                    pl.when(upstream)(with_line)
+                    self._dline_copy(a, z, direction).start()
+                else:
+
+                    def one(slot, a=a, target=target):
+                        self._dline_wait(a, slot)
+                        add_into(target, [self.dline[a].at[slot]], 16)
+
+                    pl.when(place.z > 0)(lambda one=one: one(place.z))
+                    pl.when(place.z < place.depth - 1)(lambda one=one: one(place.depth))
+                    self._dcross_copy(a).start()
+
+        self._order(run)
+
+    def dense_finish(self, a):
+        place = self.place
+        cross = self._dcross_copy(a)
+        cross.wait_recv()
+        add_into(self.dcross[a], [self.dlow[a].at[place.z, place.high]], 16)
+        pltpu.make_async_copy(self.dcross[a], self.dense_outs[a], self.out_sem.at[a]).start()
+
+    def dense_drain(self, a):
+        place = self.place
+        self._low_copy(a).wait_send()
+        for step in range(1, place.high_count):
+            self._high_copy(a, step).wait_send()
+
+        def drain(z, direction, step):
+            if direction:
+                self._dline_copy(a, z, direction).wait_send()
+
+        self._order(drain)
+        self._dcross_copy(a).wait_send()
+        pltpu.make_async_copy(self.dcross[a], self.dense_outs[a], self.out_sem.at[a]).wait()
+
+    def gains_all(self):
+        place = self.place
+        depth, high_count = place.depth, place.high_count
+
+        def stage(first, targets, slots):
+            copies = [
+                remote(self.gmine, slot, self.g_send.at[first + i], self.g_recv.at[first + i], **target)
+                for i, (target, slot) in enumerate(zip(targets, slots))
+            ]
+            for copy in copies:
+                copy.start()
+            for copy in copies:
+                copy.wait()
+            self.gmine[...] = sum((slot[...] for slot in slots), self.gmine[...])
+
+        stage(0, [dict(experts=place.e + 1 - 2 * place.low)], [self.glow])
+        stage(
+            1,
+            [dict(experts=place.peer_high(s) * 2 + place.low) for s in range(1, high_count)],
+            [self.ghigh.at[s - 1] for s in range(1, high_count)],
+        )
+        stage(
+            high_count,
+            [dict(context=lax.rem(place.z + s, depth)) for s in range(1, depth)],
+            [self.gline.at[s - 1] for s in range(1, depth)],
+        )
+        stage(high_count + depth - 1, [dict(dp=1 - place.x)], [self.gcross])
+        self.gain_out[...] = self.gmine[...]
+
+
+def scatter_kernel(sizes, count, *refs):
+    place = PlaceS(sizes)
+    dense, refs = refs[:count], refs[count:]
+    expert, refs = refs[:3], refs[3:]
+    gain, refs = refs[0], refs[1:]
+    dense_outs, refs = refs[:count], refs[count:]
+    expert_outs, refs = refs[:3], refs[3:]
+    gain_out, refs = refs[0], refs[1:]
+    buffers, sems = refs[: 4 * count + 15], refs[4 * count + 15 :]
+    work = ScatterAll(
+        place, dense, expert, dense_outs, expert_outs, gain, gain_out, buffers, sems
+    )
+    place.greet(everyone=True)
+    for a in range(count):
+        work.dense_start(a)
+    work.expert_start()
+    work.gmine[...] = gain[...]
+    for a in range(count):
+        work.dense_low(a)
+    for a in range(count):
+        work.dense_high(a)
+    work.dense_line(list(range(count)))
+    work.expert_all()
+    work.gains_all()
+    for a in range(count):
+        work.dense_finish(a)
+    for a in range(count):
+        work.dense_drain(a)
+    work.expert_drain()
+
+
+def scatter_gradients(sizes, dense, experts, gain):
+    depth, high_count = sizes
+    hbm = pl.BlockSpec(memory_space=pltpu.HBM)
+    vmem = pl.BlockSpec(memory_space=pltpu.VMEM)
+    count = len(dense)
+    rows = [a.shape[3] for a in dense]
+    features = gain.shape[1]
+    local_count = experts[0].shape[0]
+    width = experts[2].shape[1] // (2 * depth)
+    shapes = [jax.ShapeDtypeStruct(a.shape[3:], a.dtype) for a in dense]
+    shapes += [
+        jax.ShapeDtypeStruct(
+            (local_count,) + ((features, width) if a < 2 else (width, features)), experts[a].dtype
+        )
+        for a in range(3)
+    ]
+    shapes += [jax.ShapeDtypeStruct(gain.shape, gain.dtype)]
+    buffers, sems = ScatterAll.scratch(sizes, rows, features, local_count, width)
+    outs = pl.pallas_call(
+        functools.partial(scatter_kernel, sizes, count),
+        out_shape=shapes,
+        in_specs=[hbm] * (count + 3) + [vmem],
+        out_specs=[hbm] * (count + 3) + [vmem],
+        scratch_shapes=buffers + sems,
+        compiler_params=pltpu.CompilerParams(
+            collective_id=1, has_side_effects=True, vmem_limit_bytes=60 * MIB
+        ),
+        name="scatter_gradients",
+    )(*dense, *experts, gain)
+    return outs[:count], outs[count : count + 3], outs[count + 3]
+
+
+def on_device_plain(
     tokens,
     cotangent,
     gates,
@@ -71,29 +1447,29 @@
     micro_count = tokens.shape[2]
     row_count = tokens.shape[4]
     feature_count = tokens.shape[5]
-    owners = lax.axis_size("experts")
+    owners = lax.axis_size(EXPERTS)
     local_experts = expert_gate.shape[0]
     total_experts = owners * local_experts
     capacity = row_count * 8 // (3 * total_experts)
-    blocks = lax.axis_size("context")
+    blocks = lax.axis_size(CONTEXT)
     prompt = blocks * PB
     scaling = HD ** (-0.5)
     w_qkv, w_out, w_sgate, w_sup, w_sdown, w_gains = (
-        lax.all_gather(qkv_weight, ("context", "experts"), axis=1, tiled=True),
-        lax.all_gather(out_weight, ("context", "experts"), axis=0, tiled=True),
-        lax.all_gather(shared_gate, ("context", "experts"), axis=1, tiled=True),
-        lax.all_gather(shared_up, ("context", "experts"), axis=1, tiled=True),
-        lax.all_gather(shared_down, ("context", "experts"), axis=0, tiled=True),
-        lax.all_gather(gains, ("context", "experts"), axis=1, tiled=True),
+        lax.all_gather(qkv_weight, (CONTEXT, EXPERTS), axis=1, tiled=True),
+        lax.all_gather(out_weight, (CONTEXT, EXPERTS), axis=0, tiled=True),
+        lax.all_gather(shared_gate, (CONTEXT, EXPERTS), axis=1, tiled=True),
+        lax.all_gather(shared_up, (CONTEXT, EXPERTS), axis=1, tiled=True),
+        lax.all_gather(shared_down, (CONTEXT, EXPERTS), axis=0, tiled=True),
+        lax.all_gather(gains, (CONTEXT, EXPERTS), axis=1, tiled=True),
     )
     e_gate, expert_up_weight, e_down = (
-        lax.all_gather(expert_gate, ("dp", "context"), axis=2, tiled=True),
-        lax.all_gather(expert_up, ("dp", "context"), axis=2, tiled=True),
-        lax.all_gather(expert_down, ("dp", "context"), axis=1, tiled=True),
+        lax.all_gather(expert_gate, (DP, CONTEXT), axis=2, tiled=True),
+        lax.all_gather(expert_up, (DP, CONTEXT), axis=2, tiled=True),
+        lax.all_gather(expert_down, (DP, CONTEXT), axis=1, tiled=True),
     )
     gain_one = w_gains[0].astype(jnp.float32)
     gain_two = w_gains[1].astype(jnp.float32)
-    here_index = lax.axis_index("context")
+    here_index = lax.axis_index(CONTEXT)
     row_ids = jnp.arange(row_count, dtype=jnp.int32)
     query_pos = jnp.where(row_ids < PB, here_index * PB + row_ids, prompt + row_ids - PB)
     key_pos = jnp.arange(prompt + CONT, dtype=jnp.int32)
@@ -116,8 +1492,8 @@
         ).astype(jnp.bfloat16)
         value_rows = projected[:, 2 * feature_count :].astype(jnp.bfloat16)
         prompt_key, prompt_value = (
-            lax.all_gather(key_rows[:PB], "context", axis=0, tiled=True),
-            lax.all_gather(value_rows[:PB], "context", axis=0, tiled=True),
+            lax.all_gather(key_rows[:PB], CONTEXT, axis=0, tiled=True),
+            lax.all_gather(value_rows[:PB], CONTEXT, axis=0, tiled=True),
         )
         key_heads = jnp.concatenate([prompt_key, key_rows[PB:]], 0).reshape(prompt + CONT, H, HD)
         value_heads = jnp.concatenate([prompt_value, value_rows[PB:]], 0).reshape(
@@ -156,7 +1532,7 @@
         )
         padded = jnp.concatenate([normed_two, jnp.zeros((1, feature_count), jnp.bfloat16)], 0)
         send = padded[source // 2].reshape(total_experts, capacity, feature_count)
-        received = lax.all_to_all(send, "experts", split_axis=0, concat_axis=0, tiled=True)
+        received = lax.all_to_all(send, EXPERTS, split_axis=0, concat_axis=0, tiled=True)
         count = received.shape[1]
         expert_grouped = received.reshape(owners, local_experts, count, feature_count)
         expert_gate_act = jnp.einsum(
@@ -172,7 +1548,7 @@
         expert_out = result.reshape(owners * local_experts, count, feature_count)
         expert_in = received
         returned = lax.all_to_all(
-            expert_out, "experts", split_axis=0, concat_axis=0, tiled=True
+            expert_out, EXPERTS, split_axis=0, concat_axis=0, tiled=True
         ).reshape(-1, feature_count)
         gate_rows = gates[0, 0, step_index, 0]
         picked = returned[flat_dest].reshape(row_count, 2, feature_count).astype(jnp.float32)
@@ -252,7 +1628,7 @@
         )
         padded_grad = jnp.concatenate([d_pairs, jnp.zeros((1, feature_count), jnp.bfloat16)], 0)
         grad_send = padded_grad[source].reshape(total_experts, capacity, feature_count)
-        grad_in = lax.all_to_all(grad_send, "experts", split_axis=0, concat_axis=0, tiled=True)
+        grad_in = lax.all_to_all(grad_send, EXPERTS, split_axis=0, concat_axis=0, tiled=True)
         grouped_grad = grad_in.reshape(owners, local_experts, capacity, feature_count)
         grouped = expert_in.reshape(owners, local_experts, capacity, feature_count)
         gate_act = jnp.einsum("send,edf->senf", grouped, e_gate, preferred_element_type=jnp.float32)
@@ -289,7 +1665,7 @@
             total_experts, capacity, feature_count
         )
         back = lax.all_to_all(
-            d_expert_in, "experts", split_axis=0, concat_axis=0, tiled=True
+            d_expert_in, EXPERTS, split_axis=0, concat_axis=0, tiled=True
         ).reshape(-1, feature_count)
         d_normed_two = d_normed_two + jnp.sum(
             back[flat_dest].reshape(row_count, 2, feature_count).astype(jnp.float32), 1
@@ -339,10 +1715,10 @@
         ).reshape(prompt + CONT, feature_count)
         own_dkey, own_dvalue = (
             lax.psum_scatter(
-                d_keys[:prompt].astype(jnp.bfloat16), "context", scatter_dimension=0, tiled=True
+                d_keys[:prompt].astype(jnp.bfloat16), CONTEXT, scatter_dimension=0, tiled=True
             ).astype(jnp.float32),
             lax.psum_scatter(
-                d_values[:prompt].astype(jnp.bfloat16), "context", scatter_dimension=0, tiled=True
+                d_values[:prompt].astype(jnp.bfloat16), CONTEXT, scatter_dimension=0, tiled=True
             ).astype(jnp.float32),
         )
         d_key_rows = jnp.concatenate([own_dkey, d_keys[prompt:]], 0)
@@ -367,34 +1743,34 @@
         input_list.append(d_inputs.astype(jnp.bfloat16))
     sharded_expert_gate, sharded_expert_up, sharded_expert_down = (
         lax.psum_scatter(
-            local_egate.astype(jnp.bfloat16), ("dp", "context"), scatter_dimension=2, tiled=True
+            local_egate.astype(jnp.bfloat16), (DP, CONTEXT), scatter_dimension=2, tiled=True
         ).astype(jnp.float32),
         lax.psum_scatter(
             local_expert_up_weight.astype(jnp.bfloat16),
-            ("dp", "context"),
+            (DP, CONTEXT),
             scatter_dimension=2,
             tiled=True,
         ).astype(jnp.float32),
         lax.psum_scatter(
-            local_edown.astype(jnp.bfloat16), ("dp", "context"), scatter_dimension=1, tiled=True
+            local_edown.astype(jnp.bfloat16), (DP, CONTEXT), scatter_dimension=1, tiled=True
         ).astype(jnp.float32),
     )
     acc_gains = jnp.stack([acc_gain_one, acc_gain_two], 0)
     dense_shards = (
-        lax.psum_scatter(acc_qkv, ("context", "experts"), scatter_dimension=1, tiled=True),
-        lax.psum_scatter(acc_out, ("context", "experts"), scatter_dimension=0, tiled=True),
-        lax.psum_scatter(acc_sgate, ("context", "experts"), scatter_dimension=1, tiled=True),
-        lax.psum_scatter(acc_sup, ("context", "experts"), scatter_dimension=1, tiled=True),
-        lax.psum_scatter(acc_sdown, ("context", "experts"), scatter_dimension=0, tiled=True),
-        lax.psum_scatter(acc_gains, ("context", "experts"), scatter_dimension=1, tiled=True),
+        lax.psum_scatter(acc_qkv, (CONTEXT, EXPERTS), scatter_dimension=1, tiled=True),
+        lax.psum_scatter(acc_out, (CONTEXT, EXPERTS), scatter_dimension=0, tiled=True),
+        lax.psum_scatter(acc_sgate, (CONTEXT, EXPERTS), scatter_dimension=1, tiled=True),
+        lax.psum_scatter(acc_sup, (CONTEXT, EXPERTS), scatter_dimension=1, tiled=True),
+        lax.psum_scatter(acc_sdown, (CONTEXT, EXPERTS), scatter_dimension=0, tiled=True),
+        lax.psum_scatter(acc_gains, (CONTEXT, EXPERTS), scatter_dimension=1, tiled=True),
     )
     grad_qkv, grad_out, grad_sgate, grad_sup, grad_sdown, grad_gains = (
-        lax.psum(dense_shards[0].astype(jnp.bfloat16), "dp").astype(jnp.float32),
-        lax.psum(dense_shards[1].astype(jnp.bfloat16), "dp").astype(jnp.float32),
-        lax.psum(dense_shards[2].astype(jnp.bfloat16), "dp").astype(jnp.float32),
-        lax.psum(dense_shards[3].astype(jnp.bfloat16), "dp").astype(jnp.float32),
-        lax.psum(dense_shards[4].astype(jnp.bfloat16), "dp").astype(jnp.float32),
-        lax.psum(dense_shards[5].astype(jnp.bfloat16), "dp").astype(jnp.float32),
+        lax.psum(dense_shards[0].astype(jnp.bfloat16), DP).astype(jnp.float32),
+        lax.psum(dense_shards[1].astype(jnp.bfloat16), DP).astype(jnp.float32),
+        lax.psum(dense_shards[2].astype(jnp.bfloat16), DP).astype(jnp.float32),
+        lax.psum(dense_shards[3].astype(jnp.bfloat16), DP).astype(jnp.float32),
+        lax.psum(dense_shards[4].astype(jnp.bfloat16), DP).astype(jnp.float32),
+        lax.psum(dense_shards[5].astype(jnp.bfloat16), DP).astype(jnp.float32),
     )
     mixed = jnp.stack(mixed_list, 0).reshape(tokens.shape)
     input_grad = jnp.stack(input_list, 0).reshape(tokens.shape)
@@ -413,37 +1789,251 @@
     )
 
 
+def on_device(
+    tokens,
+    cotangent,
+    gates,
+    routes,
+    qkv_weight,
+    out_weight,
+    shared_gate,
+    shared_up,
+    shared_down,
+    gains,
+    expert_gate,
+    expert_up,
+    expert_down,
+):
+    micro_count = tokens.shape[2]
+    row_count = tokens.shape[4]
+    feature_count = tokens.shape[5]
+    owners = lax.axis_size(EXPERTS)
+    local_experts = expert_gate.shape[0]
+    total_experts = owners * local_experts
+    capacity = row_count * 8 // (3 * total_experts)
+    blocks = lax.axis_size(CONTEXT)
+    prompt = blocks * PB
+    scaling = HD ** (-0.5)
+    sizes = (blocks, owners // 2)
+    own_at = lax.axis_index(CONTEXT) * owners + lax.axis_index(EXPERTS)
+    gain_width = gains.shape[1]
+    gain_rows = lax.dynamic_update_slice(
+        jnp.zeros((16, feature_count), jnp.bfloat16), gains, (0, own_at * gain_width)
+    )
+    (
+        w_qkv, w_out, w_gains, _, _, _, _, _, _,
+        n1_all, k_all, v_all, q_all, att_all, hid_all, lse_all, side_all, dn2_all,
+        gsg, gsu, gsd, geg, geu, ged, outs, dins,
+    ) = run_forward(
+        sizes,
+        tokens[0, 0, :, 0],
+        cotangent[0, 0, :, 0],
+        gates[0, 0, :, 0].transpose(0, 2, 1),
+        routes[0, 0, :, 0].transpose(0, 2, 1),
+        (qkv_weight.T, out_weight, gain_rows, shared_gate, shared_up, shared_down),
+        (expert_gate, expert_up, expert_down),
+    )
+    gain_one, gain_two = w_gains[0], w_gains[1]
+    here_index = lax.axis_index(CONTEXT)
+    row_ids = jnp.arange(row_count, dtype=jnp.int32)
+    query_pos = jnp.where(row_ids < PB, here_index * PB + row_ids, prompt + row_ids - PB)
+    key_pos = jnp.arange(prompt + CONT, dtype=jnp.int32)
+    allowed = key_pos[None, None, :] <= query_pos[None, :, None]
+    half_size = HD // 2
+    frequency = 10000.0 ** (-2.0 * jnp.arange(half_size, dtype=jnp.float32) / HD)
+    angles = query_pos.astype(jnp.float32)[:, None] * frequency
+    cosine = jnp.cos(angles)[:, None, :]
+    sine_part = jnp.sin(angles)[:, None, :]
+    acc_qkv = jnp.zeros(w_qkv.shape, jnp.float32)
+    acc_out = jnp.zeros(w_out.shape, jnp.float32)
+    acc_gain_one = jnp.zeros((feature_count,), jnp.float32)
+    acc_gain_two = jnp.zeros((feature_count,), jnp.float32)
+    mixed_list = []
+    input_list = []
+    for step_index in range(micro_count):
+        inputs = tokens[0, 0, step_index, 0].astype(jnp.float32)
+        root_one = lax.rsqrt(jnp.mean(inputs * inputs, -1, keepdims=True) + EPSILON)
+        hidden = hid_all[step_index]
+        root_two = lax.rsqrt(jnp.mean(hidden * hidden, -1, keepdims=True) + EPSILON)
+        grad_rows = cotangent[0, 0, step_index, 0].astype(jnp.float32)
+        rows_here = slice(step_index * row_count, (step_index + 1) * row_count)
+        side, d_normed_two = side_all[rows_here], dn2_all[rows_here]
+        route_rows = routes[0, 0, step_index, 0]
+        slots = slot_table(route_rows, total_experts)
+        flat_dest = (route_rows * capacity + slots).reshape(-1)
+        gate_rows = gates[0, 0, step_index, 0]
+
+        def come_back(item):
+            item = item.reshape(local_experts, micro_count, owners, capacity, feature_count)
+            item = item[:, step_index].transpose(1, 0, 2, 3)
+            item = item.reshape(total_experts, capacity, feature_count)
+            return lax.all_to_all(item, EXPERTS, split_axis=0, concat_axis=0, tiled=True).reshape(-1, feature_count)
+
+        returned, back = come_back(outs), come_back(dins)
+        picked = returned[flat_dest].reshape(row_count, 2, feature_count).astype(jnp.float32)
+        routed = jnp.sum(gate_rows[:, :, None] * picked, 1)
+        mixed_list.append((hidden + routed + side).astype(jnp.bfloat16))
+        d_normed_two = d_normed_two + jnp.sum(
+            back[flat_dest].reshape(row_count, 2, feature_count).astype(jnp.float32), 1
+        )
+        query, key_rows, value_rows = q_all[step_index], k_all[step_index], v_all[step_index]
+        attended = att_all[step_index]
+        log_total = lse_all[step_index][:, :H].T[:, :, None]
+        normed_one = jnp.concatenate(
+            [
+                lax.dynamic_slice(n1_all[step_index], (here_index * PB, 0), (PB, feature_count)),
+                n1_all[step_index][prompt:],
+            ],
+            0,
+        )
+        scaled_two = gain_two * d_normed_two
+        d_hidden = (
+            grad_rows
+            + root_two * scaled_two
+            - hidden * root_two**3 * jnp.mean(hidden * scaled_two, -1, keepdims=True)
+        )
+        acc_gain_two = acc_gain_two + jnp.sum(d_normed_two * hidden * root_two, 0)
+        d_attn = d_hidden.astype(jnp.bfloat16)
+        acc_out = acc_out + tdot(attended, d_attn)
+        d_attended = ndot(d_attn, w_out).astype(jnp.bfloat16)
+        key_heads = key_rows.reshape(prompt + CONT, H, HD)
+        value_heads = value_rows.reshape(prompt + CONT, H, HD)
+        query_heads = query.reshape(row_count, H, HD)
+        scores = (
+            jnp.einsum("qhd,khd->hqk", query_heads, key_heads, preferred_element_type=jnp.float32)
+        )
+        scores = jnp.where(allowed, scores, -1000000000.0)
+        probs = jnp.exp(scores - log_total)
+        d_heads = d_attended.reshape(row_count, H, HD)
+        d_probs = jnp.einsum(
+            "qhd,khd->hqk", d_heads, value_heads, preferred_element_type=jnp.float32
+        )
+        centre = jnp.sum(probs * d_probs, -1, keepdims=True)
+        d_scores = (probs * (d_probs - centre)).astype(jnp.bfloat16)
+        d_query = (
+            jnp.einsum(
+                "hqk,khd->qhd", d_scores, key_heads, preferred_element_type=jnp.float32
+            ).reshape(row_count, feature_count)
+            * scaling
+        )
+        d_keys = (
+            jnp.einsum(
+                "hqk,qhd->khd", d_scores, query_heads, preferred_element_type=jnp.float32
+            ).reshape(prompt + CONT, feature_count)
+        )
+        d_values = jnp.einsum(
+            "hqk,qhd->khd", probs.astype(jnp.bfloat16), d_heads, preferred_element_type=jnp.float32
+        ).reshape(prompt + CONT, feature_count)
+        own_dkey, own_dvalue = (
+            lax.psum_scatter(
+                d_keys[:prompt].astype(jnp.bfloat16), CONTEXT, scatter_dimension=0, tiled=True
+            ).astype(jnp.float32),
+            lax.psum_scatter(
+                d_values[:prompt].astype(jnp.bfloat16), CONTEXT, scatter_dimension=0, tiled=True
+            ).astype(jnp.float32),
+        )
+        d_key_rows = jnp.concatenate([own_dkey, d_keys[prompt:]], 0)
+        d_value_rows = jnp.concatenate([own_dvalue, d_values[prompt:]], 0)
+        d_projected = jnp.concatenate(
+            [
+                rotate(d_query, cosine, -sine_part).astype(jnp.bfloat16),
+                rotate(d_key_rows, cosine, -sine_part).astype(jnp.bfloat16),
+                d_value_rows.astype(jnp.bfloat16),
+            ],
+            1,
+        )
+        acc_qkv = acc_qkv + tdot(d_projected, normed_one)
+        d_normed_one = mdot(d_projected, w_qkv)
+        scaled_one = gain_one * d_normed_one
+        d_inputs = (
+            d_hidden
+            + root_one * scaled_one
+            - inputs * root_one**3 * jnp.mean(inputs * scaled_one, -1, keepdims=True)
+        )
+        acc_gain_one = acc_gain_one + jnp.sum(d_normed_one * inputs * root_one, 0)
+        input_list.append(d_inputs.astype(jnp.bfloat16))
+    acc_gains = jnp.concatenate(
+        [acc_gain_one[None], acc_gain_two[None], jnp.zeros((6, feature_count), jnp.float32)], 0
+    )
+    dense_sums, expert_sums, gain_sum = scatter_gradients(
+        sizes,
+        tuple(
+            item.astype(jnp.bfloat16).reshape(blocks, owners // 2, 2, -1, feature_count)
+            for item in (acc_qkv, acc_out, gsg.T, gsu.T, gsd)
+        ),
+        (geg, geu, ged),
+        acc_gains,
+    )
+    grad_qkv, grad_out, grad_sgate, grad_sup, grad_sdown = (
+        item.astype(jnp.float32) for item in dense_sums
+    )
+    grad_qkv, grad_sgate, grad_sup = grad_qkv.T, grad_sgate.T, grad_sup.T
+    grad_gains = lax.dynamic_slice(gain_sum, (0, own_at * gain_width), (2, gain_width))
+    sharded_expert_gate, sharded_expert_up, sharded_expert_down = (
+        item.astype(jnp.float32) for item in expert_sums
+    )
+    mixed = jnp.stack(mixed_list, 0).reshape(tokens.shape)
+    input_grad = jnp.stack(input_list, 0).reshape(tokens.shape)
+    return (
+        mixed,
+        input_grad,
+        grad_qkv,
+        grad_out,
+        grad_sgate,
+        grad_sup,
+        grad_sdown,
+        grad_gains,
+        sharded_expert_gate,
+        sharded_expert_up,
+        sharded_expert_down,
+    )
+
+
+def kernels_fit(mesh_shape, arrays):
+    qkv_weight, out_weight, shared_gate, _, shared_down = arrays[4:9]
+    rows = (qkv_weight.shape[1], out_weight.shape[0], shared_gate.shape[1], shared_down.shape[0])
+    return (
+        mesh_shape[DP] == 2
+        and mesh_shape[EXPERTS] % 2 == 0
+        and all(count % 16 == 0 for count in rows)
+        and arrays[10].shape[2] % 128 == 0
+    )
+
+
 def solution(mesh):
+    def device_program(*arrays):
+        return (on_device if kernels_fit(mesh.shape, arrays) else on_device_plain)(*arrays)
+
     return jax.shard_map(
-        on_device,
+        device_program,
         mesh=mesh,
         in_specs=(
-            P("dp", "experts", None, "context", None, None),
-            P("dp", "experts", None, "context", None, None),
-            P("dp", "experts", None, "context", None, None),
-            P("dp", "experts", None, "context", None, None),
-            P(None, ("context", "experts")),
-            P(("context", "experts"), None),
-            P(None, ("context", "experts")),
-            P(None, ("context", "experts")),
-            P(("context", "experts"), None),
-            P(None, ("context", "experts")),
-            P("experts", None, ("dp", "context")),
-            P("experts", None, ("dp", "context")),
-            P("experts", ("dp", "context"), None),
+            P(DP, EXPERTS, None, CONTEXT, None, None),
+            P(DP, EXPERTS, None, CONTEXT, None, None),
+            P(DP, EXPERTS, None, CONTEXT, None, None),
+            P(DP, EXPERTS, None, CONTEXT, None, None),
+            P(None, (CONTEXT, EXPERTS)),
+            P((CONTEXT, EXPERTS), None),
+            P(None, (CONTEXT, EXPERTS)),
+            P(None, (CONTEXT, EXPERTS)),
+            P((CONTEXT, EXPERTS), None),
+            P(None, (CONTEXT, EXPERTS)),
+            P(EXPERTS, None, (DP, CONTEXT)),
+            P(EXPERTS, None, (DP, CONTEXT)),
+            P(EXPERTS, (DP, CONTEXT), None),
         ),
         out_specs=(
-            P("dp", "experts", None, "context", None, None),
-            P("dp", "experts", None, "context", None, None),
-            P(None, ("context", "experts")),
-            P(("context", "experts"), None),
-            P(None, ("context", "experts")),
-            P(None, ("context", "experts")),
-            P(("context", "experts"), None),
-            P(None, ("context", "experts")),
-            P("experts", None, ("dp", "context")),
-            P("experts", None, ("dp", "context")),
-            P("experts", ("dp", "context"), None),
+            P(DP, EXPERTS, None, CONTEXT, None, None),
+            P(DP, EXPERTS, None, CONTEXT, None, None),
+            P(None, (CONTEXT, EXPERTS)),
+            P((CONTEXT, EXPERTS), None),
+            P(None, (CONTEXT, EXPERTS)),
+            P(None, (CONTEXT, EXPERTS)),
+            P((CONTEXT, EXPERTS), None),
+            P(None, (CONTEXT, EXPERTS)),
+            P(EXPERTS, None, (DP, CONTEXT)),
+            P(EXPERTS, None, (DP, CONTEXT)),
+            P(EXPERTS, (DP, CONTEXT), None),
         ),
         check_vma=False,
     )

time: 1790 us -> 1040 us (0.58)
  waiting for transfers between devices: 1010 us -> 31.6 us
  Pallas kernels: 0 us -> 689 us
  matrix products: 350 us -> 84.1 us
  blocking collectives: 122 us -> 0 us
  local copies, waits for them, and re-layouts: 153 us -> 124 us
  other arithmetic: 98.5 us -> 72.1 us
    pallas_call x0 -> x2, Pallas kernels: none -> 689 us  [the longest x1 373 us: run_forward(): pl.pallas_call(functools.partial(forward_kernel, sizes), out_shape=out_sh...]
    reduce_scatter x8 -> x0, waiting for transfers between devices: 612 us -> none  [the longest x1 119 us: on_device(): lax.psum_scatter(local_expert_up_weight.astype(jnp.bfloat16), ('dp', 'con...]
    all_gather x8 -> x0, waiting for transfers between devices: 241 us -> none  [the longest x1 91.6 us: on_device(): lax.all_gather(expert_gate, ('dp', 'context'), axis=2, tiled=True)]
    dot_general x20 -> x0, matrix products: 174 us -> none  [the longest x2 27.4 us: on_device(): jnp.einsum('send,efd->senf', grouped_grad, e_down, preferred_element_type...]
    all_gather x5 -> x0, blocking collectives: 117 us -> none  [the longest x2 56 us: on_device(): lax.all_gather(key_rows[:PB], 'context', axis=0, tiled=True)]
    unnamed x27 -> x8, waiting for transfers between devices: 59.1 us -> 14.7 us
    all_to_all x8 -> x4, waiting for transfers between devices: 56.2 us -> 16.9 us  [come_back(): lax.all_to_all(item, EXPERTS, split_axis=0, concat_axis=0, tiled=True)]
    psum x1 -> x0, waiting for transfers between devices: 37.1 us -> none  [on_device(): lax.psum(dense_shards[0].astype(jnp.bfloat16), 'dp').astype(jnp.float32)]
  transfers between devices with their start and end apart: 30 -> 8, of which waited for: 19 -> 3; matrix products, arithmetic and copies ran while one was open for 26% -> 17% of each run, Pallas kernels for 0% -> 0%
where the time goes in v1:
time: 1040 us; the launch traced here: 1030 us
  Pallas kernels  689 us (66%)
  local copies, waits for them, and re-layouts  124 us (12%)
  matrix products  84.1 us (8%)
  other arithmetic  72.1 us (7%)
  waiting for transfers between devices  31.6 us (3%)
  starting transfers between devices  16.8 us (2%)
  between operations  15.3 us (1%)
    pallas_call x1, Pallas kernels, run_forward(): pl.pallas_call(functools.partial(forward_kernel, sizes), out_shape=out_sh...  373 us
    pallas_call x1, Pallas kernels, scatter_gradients(): pl.pallas_call(functools.partial(scatter_kernel, sizes, count), out_shape...  315 us
    unnamed x170, local copies, waits for them, and re-layouts  33.9 us
    convert_element_type x2, other arithmetic, on_device(): d_scores = (probs * (d_probs - centre)).astype(jnp.bfloat16)  22.9 us
  transfers between devices with their start and end apart: 8, of which 3 were waited for; matrix products, arithmetic and copies ran while one was open for 17% of the time, Pallas kernels for 0%

profile of v1, /device:TPU:0, one launch (start us, length us, event | category | flops | bytes accessed | tf_op | source)
XLA Modules:
  0.0 1032.3 jit_solution(10031789227943043881)
XLA Ops:
  9.3 373.4 %gather_and_forward.1 = (bf16[2304,768]{1,0:T(8,128)(2,1)}, bf16[768,768]{1,0:T(8,128)(2,1)}, f32[8,768]{1,0:T(8,128)}, bf16[768,2048]{1,0:T(8,128)(2,1)}, bf16[...) custom-call(bf16[2,384,768]{2,1,0:T(8,128)(2,1)} %bitcast.260, ...), custom_call_target="tpu_custom_call" | custom-call | tf_op jit(solution)/shard_map/gather_and_forward/pallas_call | solution.py:936
  438.8 4.5 all-to-all-start.1
  450.4 13.1 %all-to-all-done.1 = bf16[8,128,768]{2,1,0:T(8,128)(2,1)} async-done(((bf16[8,128,768]{2,1,0:T(8,128)(2,1)}), bf16[8,128,768]{2,1,0:T(8,128)(2,1)}, u32[]{:S(2)}, u32[]{:S(2)}) %all-to-all-start.1) | async-done | bytes 1572896 | tf_op jit(solution)/shard_map/all_to_all | solution.py:1870
  463.5 4.3 all-to-all-start
  486.2 4.5 reduce_sum.191
  490.7 4.5 reduce_sum.197
  495.2 4.9 gather_fusion.1
  502.4 5.3 gather_fusion
  509.9 7.5 multiply_reduce_fusion.2
  523.1 8.6 fusion.94
  531.8 8.1 multiply_reduce_fusion
  539.9 11.5 %multiply_convert_fusion = bf16[12,384,768]{2,1,0:T(8,128)(2,1)S(1)} fusion(f32[12,384,768]{2,1,0:T(8,128)S(1)} %get-tuple-element.175, f32[12,384,768]{2,1,0:T(8,128)} %fusion.94, f32[12,384]{1,0:T(8,128)S(1)} %get-tuple-element.174), kind=kLoop, calls=%fused_computation.4 | loop fusion | flops 10616832 | bytes 35407872 | tf_op jit(solution)/shard_map/convert_element_type | solution.py:1912
  562.7 8.5 fusion.93
  571.2 10.4 %multiply_reduce_fusion.1 = (f32[12,384]{1,0:T(8,128)S(1)}, f32[12,384,768]{2,1,0:T(8,128)S(1)}) fusion(f32[12,384,768]{2,1,0:T(8,128)} %fusion.93, f32[12,384]{1,0:T(8,128)S(1)} %copy-done.53, bf16[384,12,64]{0,2,1:T(8,128)(2,1)} %bitcast.261, bf16[768,12,64]{0,2,1:T(8,128)(2,1)} %bitcast.258, pred[384,768]{1,0:T(8,128)(4,1)} %iota_compare_fusion), kind=kOutput, calls=%fused_computation.8 | convolution fusion | flops 467136000 | bytes 30412800 | tf_op jit(solution)/shard_map/qhd,khd->hqk/dot_general | solution.py:1903
  581.6 11.5 %multiply_convert_fusion.1 = bf16[12,384,768]{2,1,0:T(8,128)(2,1)S(1)} fusion(f32[12,384,768]{2,1,0:T(8,128)S(1)} %get-tuple-element.173, f32[12,384,768]{2,1,0:T(8,128)} %fusion.93, f32[12,384]{1,0:T(8,128)S(1)} %get-tuple-element.172), kind=kLoop, calls=%fused_computation.7 | loop fusion | flops 10616832 | bytes 35407872 | tf_op jit(solution)/shard_map/convert_element_type | solution.py:1912
  600.1 4.7 copy.112
  604.7 4.7 copy.113
  610.9 6.7 fusion.10
  621.9 7.6 fusion.13
  642.6 3.9 add_convert_fusion.1
  662.2 14.6 %reduce-scatter.15.cloned.1.call-done = bf16[128,768]{1,0:T(8,128)(2,1)} async-done(((bf16[512,768]{1,0:T(8,128)(2,1)}), bf16[128,768]{1,0:T(8,128)(2,1)}) %reduce-scatter.15.cloned.1.call-update) | async-done | bytes 196624
  678.6 5.7 fusion.24
  686.5 6.0 add_convert_fusion
  693.2 315.2 %scatter_gradients.1 = (bf16[144,768]{1,0:T(8,128)(2,1)}, bf16[48,768]{1,0:T(8,128)(2,1)}, bf16[128,768]{1,0:T(8,128)(2,1)}, bf16[128,768]{1,0:T(8,128)(2,1)}, b...) custom-call(bf16[4,2,2,144,768]{4,3,2,1,0:T(8,128)(2,1)} %bitcast.27, ...), custom_call_target="tpu_custom_call" | custom-call | tf_op jit(solution)/shard_map/scatter_gradients/pallas_call | solution.py:1418
  (309 shorter events, 167.4 us)
Async XLA Ops:
  386.1 23.7 %all-to-all-start.2 = ((bf16[8,128,768]{2,1,0:T(8,128)(2,1)}), bf16[8,128,768]{2,1,0:T(8,128)(2,1)S(1)}, u32[]{:S(2)}, u32[]{:S(2)}) async-start(bf16[8,128,768]{2,1,0:T(8,128)(2,1)} %bitcast.34), calls=%async_computation.2 | async-start | bytes 3145728 | tf_op jit(solution)/shard_map/all_to_all | solution.py:1870
  409.9 28.9 %all-to-all-start.3 = ((bf16[8,128,768]{2,1,0:T(8,128)(2,1)}), bf16[8,128,768]{2,1,0:T(8,128)(2,1)S(1)}, u32[]{:S(2)}, u32[]{:S(2)}) async-start(bf16[8,128,768]{2,1,0:T(8,128)(2,1)} %bitcast.267), calls=%async_computation.3 | async-start | bytes 3145728 | tf_op jit(solution)/shard_map/all_to_all | solution.py:1870
  438.8 24.6 %all-to-all-start.1 = ((bf16[8,128,768]{2,1,0:T(8,128)(2,1)}), bf16[8,128,768]{2,1,0:T(8,128)(2,1)}, u32[]{:S(2)}, u32[]{:S(2)}) async-start(bf16[8,128,768]{2,1,0:T(8,128)(2,1)} %bitcast.266), calls=%async_computation.1 | async-start | bytes 3145728 | tf_op jit(solution)/shard_map/all_to_all | solution.py:1870
  463.5 38.9 %all-to-all-start = ((bf16[8,128,768]{2,1,0:T(8,128)(2,1)}), bf16[8,128,768]{2,1,0:T(8,128)(2,1)}, u32[]{:S(2)}, u32[]{:S(2)}) async-start(bf16[8,128,768]{2,1,0:T(8,128)(2,1)} %bitcast.265), calls=%async_computation | async-start | bytes 3145728 | tf_op jit(solution)/shard_map/all_to_all | solution.py:1870
  467.8 184.3 %reduce-scatter.17.cloned.1.call-start = ((), (), s32[]{:S(2)}) async-start(), calls=%async_computation.10 | async-start | bytes 983040
  521.0 108.7 %copy-start.5 = (f32[384,768]{1,0:T(8,128)}, f32[384,768]{1,0:T(8,128)S(1)}, u32[]{:S(2)}) copy-start(f32[384,768]{1,0:T(8,128)S(1)} %get-tuple-element.120) | copy-start | bytes 3538948
  523.1 8.7 copy-start.20
  523.1 8.6 copy-start.12
  523.1 8.6 copy-start.18
  523.1 8.6 copy-start.54
  539.9 11.5 %copy-start = (f32[12,384,768]{2,1,0:T(8,128)}, f32[12,384,768]{2,1,0:T(8,128)S(1)}, u32[]{:S(2)}) copy-start(f32[12,384,768]{2,1,0:T(8,128)S(1)} %get-tuple-element.175) | copy-start | bytes 42467332
  539.9 11.5 %copy-start.19 = (bf16[1,384,768]{1,2,0:T(8,128)(2,1)S(1)}, bf16[1,384,768]{1,2,0:T(8,128)(2,1)}, u32[]{:S(2)}) copy-start(bf16[1,384,768]{1,2,0:T(8,128)(2,1)} %copy.108) | copy-start | bytes 1769476
  554.2 80.6 %copy-start.10 = (f32[768,12,64]{0,2,1:T(8,128)}, f32[768,12,64]{0,2,1:T(8,128)S(1)}, u32[]{:S(2)}) copy-start(f32[768,12,64]{0,2,1:T(8,128)S(1)} %convolution_bitcast_fusion) | copy-start | bytes 7077892
  557.6 95.7 %reduce-scatter.13.cloned.1.call-start = ((), (), s32[]{:S(2)}) async-start(), calls=%async_computation.8 | async-start | bytes 983040
  562.7 8.5 copy-start.53
  581.6 11.5 %copy-start.1 = (f32[12,384,768]{2,1,0:T(8,128)}, f32[12,384,768]{2,1,0:T(8,128)S(1)}, u32[]{:S(2)}) copy-start(f32[12,384,768]{2,1,0:T(8,128)S(1)} %get-tuple-element.173) | copy-start | bytes 42467332
  581.6 11.5 %copy-start.17 = (bf16[1,384,768]{1,2,0:T(8,128)(2,1)S(1)}, bf16[1,384,768]{1,2,0:T(8,128)(2,1)}, u32[]{:S(2)}) copy-start(bf16[1,384,768]{1,2,0:T(8,128)(2,1)} %copy.102) | copy-start | bytes 1769476
  600.0 54.5 %reduce-scatter.19.cloned.1.call-start = ((), (), s32[]{:S(2)}) async-start(), calls=%async_computation.11 | async-start | bytes 983040
  629.5 47.3 %reduce-scatter.15.cloned.1.call-start = ((), (), s32[]{:S(2)}) async-start(), calls=%async_computation.9 | async-start | bytes 983040
  634.8 11.7 %slice-start.2 = ((s8[7077888]{0:T(1024)(128)(4,1)}), s8[2883584]{0:T(1024)(128)(4,1)S(1)}, s32[]{:S(2)}) async-start(s8[7077888]{0:T(1024)(128)(4,1)} %bitcast.250), calls=%async_computation.14 | async-start | bytes 5767168
  660.6 17.9 %copy-start.15 = (bf16[1,1,2,1,384,768]{5,4,3,2,1,0:T(8,128)(2,1)S(1)}, bf16[1,1,2,1,384,768]{5,4,3,2,1,0:T(8,128)(2,1)}, u32[]{:S(2)}) copy-start(bf16[1,1,2,1,384,768]{5,4,3,2,1,0:T(8,128)(2,1)} %param.15) | copy-start | bytes 3538948
  660.6 17.9 %copy-start.59 = (f32[768]{0:T(1024)S(1)}, f32[768]{0:T(1024)}, u32[]{:S(2)}) copy-start(f32[768]{0:T(1024)} %get-tuple-element.118) | copy-start | bytes 9220
  660.6 17.9 %copy-start.64 = (f32[384]{0:T(512)S(1)}, f32[384]{0:T(512)}, u32[]{:S(2)}) copy-start(f32[384]{0:T(512)} %get-tuple-element.167) | copy-start | bytes 4612
  660.6 17.9 %copy-start.66 = (f32[384]{0:T(512)S(1)}, f32[384]{0:T(512)}, u32[]{:S(2)}) copy-start(f32[384]{0:T(512)} %get-tuple-element.183) | copy-start | bytes 4612
  (64 other events, 237.1 us)
Sparse Core Ops, SparseCore 0:
  557.7 22.4 reduce-scatter.16
  600.1 22.4 reduce-scatter.12
  629.6 22.4 reduce-scatter.18
  654.2 22.5 reduce-scatter.14

commit v2 on v1

--- a/solution.py
+++ b/solution.py
@@ -119,10 +119,9 @@
         signal(dp=1 - self.x)
         for step in range(1, self.owners):
             signal(experts=self.peer_owner(step))
-        pl.when(self.z > 0)(lambda: signal(context=self.z - 1))
-        pl.when(self.z < self.depth - 1)(lambda: signal(context=self.z + 1))
-        count = 1 + self.owners - 1
-        count += jnp.where(self.z > 0, 1, 0) + jnp.where(self.z < self.depth - 1, 1, 0)
+        for step in range(1, self.depth):
+            signal(context=lax.rem(self.z + step, self.depth))
+        count = self.owners + self.depth - 1
         pl.semaphore_wait(barrier, count)
 
 
@@ -946,487 +945,842 @@
     )(tokens, cot, gates, routes, cosine, sine_part, *dense, *experts)
 
 
-class PlaceS:
-    def __init__(self, sizes):
-        self.depth, self.high_count = sizes
-        self.x = lax.axis_index(DP)
-        self.z = lax.axis_index(CONTEXT)
-        self.e = lax.axis_index(EXPERTS)
-        self.high = self.e // 2
-        self.low = self.e % 2
-
-    def shard(self, z):
-        return self.x * self.depth + z
-
-    def other_shard(self, z):
-        return (1 - self.x) * self.depth + z
-
-    def peer_high(self, step):
-        return lax.rem(self.high + step, self.high_count)
-
-    def greet(self, everyone=False):
-        barrier = pltpu.get_barrier_semaphore()
-
-        def signal(**device):
-            pl.semaphore_signal(barrier, inc=1, device_id=device, device_id_type=MESH)
-
-        signal(dp=1 - self.x)
-        signal(experts=self.e + 1 - 2 * self.low)
-        count = 2
-        for step in range(1, self.high_count):
-            signal(experts=self.peer_high(step) * 2 + self.low)
-            count += 1
-            if everyone:
-                signal(experts=self.peer_high(step) * 2 + 1 - self.low)
-                count += 1
-        if everyone:
-            for step in range(1, self.depth):
-                signal(context=lax.rem(self.z + step, self.depth))
-                count += 1
-            pl.semaphore_wait(barrier, count)
-        else:
-            pl.when(self.z > 0)(lambda: signal(context=self.z - 1))
-            pl.when(self.z < self.depth - 1)(lambda: signal(context=self.z + 1))
-            count += jnp.where(self.z > 0, 1, 0) + jnp.where(self.z < self.depth - 1, 1, 0)
-            pl.semaphore_wait(barrier, count)
-
-
-def slab(ref, index, rows):
-    return ref.at[pl.ds(pl.multiple_of(index * rows, 16), rows)]
-
-
-def add_into(target, sources, rows):
-    total = target.shape[0]
-
-    def body(i, carry):
-        here = pl.ds(pl.multiple_of(i * rows, rows), rows)
-        value = target[here, :].astype(jnp.float32)
+def add_into(target, sources, step):
+    def body(here):
+        value = target[here, :].astype(F32)
         for source in sources:
-            value = value + source[here, :].astype(jnp.float32)
+            value = value + source[here, :].astype(F32)
         target[here, :] = value.astype(target.dtype)
-        return carry
-
-    lax.fori_loop(0, total // rows, body, 0)
-
-
-class ScatterAll:
-    def __init__(self, place, dense, expert, dense_outs, expert_outs, gain, gain_out, buffers, sems):
-        self.place = place
-        self.dense, self.expert = dense, expert
-        self.dense_outs, self.expert_outs = dense_outs, expert_outs
-        self.gain, self.gain_out = gain, gain_out
-        count = len(dense)
-        self.count = count
-        self.dlow = buffers[:count]
-        self.dhigh = buffers[count : 2 * count]
-        self.dline = buffers[2 * count : 3 * count]
-        self.dcross = buffers[3 * count : 4 * count]
-        rest = buffers[4 * count :]
-        self.dense_own, self.ecross, self.eline, self.eown = rest[0], rest[1:4], rest[4:7], rest[7:10]
-        self.gmine, self.glow, self.ghigh, self.gline, self.gcross = rest[10:15]
+
+    tiles(target.shape[0], step, body)
+
+
+class LineSum:
+    def __init__(self, place, part, land, send_sem, recv_sem):
+        self.place, self.part, self.land = place, part, land
+        self.send_sem, self.recv_sem = send_sem, recv_sem
+
+    def copy(self, z, direction):
+        place = self.place
+        slot = z if direction > 0 else jnp.where(z == place.z - 1, place.depth, z)
+        return remote(
+            self.part(z),
+            self.land(slot),
+            self.send_sem.at[z],
+            self.recv_sem.at[slot],
+            context=place.z + direction,
+        )
+
+    def upstream(self, direction):
+        return self.place.z > 0 if direction > 0 else self.place.z < self.place.depth - 1
+
+    def arrive(self, slot):
+        arrived(self.land(slot), self.recv_sem.at[slot])
+
+    def at(self, direction, step, body):
+        z = self.place.z + direction * step
+        pl.when(self.place.on_line(z))(lambda: body(z))
+
+    def pass_on(self, direction, step, add):
+        def body(z):
+            def more():
+                self.arrive(z)
+                add(self.part(z), self.land(z))
+
+            pl.when(self.upstream(direction))(more)
+            self.copy(z, direction).start()
+
+        self.at(direction, step, body)
+
+    def end(self, add):
+        for direction, slot in ((1, self.place.z), (-1, self.place.depth)):
+
+            def body(slot=slot):
+                self.arrive(slot)
+                add(self.part(self.place.z), self.land(slot))
+
+            pl.when(self.upstream(direction))(body)
+
+    def drain(self):
+        for step in range(1, self.place.depth):
+            for direction in (1, -1):
+                self.at(direction, step, lambda z, d=direction: self.copy(z, d).wait_send())
+
+
+class DenseScatter:
+    def __init__(self, place, source, low, high, line, cross, spare, out, sems):
+        self.place, self.source, self.spare, self.out = place, source, spare, out
+        self.low, self.high, self.cross = low, high, cross
         (
-            self.sl_send,
-            self.sl_recv,
-            self.sh_send,
-            self.sh_recv,
-            self.sz_send,
-            self.sz_recv,
-            self.sx_send,
-            self.sx_recv,
-            self.ez_send,
-            self.ez_recv,
-            self.ex_send,
-            self.ex_recv,
-            self.own_sem,
-            self.eown_sem,
-            self.out_sem,
-            self.eout_sem,
-            self.g_send,
-            self.g_recv,
+            self.l_send, self.l_recv, self.h_send, self.h_recv, z_send, z_recv,
+            self.x_send, self.x_recv, self.own_sem,
         ) = sems
-        self.local_count = self.ecross[0].shape[1]
-        self.pieces = [(a, e) for e in range(self.local_count) for a in range(3)]
-        self.width = self.ecross[0].shape[3]
+        self.step = min(64, low.shape[2]) if low.shape[2] % 64 == 0 else 16
+        self.line = LineSum(
+            place, lambda z: low.at[z, place.high], lambda slot: line.at[slot], z_send, z_recv
+        )
 
     @staticmethod
-    def scratch(sizes, rows, features, local_count, width):
-        depth, high_count = sizes
-        bf = jnp.bfloat16
-        buffers = [pltpu.VMEM((depth, high_count, r, features), bf) for r in rows]
-        buffers += [pltpu.VMEM((high_count - 1, depth, r, features), bf) for r in rows]
-        buffers += [pltpu.VMEM((depth + 1, r, features), bf) for r in rows]
-        buffers += [pltpu.VMEM((r, features), bf) for r in rows]
-        buffers += [pltpu.VMEM((depth, high_count, max(rows), features), bf)]
-        for lead in (depth, depth + 1, None):
-            for a in range(3):
-                shape = (local_count,) + ((features, width) if a < 2 else (width, features))
-                buffers.append(pltpu.VMEM(shape if lead is None else (lead,) + shape, bf))
-        gain = (8, features)
-        buffers += [
-            pltpu.VMEM(gain, jnp.float32),
-            pltpu.VMEM(gain, jnp.float32),
-            pltpu.VMEM((high_count - 1,) + gain, jnp.float32),
-            pltpu.VMEM((depth - 1,) + gain, jnp.float32),
-            pltpu.VMEM(gain, jnp.float32),
+    def semaphores(count, depth, high_count):
+        dma = pltpu.SemaphoreType.DMA
+        cross = dma((count, depth, high_count))
+        return [
+            cross, cross, dma((count, high_count)), dma((count, high_count)),
+            dma((count, depth + 1)), dma((count, depth + 1)),
+            dma((count,)), dma((count,)), dma((count, 2)),
         ]
+
+    def _index(self, z, high, low):
+        return (z * self.place.high_count + high) * 2 + low
+
+    def _to_low(self, z, high):
+        place = self.place
+        return remote(
+            self.source(self._index(z, high, 1 - place.low)),
+            self.low.at[z, high],
+            self.l_send.at[z, high],
+            self.l_recv.at[z, high],
+            experts=place.e + 1 - 2 * place.low,
+        )
+
+    def _each(self, body):
+        for z in range(self.place.depth):
+            for high in range(self.place.high_count):
+                body(z, high)
+
+    def start(self):
+        self._each(lambda z, high: self._to_low(z, high).start())
+
+    def add_low(self):
+        place = self.place
+        places = [(z, high) for z in range(place.depth) for high in range(place.high_count)]
+
+        def load(i):
+            z, high = places[i]
+            return pltpu.make_async_copy(
+                self.source(self._index(z, high, place.low)),
+                self.spare.at[i % 2],
+                self.own_sem.at[i % 2],
+            )
+
+        if self.spare is not None:
+            load(0).start()
+        for i, (z, high) in enumerate(places):
+            self._to_low(z, high).wait_recv()
+            if self.spare is None:
+                own = self.source(self._index(z, high, place.low))
+            else:
+                if i + 1 < len(places):
+                    load(i + 1).start()
+                load(i).wait()
+                own = self.spare.at[i % 2]
+            add_into(self.low.at[z, high], [own], self.step)
+        for step in range(1, place.high_count):
+            self._to_high(step).start()
+
+    def _to_high(self, step):
+        place = self.place
+        peer = place.peer_high(step)
+        return remote(
+            self.low.at[:, peer],
+            self.high.at[step - 1],
+            self.h_send.at[step],
+            self.h_recv.at[step],
+            experts=peer * 2 + place.low,
+        )
+
+    def add_high(self):
+        place = self.place
+        for step in range(1, place.high_count):
+            self._to_high(step).wait_recv()
+        for z in range(place.depth):
+            add_into(
+                self.low.at[z, place.high],
+                [self.high.at[step - 1, z] for step in range(1, place.high_count)],
+                self.step,
+            )
+
+    def _add(self, target, more):
+        add_into(target, [more], self.step)
+
+    def pass_on(self, direction, step):
+        self.line.pass_on(direction, step, self._add)
+
+    def _across(self):
+        place = self.place
+        return remote(
+            self.low.at[place.z, place.high], self.cross, self.x_send, self.x_recv, dp=1 - place.x
+        )
+
+    def end(self):
+        self.line.end(self._add)
+        self._across().start()
+
+    def _store(self):
+        return pltpu.make_async_copy(self.cross, self.out, self.own_sem.at[0])
+
+    def finish(self):
+        self._across().wait_recv()
+        self._add(self.cross, self.low.at[self.place.z, self.place.high])
+        self._store().start()
+
+    def drain(self):
+        self._each(lambda z, high: self._to_low(z, high).wait_send())
+        for step in range(1, self.place.high_count):
+            self._to_high(step).wait_send()
+        self.line.drain()
+        self._across().wait_send()
+        self._store().wait()
+
+
+class ExpertScatter:
+    def __init__(self, place, sums, cross, land, own, more, outs, sems):
+        self.place, self.sums, self.cross, self.land = place, sums, cross, land
+        self.own, self.more, self.outs = own, more, outs
+        self.x_send, self.x_recv, self.z_send, self.z_recv, self.load_sem, self.out_sem = sems
+        self.local_count, self.width = cross[0].shape[1], cross[0].shape[3]
+
+    @staticmethod
+    def semaphores(depth, local_count):
         dma = pltpu.SemaphoreType.DMA
-        count, pieces = len(rows), 3 * local_count
-        sems = [
-            dma((count,)),
-            dma((count,)),
-            dma((count, high_count)),
-            dma((count, high_count)),
-            dma((count, depth)),
-            dma((count, depth + 1)),
-            dma((count,)),
-            dma((count,)),
-            dma((pieces, depth)),
-            dma((pieces, depth + 1)),
-            dma((pieces, depth)),
-            dma((pieces, depth)),
-            dma((1,)),
-            dma((pieces,)),
-            dma((count,)),
-            dma((pieces,)),
-            dma((3 + depth + high_count,)),
-            dma((3 + depth + high_count,)),
+        return [
+            dma((local_count, 3, depth)),
+            dma((local_count, 3, depth)),
+            dma((local_count, 3, depth + 1)),
+            dma((local_count, 3, depth + 1)),
+            dma((3, 3)),
+            dma((local_count, 3)),
         ]
-        return buffers, sems
-
-    def _x_copy(self, p, z):
-        a, local = self.pieces[p]
+
+    def _line(self, local, kind):
+        return LineSum(
+            self.place,
+            lambda z: self.cross[kind].at[z, local],
+            lambda slot: self.land[kind].at[slot, local],
+            self.z_send.at[local, kind],
+            self.z_recv.at[local, kind],
+        )
+
+    def _across(self, local, kind, z):
         return remote(
-            expert_slab(self.expert[a], a, local, self.place.other_shard(z), self.width),
-            self.ecross[a].at[z, local],
-            self.ex_send.at[p, z],
-            self.ex_recv.at[p, z],
+            expert_slab(self.sums[kind], kind, local, self.place.other_shard(z), self.width),
+            self.cross[kind].at[z, local],
+            self.x_send.at[local, kind, z],
+            self.x_recv.at[local, kind, z],
             dp=1 - self.place.x,
         )
 
-    def _order(self, do):
+    def _order(self, body):
         place = self.place
         for step in range(place.depth - 1, 0, -1):
             for direction in (1, -1):
                 z = place.z + direction * step
-                pl.when((z >= 0) & (z < place.depth))(
-                    lambda z=z, d=direction, s=step: do(z, d, s)
+                pl.when(place.on_line(z))(lambda z=z: body(z))
+        body(place.z)
+
+    def start(self):
+        def body(z):
+            for local in range(self.local_count):
+                for kind in range(3):
+                    self._across(local, kind, z).start()
+
+        self._order(body)
+
+    def _own_load(self, local, kind, z):
+        return pltpu.make_async_copy(
+            expert_slab(self.sums[kind], kind, local, self.place.shard(z), self.width),
+            self.own[kind],
+            self.load_sem.at[0, kind],
+        )
+
+    def _more_load(self, local, kind, slot, which):
+        return pltpu.make_async_copy(
+            self.land[kind].at[slot, local], self.more[kind].at[which], self.load_sem.at[1 + which, kind]
+        )
+
+    def pass_on(self, direction, step, local):
+        def body(z):
+            line = self._line(local, 0)
+            for kind in range(3):
+                self._own_load(local, kind, z).start()
+            for kind in range(3):
+                line = self._line(local, kind)
+                target = self.cross[kind].at[z, local]
+
+                def come(line=line, kind=kind):
+                    line.arrive(z)
+                    self._more_load(local, kind, z, 0).start()
+
+                pl.when(line.upstream(direction))(come)
+                self._across(local, kind, z).wait_recv()
+                self._own_load(local, kind, z).wait()
+
+                def both(target=target, kind=kind):
+                    self._more_load(local, kind, z, 0).wait()
+                    add_into(target, [self.own[kind], self.more[kind].at[0]], 64)
+
+                def single(target=target, kind=kind):
+                    add_into(target, [self.own[kind]], 64)
+
+                pl.when(line.upstream(direction))(both)
+                pl.when(jnp.logical_not(line.upstream(direction)))(single)
+                line.copy(z, direction).start()
+
+        self._line(local, 0).at(direction, step, body)
+
+    def end(self, local):
+        place = self.place
+        z = place.z
+        for kind in range(3):
+            self._own_load(local, kind, z).start()
+        for kind in range(3):
+            line = self._line(local, kind)
+            target = self.cross[kind].at[z, local]
+            for which, (direction, slot) in enumerate(((1, z), (-1, place.depth))):
+
+                def come(slot=slot, which=which, line=line, kind=kind):
+                    line.arrive(slot)
+                    self._more_load(local, kind, slot, which).start()
+
+                pl.when(line.upstream(direction))(come)
+            self._across(local, kind, z).wait_recv()
+            self._own_load(local, kind, z).wait()
+            add_into(target, [self.own[kind]], 64)
+            for which, (direction, slot) in enumerate(((1, z), (-1, place.depth))):
+
+                def more(slot=slot, which=which, kind=kind, target=target):
+                    self._more_load(local, kind, slot, which).wait()
+                    add_into(target, [self.more[kind].at[which]], 64)
+
+                pl.when(line.upstream(direction))(more)
+            self._store(local, kind).start()
+
+    def _store(self, local, kind):
+        return pltpu.make_async_copy(
+            self.cross[kind].at[self.place.z, local],
+            self.outs[kind].at[local],
+            self.out_sem.at[local, kind],
+        )
+
+    def drain(self):
+        for local in range(self.local_count):
+            for kind in range(3):
+                for z in range(self.place.depth):
+                    self._across(local, kind, z).wait_send()
+                self._line(local, kind).drain()
+                self._store(local, kind).wait()
+
+
+def backward_kernel(sizes, *refs):
+    place = Place(sizes)
+    depth, high_count = sizes
+    owners = place.owners
+    (
+        tokens, cot, gates, routes, gate_rows, cosine, sine_part,
+        qkv_w, out_w, gain_v, n1_i, k_i, v_i, q_i, att_i, hid_i, lse_i, side_i, dn2_i,
+        gsg, gsu, gsd, geg, geu, ged, outs_i, dins_i,
+        mixed_o, input_o, gqkv_o, gout_o, gsg_o, gsu_o, gsd_o, geg_o, geu_o, ged_o, gain_o,
+        eland_g, eland_u, eland_d, ret_in, ret_out, d_hidden_o, dn1_o,
+        *rest,
+    ) = refs
+    count = 5
+    low, rest = rest[:count], rest[count:]
+    high, rest = rest[:count], rest[count:]
+    line, rest = rest[:count], rest[count:]
+    cross, rest = rest[:count], rest[count:]
+    (
+        spare_w, spare_t, ecross_g, ecross_u, ecross_d, eown_g, eown_u, eown_d,
+        emore_g, emore_u, emore_d,
+        d_att, dpq, dpk, dpv, g_qkv, g_out, part, part_land,
+        gain_own, gain_low, gain_high, gain_line, gain_cross, out_rows,
+        *sems,
+    ) = rest
+    dense_sems, sems = sems[:9], sems[9:]
+    expert_sems, sems = sems[:6], sems[6:]
+    (
+        part_send, part_recv, ri_send, ri_recv, ro_send, ro_recv,
+        gain_send, gain_recv, load_sem, wq_sem, out_sem,
+    ) = sems
+    micro_count, rows, features = tokens.shape
+    prompt = depth * PB
+    length = prompt + CONT
+    local_count, slots = outs_i.shape[0], outs_i.shape[1]
+    total = owners * local_count
+    capacity = rows * 8 // (3 * total)
+    me = place.e
+
+    def rows_of(ref, size):
+        return lambda s: ref.at[pl.ds(pl.multiple_of(s * size, 16), size)]
+
+    def columns_of(ref, size):
+        return lambda s: ref.at[:, pl.ds(pl.multiple_of(s * size, 128), size)]
+
+    sources = [
+        columns_of(gsg, gsg_o.shape[1]),
+        columns_of(gsu, gsu_o.shape[1]),
+        rows_of(gsd, gsd_o.shape[0]),
+        rows_of(g_qkv, gqkv_o.shape[0]),
+        rows_of(g_out, gout_o.shape[0]),
+    ]
+    spares = [spare_w, spare_w, spare_t, None, None]
+    dense = [
+        DenseScatter(
+            place, sources[i], low[i], high[i], line[i], cross[i], spares[i], out,
+            [s.at[i] for s in dense_sems],
+        )
+        for i, out in enumerate((gsg_o, gsu_o, gsd_o, gqkv_o, gout_o))
+    ]
+    early, late = dense[:3], dense[3:]
+    experts = ExpertScatter(
+        place,
+        (geg, geu, ged),
+        (ecross_g, ecross_u, ecross_d),
+        (eland_g, eland_u, eland_d),
+        (eown_g, eown_u, eown_d),
+        (emore_g, emore_u, emore_d),
+        (geg_o, geu_o, ged_o),
+        expert_sems,
+    )
+    prompts = [
+        LineSum(
+            place,
+            lambda z, m=m: part.at[m, z],
+            lambda slot, m=m: part_land.at[m, slot],
+            part_send.at[m],
+            part_recv.at[m],
+        )
+        for m in range(micro_count)
+    ]
+
+    def slot_rows(m, owner_of_rows):
+        return pl.ds(pl.multiple_of((m * owners + owner_of_rows) * capacity, 16), capacity)
+
+    def hand_back(source, land, send_sem, recv_sem, m, step):
+        peer = place.peer_owner(step)
+        return remote(
+            source.at[:, slot_rows(m, peer)],
+            land.at[m, owners - step],
+            send_sem.at[step, m],
+            recv_sem.at[owners - step, m],
+            experts=peer,
+        )
+
+    returns = [(dins_i, ret_in, ri_send, ri_recv), (outs_i, ret_out, ro_send, ro_recv)]
+    place.greet()
+    for m in range(micro_count):
+        for step in range(1, owners):
+            hand_back(*returns[0], m, step).start()
+    for d in early:
+        d.start()
+    experts.start()
+    for m in range(micro_count):
+        for step in range(1, owners):
+            hand_back(*returns[1], m, step).start()
+
+    def fetch(pairs):
+        copies = [
+            pltpu.make_async_copy(source, target, load_sem.at[i])
+            for i, (source, target) in enumerate(pairs)
+        ]
+        for copy in copies:
+            copy.start()
+        for copy in copies:
+            copy.wait()
+
+    def fetch_returned(source, land, recv_sem, target, m):
+        for step in range(1, owners):
+            arrived(land.at[m, step], recv_sem.at[step, m])
+        pairs = []
+        for step in range(owners):
+            for local in range(local_count):
+                at = pl.ds((step * local_count + local) * capacity, capacity)
+                if step == 0:
+                    piece = source.at[local, slot_rows(m, me)]
+                else:
+                    piece = land.at[m, step, local]
+                pairs.append((piece, target.at[at]))
+        fetch(pairs)
+
+    for d in early:
+        d.add_low()
+    gain_own[...] = jnp.zeros_like(gain_own)
+
+    def after_experts(hidden, extra, back, first, second, g_rows, att, d_attn, wo):
+        fetch([(out_w, wo)] + [(att_i.at[m], att.at[pl.ds(m * rows, rows)]) for m in range(micro_count)])
+        for m in range(micro_count):
+            fetch([(hid_i.at[m], hidden), (cot.at[m], g_rows), (dn2_i.at[pl.ds(m * rows, rows)], extra)])
+            for i, hit, _ in one_hots(routes.at[m], gates.at[m], me, local_count, total):
+                here = pl.ds(i * capacity, capacity)
+                expert = lax.rem(me * local_count + i, total)
+                hit_first = either(hit, routes[m, 0:1, :] == expert)
+                hit_second = either(hit, routes[m, 1:2, :] == expert)
+                first[here, :] = hit_first.astype(F32).astype(BF)
+                second[here, :] = hit_second.astype(F32).astype(BF)
+            fetch_returned(dins_i, ret_in, ri_recv, back, m)
+            gain = gain_v[1:2, :]
+            for i in range(rows // PB):
+                here = pl.ds(i * PB, PB)
+                both = first[:, here] + second[:, here]
+                d_normed = extra[here, :] + tdot(both, back[...])
+                values = hidden[here, :]
+                root = lax.rsqrt(jnp.mean(values * values, -1, keepdims=True) + EPSILON)
+                scaled = gain * d_normed
+                d_values = (
+                    g_rows[here, :].astype(F32)
+                    + root * scaled
+                    - values * (root * root * root) * jnp.mean(values * scaled, -1, keepdims=True)
                 )
-        do(place.z, 0, 0)
-
-    def expert_start(self):
-        def start(z, direction, step):
-            for p in range(len(self.pieces)):
-                self._x_copy(p, z).start()
-
-        self._order(start)
-
-    def _own_load(self, p, z):
-        a, local = self.pieces[p]
-        return pltpu.make_async_copy(
-            expert_slab(self.expert[a], a, local, self.place.shard(z), self.width),
-            self.eown[a].at[local],
-            self.eown_sem.at[p],
-        )
-
-    def _line_copy(self, p, z, direction):
-        a, local = self.pieces[p]
-        place = self.place
-        if direction > 0:
-            slot = z
-        else:
-            slot = jnp.where(z == place.z - 1, place.depth, z)
-        return remote(
-            self.ecross[a].at[z, local],
-            self.eline[a].at[slot, local],
-            self.ez_send.at[p, z],
-            self.ez_recv.at[p, slot],
-            context=place.z + direction,
-        )
-
-    def _line_wait(self, p, slot):
-        a, local = self.pieces[p]
-        here = self.eline[a].at[slot, local]
-        remote(here, here, self.ez_send.at[p, 0], self.ez_recv.at[p, slot], context=0).wait_recv()
-
-    def expert_loads(self, z):
-        for p in range(len(self.pieces)):
-            self._own_load(p, z).start()
-
-    def expert_piece(self, p, z, direction):
-        a, local = self.pieces[p]
-        place = self.place
-        rows = 64
-        self._x_copy(p, z).wait_recv()
-        self._own_load(p, z).wait()
-        target, own = self.ecross[a].at[z, local], self.eown[a].at[local]
-        if direction:
-            upstream = place.z > 0 if direction > 0 else place.z < place.depth - 1
-
-            def with_line():
-                self._line_wait(p, z)
-                add_into(target, [own, self.eline[a].at[z, local]], rows)
-
-            pl.when(upstream)(with_line)
-            pl.when(jnp.logical_not(upstream))(lambda: add_into(target, [own], rows))
-            self._line_copy(p, z, direction).start()
-        else:
-            left, right = place.z > 0, place.z < place.depth - 1
-
-            def both():
-                self._line_wait(p, z)
-                self._line_wait(p, place.depth)
-                add_into(
-                    target, [own, self.eline[a].at[z, local], self.eline[a].at[place.depth, local]], rows
+                gain_own[1:2, :] += jnp.sum(d_normed * values * root, 0, keepdims=True)
+                there = pl.ds(m * rows + i * PB, PB)
+                extra[here, :] = d_values
+                low_part = d_values.astype(BF)
+                d_attn[there, :] = low_part
+                d_att[there, :] = ndot(low_part, wo[...]).astype(BF)
+            fetch([(extra, d_hidden_o.at[m])])
+            fetch([(side_i.at[pl.ds(m * rows, rows)], extra)])
+            fetch_returned(outs_i, ret_out, ro_recv, back, m)
+            for i in range(rows // PB):
+                here = pl.ds(i * PB, PB)
+                routed = gate_rows[m, here, 0:1] * tdot(first[:, here], back[...])
+                routed += gate_rows[m, here, 1:2] * tdot(second[:, here], back[...])
+                out_rows[here, :] = (hidden[here, :] + extra[here, :] + routed).astype(BF)
+            fetch([(out_rows, mixed_o.at[m])])
+            if m < local_count:
+                experts.pass_on(1, depth - 1, m)
+                experts.pass_on(-1, depth - 1, m)
+
+        def out_grad(here):
+            g_out[here, :] = tdot(att[:, here], d_attn[...]).astype(BF)
+
+        tiles(features, 256, out_grad)
+
+    pl.run_scoped(
+        after_experts,
+        pltpu.VMEM((rows, features), F32),
+        pltpu.VMEM((rows, features), F32),
+        pltpu.VMEM((total * capacity, features), BF),
+        pltpu.VMEM((total * capacity, rows), BF),
+        pltpu.VMEM((total * capacity, rows), BF),
+        pltpu.VMEM((rows, features), BF),
+        pltpu.VMEM((micro_count * rows, features), BF),
+        pltpu.VMEM((micro_count * rows, features), BF),
+        pltpu.VMEM((features, features), BF),
+    )
+    for local in range(micro_count, local_count):
+        experts.pass_on(1, depth - 1, local)
+        experts.pass_on(-1, depth - 1, local)
+    for d in early:
+        d.add_high()
+    for step in range(depth - 1, 0, -1):
+        for direction in (1, -1):
+            for d in early:
+                if step == depth - 1:
+                    d.pass_on(direction, step)
+
+    def own_rows(i):
+        start = place.z * PB if i == 0 else prompt + (i - 1) * PB
+        return start, pl.ds(start if i else pl.multiple_of(start, PB), PB)
+
+    def attention(k, v, q, lse, ds_s, p_s, wq, dn1):
+        load_wq = pltpu.make_async_copy(qkv_w, wq, wq_sem.at[0])
+        load_wq.start()
+        lane = lax.broadcasted_iota(jnp.int32, (PB, 2 * HD), 1)
+        wide_lane = lax.broadcasted_iota(jnp.int32, (rows, 2 * HD), 1)
+        column = lax.broadcasted_iota(jnp.int32, (PB, length), 1)
+        row = lax.broadcasted_iota(jnp.int32, (PB, length), 0)
+        for m in range(micro_count):
+            fetch([(k_i.at[m], k), (v_i.at[m], v), (q_i.at[m], q), (lse_i.at[m], lse)])
+            whole = pl.ds(m * rows, rows)
+
+            def pair(index, carry):
+                lanes = pl.ds(pl.multiple_of(index * 2 * HD, 2 * HD), 2 * HD)
+                keys, values = k[:, lanes], v[:, lanes]
+                for i in range(rows // PB):
+                    here = pl.ds(i * PB, PB)
+                    there = pl.ds(m * rows + i * PB, PB)
+                    query, d_out, logs = q[here, lanes], d_att[there, lanes], lse[here, :]
+                    start, table = own_rows(i)
+                    allowed = column <= row + start
+                    parts = []
+                    for sub in range(2):
+                        mine = lane // HD == sub
+                        scores = ndot(jnp.where(mine, query, jnp.zeros_like(query)), keys)
+                        log = jnp.sum(
+                            jnp.where(lane == 2 * index + sub, logs, 0.0), -1, keepdims=True
+                        )
+                        probs = jnp.where(allowed, jnp.exp(scores - log), 0.0)
+                        d_probs = ndot(jnp.where(mine, d_out, jnp.zeros_like(d_out)), values)
+                        centre = jnp.sum(probs * d_probs, -1, keepdims=True)
+                        d_scores = (probs * (d_probs - centre)).astype(BF)
+                        ds_s[sub, here, :] = d_scores
+                        p_s[sub, here, :] = probs.astype(BF)
+                        parts.append(mdot(d_scores, keys))
+                    d_query = jnp.where(lane < HD, parts[0], parts[1]) * HD**-0.5
+                    d_query = rope(d_query, cosine[table, :], -sine_part[table, :])
+                    dpq[there, lanes] = d_query.astype(BF)
+                d_key = jnp.zeros((length, 2 * HD), F32)
+                d_value = jnp.zeros((length, 2 * HD), F32)
+                query, d_out = q[:, lanes], d_att[whole, lanes]
+                for sub in range(2):
+                    mine = wide_lane // HD == sub
+                    d_key += tdot(ds_s[sub], jnp.where(mine, query, jnp.zeros_like(query)))
+                    d_value += tdot(p_s[sub], jnp.where(mine, d_out, jnp.zeros_like(d_out)))
+                keys_here = pl.ds(m * length, length)
+                d_key = rope(d_key, cosine[...], -sine_part[...])
+                dpk[keys_here, lanes] = d_key.astype(BF)
+                dpv[keys_here, lanes] = d_value.astype(BF)
+                return carry
+
+            lax.fori_loop(0, features // (2 * HD), pair, 0)
+            if m == 0:
+                load_wq.wait()
+            key_w, value_w = wq[pl.ds(features, features), :], wq[pl.ds(2 * features, features), :]
+            for z in range(depth):
+                here = pl.ds(m * length + z * PB, PB)
+                part[m, z] = (mdot(dpk[here, :], key_w) + mdot(dpv[here, :], value_w)).astype(BF)
+            for step in range(depth - 1, 0, -1):
+                if step == depth - 1:
+                    for direction in (1, -1):
+                        prompts[m].pass_on(direction, step, lambda t, s: add_into(t, [s], 64))
+            for i in range(rows // PB):
+                _, table = own_rows(i)
+                start = own_rows(i)[0] + m * length
+                here = pl.ds(pl.multiple_of(start, PB), PB)
+                there = pl.ds(m * rows + i * PB, PB)
+                dn1[pl.ds(i * PB, PB), :] = (
+                    mdot(dpq[there, :], wq[pl.ds(0, features), :])
+                    + mdot(dpk[here, :], key_w)
+                    + mdot(dpv[here, :], value_w)
                 )
-
-            def one(slot):
-                self._line_wait(p, slot)
-                add_into(target, [own, self.eline[a].at[slot, local]], rows)
-
-            pl.when(left & right)(both)
-            pl.when(left & jnp.logical_not(right))(lambda: one(z))
-            pl.when(jnp.logical_not(left) & right)(lambda: one(place.depth))
-            pltpu.make_async_copy(
-                target, self.expert_outs[a].at[local], self.eout_sem.at[p]
-            ).start()
-
-    def expert_all(self):
-        def run(z, direction, step):
-            self.expert_loads(z)
-            for p in range(len(self.pieces)):
-                self.expert_piece(p, z, direction)
-
-        self._order(run)
-
-    def expert_drain(self):
-        def drain(z, direction, step):
-            for p, (a, local) in enumerate(self.pieces):
-                self._x_copy(p, z).wait_send()
-                if direction:
-                    self._line_copy(p, z, direction).wait_send()
-                else:
-                    pltpu.make_async_copy(
-                        self.ecross[a].at[z, local], self.expert_outs[a].at[local], self.eout_sem.at[p]
-                    ).wait()
-
-        self._order(drain)
-
-    def _low_copy(self, a):
-        place = self.place
-        return remote(
-            self.dense[a].at[:, :, 1 - place.low],
-            self.dlow[a],
-            self.sl_send.at[a],
-            self.sl_recv.at[a],
-            experts=place.e + 1 - 2 * place.low,
-        )
-
-    def dense_start(self, a):
-        self._low_copy(a).start()
-
-    def _high_copy(self, a, step):
-        place = self.place
-        peer = place.peer_high(step)
-        return remote(
-            self.dlow[a].at[:, peer],
-            self.dhigh[a].at[step - 1],
-            self.sh_send.at[a, step],
-            self.sh_recv.at[a, step],
-            experts=peer * 2 + place.low,
-        )
-
-    def dense_low(self, a):
-        place = self.place
-        rows = self.dlow[a].shape[2]
-        own = self.dense_own.at[:, :, pl.ds(0, rows)]
-        copy = pltpu.make_async_copy(self.dense[a].at[:, :, place.low], own, self.own_sem.at[0])
-        copy.start()
-        self._low_copy(a).wait_recv()
-        copy.wait()
-        for z in range(place.depth):
-            for high in range(place.high_count):
-                add_into(self.dlow[a].at[z, high], [self.dense_own.at[z, high, pl.ds(0, rows)]], 16)
-        for step in range(1, place.high_count):
-            self._high_copy(a, step).start()
-
-    def dense_high(self, a):
-        place = self.place
-        for step in range(1, place.high_count):
-            self._high_copy(a, step).wait_recv()
-        for z in range(place.depth):
-            add_into(
-                self.dlow[a].at[z, place.high],
-                [self.dhigh[a].at[step - 1, z] for step in range(1, place.high_count)],
-                16,
-            )
-
-    def _dline_copy(self, a, z, direction):
-        place = self.place
-        if direction > 0:
-            slot = z
-        else:
-            slot = jnp.where(z == place.z - 1, place.depth, z)
-        return remote(
-            self.dlow[a].at[z, place.high],
-            self.dline[a].at[slot],
-            self.sz_send.at[a, z],
-            self.sz_recv.at[a, slot],
-            context=place.z + direction,
-        )
-
-    def _dline_wait(self, a, slot):
-        here = self.dline[a].at[slot]
-        remote(here, here, self.sz_send.at[a, 0], self.sz_recv.at[a, slot], context=0).wait_recv()
-
-    def _dcross_copy(self, a):
-        place = self.place
-        return remote(
-            self.dlow[a].at[place.z, place.high],
-            self.dcross[a],
-            self.sx_send.at[a],
-            self.sx_recv.at[a],
-            dp=1 - place.x,
-        )
-
-    def dense_line(self, which):
-        place = self.place
-
-        def run(z, direction, step):
-            for a in which:
-                target = self.dlow[a].at[z, place.high]
-                if direction:
-                    upstream = place.z > 0 if direction > 0 else place.z < place.depth - 1
-
-                    def with_line(a=a, target=target):
-                        self._dline_wait(a, z)
-                        add_into(target, [self.dline[a].at[z]], 16)
-
-                    pl.when(upstream)(with_line)
-                    self._dline_copy(a, z, direction).start()
-                else:
-
-                    def one(slot, a=a, target=target):
-                        self._dline_wait(a, slot)
-                        add_into(target, [self.dline[a].at[slot]], 16)
-
-                    pl.when(place.z > 0)(lambda one=one: one(place.z))
-                    pl.when(place.z < place.depth - 1)(lambda one=one: one(place.depth))
-                    self._dcross_copy(a).start()
-
-        self._order(run)
-
-    def dense_finish(self, a):
-        place = self.place
-        cross = self._dcross_copy(a)
-        cross.wait_recv()
-        add_into(self.dcross[a], [self.dlow[a].at[place.z, place.high]], 16)
-        pltpu.make_async_copy(self.dcross[a], self.dense_outs[a], self.out_sem.at[a]).start()
-
-    def dense_drain(self, a):
-        place = self.place
-        self._low_copy(a).wait_send()
-        for step in range(1, place.high_count):
-            self._high_copy(a, step).wait_send()
-
-        def drain(z, direction, step):
-            if direction:
-                self._dline_copy(a, z, direction).wait_send()
-
-        self._order(drain)
-        self._dcross_copy(a).wait_send()
-        pltpu.make_async_copy(self.dcross[a], self.dense_outs[a], self.out_sem.at[a]).wait()
-
-    def gains_all(self):
-        place = self.place
-        depth, high_count = place.depth, place.high_count
-
-        def stage(first, targets, slots):
-            copies = [
-                remote(self.gmine, slot, self.g_send.at[first + i], self.g_recv.at[first + i], **target)
-                for i, (target, slot) in enumerate(zip(targets, slots))
-            ]
-            for copy in copies:
-                copy.start()
-            for copy in copies:
-                copy.wait()
-            self.gmine[...] = sum((slot[...] for slot in slots), self.gmine[...])
-
-        stage(0, [dict(experts=place.e + 1 - 2 * place.low)], [self.glow])
-        stage(
-            1,
-            [dict(experts=place.peer_high(s) * 2 + place.low) for s in range(1, high_count)],
-            [self.ghigh.at[s - 1] for s in range(1, high_count)],
-        )
-        stage(
-            high_count,
-            [dict(context=lax.rem(place.z + s, depth)) for s in range(1, depth)],
-            [self.gline.at[s - 1] for s in range(1, depth)],
-        )
-        stage(high_count + depth - 1, [dict(dp=1 - place.x)], [self.gcross])
-        self.gain_out[...] = self.gmine[...]
-
-
-def scatter_kernel(sizes, count, *refs):
-    place = PlaceS(sizes)
-    dense, refs = refs[:count], refs[count:]
-    expert, refs = refs[:3], refs[3:]
-    gain, refs = refs[0], refs[1:]
-    dense_outs, refs = refs[:count], refs[count:]
-    expert_outs, refs = refs[:3], refs[3:]
-    gain_out, refs = refs[0], refs[1:]
-    buffers, sems = refs[: 4 * count + 15], refs[4 * count + 15 :]
-    work = ScatterAll(
-        place, dense, expert, dense_outs, expert_outs, gain, gain_out, buffers, sems
-    )
-    place.greet(everyone=True)
-    for a in range(count):
-        work.dense_start(a)
-    work.expert_start()
-    work.gmine[...] = gain[...]
-    for a in range(count):
-        work.dense_low(a)
-    for a in range(count):
-        work.dense_high(a)
-    work.dense_line(list(range(count)))
-    work.expert_all()
-    work.gains_all()
-    for a in range(count):
-        work.dense_finish(a)
-    for a in range(count):
-        work.dense_drain(a)
-    work.expert_drain()
-
-
-def scatter_gradients(sizes, dense, experts, gain):
+            fetch([(dn1, dn1_o.at[m])])
+            for local in range(local_count):
+                for direction in (1, -1):
+                    if depth > 2 and m == 0:
+                        experts.pass_on(direction, depth - 2, local)
+            for step in range(depth - 2, 0, -1):
+                for direction in (1, -1):
+                    prompts[m].pass_on(direction, step, lambda t, s: add_into(t, [s], 64))
+            if m == 0:
+                for step in range(depth - 2, 0, -1):
+                    for direction in (1, -1):
+                        for d in early:
+                            d.pass_on(direction, step)
+
+    pl.run_scoped(
+        attention,
+        pltpu.VMEM((length, features), BF),
+        pltpu.VMEM((length, features), BF),
+        pltpu.VMEM((rows, features), BF),
+        pltpu.VMEM((rows, 2 * HD), F32),
+        pltpu.VMEM((2, rows, length), BF),
+        pltpu.VMEM((2, rows, length), BF),
+        pltpu.VMEM(qkv_w.shape, BF),
+        pltpu.VMEM((rows, features), F32),
+    )
+
+    def weight_grads(n1, n1_own):
+        pairs = []
+        for m in range(micro_count):
+            pairs.append((n1_i.at[m], n1.at[pl.ds(m * length, length)]))
+            for i in range(rows // PB):
+                _, here = own_rows(i)
+                pairs.append((n1_i.at[m, here], n1_own.at[pl.ds(m * rows + i * PB, PB)]))
+        fetch(pairs)
+
+        def make(here):
+            g_qkv[here, :] = tdot(dpq[:, here], n1_own[...]).astype(BF)
+
+        def make_key(here):
+            there = pl.ds(pl.multiple_of(here.start + features, 256), 256)
+            g_qkv[there, :] = tdot(dpk[:, here], n1[...]).astype(BF)
+
+        def make_value(here):
+            there = pl.ds(pl.multiple_of(here.start + 2 * features, 256), 256)
+            g_qkv[there, :] = tdot(dpv[:, here], n1[...]).astype(BF)
+
+        tiles(features, 256, make)
+        tiles(features, 256, make_key)
+        tiles(features, 256, make_value)
+
+    pl.run_scoped(
+        weight_grads,
+        pltpu.VMEM((micro_count * length, features), BF),
+        pltpu.VMEM((micro_count * rows, features), BF),
+    )
+    for d in late:
+        d.start()
+    for local in range(local_count):
+        for step in range(depth - 3, 0, -1):
+            for direction in (1, -1):
+                experts.pass_on(direction, step, local)
+    for d in late:
+        d.add_low()
+    for d in early:
+        d.end()
+
+    def inputs(x_rows, d_hidden, dn1):
+        for m in range(micro_count):
+            fetch([(tokens.at[m], x_rows), (d_hidden_o.at[m], d_hidden), (dn1_o.at[m], dn1)])
+            for direction, slot in ((1, place.z), (-1, depth)):
+
+                def body(m=m, slot=slot):
+                    prompts[m].arrive(slot)
+                    dn1[pl.ds(0, PB), :] += part_land[m, slot].astype(F32)
+
+                pl.when(prompts[m].upstream(direction))(body)
+            gain = gain_v[0:1, :]
+            for i in range(rows // PB):
+                here = pl.ds(i * PB, PB)
+                values, d_normed = x_rows[here, :].astype(F32), dn1[here, :]
+                root = lax.rsqrt(jnp.mean(values * values, -1, keepdims=True) + EPSILON)
+                scaled = gain * d_normed
+                d_values = (
+                    d_hidden[here, :]
+                    + root * scaled
+                    - values * (root * root * root) * jnp.mean(values * scaled, -1, keepdims=True)
+                )
+                gain_own[0:1, :] += jnp.sum(d_normed * values * root, 0, keepdims=True)
+                out_rows[here, :] = d_values.astype(BF)
+            fetch([(out_rows, input_o.at[m])])
+
+    pl.run_scoped(
+        inputs,
+        pltpu.VMEM((rows, features), BF),
+        pltpu.VMEM((rows, features), F32),
+        pltpu.VMEM((rows, features), F32),
+    )
+    for d in late:
+        d.add_high()
+    for step in range(depth - 1, 0, -1):
+        for direction in (1, -1):
+            for d in late:
+                d.pass_on(direction, step)
+
+    def stage(first, targets, lands):
+        copies = [
+            remote(gain_own, land, gain_send.at[first + i], gain_recv.at[first + i], **target)
+            for i, (target, land) in enumerate(zip(targets, lands))
+        ]
+        for copy in copies:
+            copy.start()
+        for copy in copies:
+            copy.wait()
+        total_gain = gain_own[...]
+        for land in lands:
+            total_gain = total_gain + land[...]
+        gain_own[...] = total_gain
+
+    stage(0, [dict(experts=place.e + 1 - 2 * place.low)], [gain_low])
+    stage(
+        1,
+        [dict(experts=place.peer_high(s) * 2 + place.low) for s in range(1, high_count)],
+        [gain_high.at[s - 1] for s in range(1, high_count)],
+    )
+    stage(
+        high_count,
+        [dict(context=lax.rem(place.z + s, depth)) for s in range(1, depth)],
+        [gain_line.at[s - 1] for s in range(1, depth)],
+    )
+    stage(high_count + depth - 1, [dict(dp=1 - place.x)], [gain_cross])
+    for local in range(local_count):
+        experts.end(local)
+    for d in late:
+        d.end()
+    for d in dense:
+        d.finish()
+    fetch([(gain_own, gain_o)])
+    for d in dense:
+        d.drain()
+    experts.drain()
+    for p in prompts:
+        p.drain()
+    for m in range(micro_count):
+        for step in range(1, owners):
+            for entry in returns:
+                hand_back(*entry, m, step).wait_send()
+
+
+def run_backward(sizes, tokens, cot, gates, routes, gate_rows, forward):
     depth, high_count = sizes
-    hbm = pl.BlockSpec(memory_space=pltpu.HBM)
-    vmem = pl.BlockSpec(memory_space=pltpu.VMEM)
-    count = len(dense)
-    rows = [a.shape[3] for a in dense]
-    features = gain.shape[1]
-    local_count = experts[0].shape[0]
-    width = experts[2].shape[1] // (2 * depth)
-    shapes = [jax.ShapeDtypeStruct(a.shape[3:], a.dtype) for a in dense]
-    shapes += [
-        jax.ShapeDtypeStruct(
-            (local_count,) + ((features, width) if a < 2 else (width, features)), experts[a].dtype
-        )
-        for a in range(3)
+    micro_count, rows, features = tokens.shape
+    owners = high_count * 2
+    line = depth * owners
+    prompt = depth * PB
+    length = prompt + CONT
+    cosine, sine_part = rope_tables(prompt)
+    gsg, geg, outs = forward[12], forward[15], forward[18]
+    local_count, slots, _ = outs.shape
+    total = owners * local_count
+    capacity = rows * 8 // (3 * total)
+    part = gsg.shape[1] // line
+    width = geg.shape[2] // (2 * depth)
+    hbm, vmem = pl.BlockSpec(memory_space=pltpu.HBM), pl.BlockSpec(memory_space=pltpu.VMEM)
+    shapes = [(features, part), (features, part), (part, features)]
+    shapes += [(forward[0].shape[0] // line, features), (forward[1].shape[0] // line, features)]
+    expert_shapes = [(features, width), (features, width), (width, features)]
+    returned = (micro_count, owners, local_count, capacity, features)
+    out_dims = [(micro_count, rows, features)] * 2
+    out_dims += [shapes[3], shapes[4], shapes[0], shapes[1], shapes[2]]
+    out_dims += [(local_count,) + s for s in expert_shapes]
+    out_shape = [jax.ShapeDtypeStruct(dims, BF) for dims in out_dims]
+    out_shape += [jax.ShapeDtypeStruct((8, features), F32)]
+    out_shape += [jax.ShapeDtypeStruct((depth + 1, local_count) + s, BF) for s in expert_shapes]
+    out_shape += [jax.ShapeDtypeStruct(returned, BF)] * 2
+    out_shape += [jax.ShapeDtypeStruct((micro_count, rows, features), F32)] * 2
+    scratch = [pltpu.VMEM((depth, high_count) + s, BF) for s in shapes]
+    scratch += [pltpu.VMEM((high_count - 1, depth) + s, BF) for s in shapes]
+    scratch += [pltpu.VMEM((depth + 1,) + s, BF) for s in shapes]
+    scratch += [pltpu.VMEM(s, BF) for s in shapes]
+    scratch += [pltpu.VMEM((2,) + shapes[0], BF), pltpu.VMEM((2,) + shapes[2], BF)]
+    scratch += [pltpu.VMEM((depth, local_count) + s, BF) for s in expert_shapes]
+    scratch += [pltpu.VMEM(s, BF) for s in expert_shapes]
+    scratch += [pltpu.VMEM((2,) + s, BF) for s in expert_shapes]
+    token_rows, key_rows = micro_count * rows, micro_count * length
+    gain = (8, features)
+    scratch += [
+        pltpu.VMEM((token_rows, features), BF),
+        pltpu.VMEM((token_rows, features), BF),
+        pltpu.VMEM((key_rows, features), BF),
+        pltpu.VMEM((key_rows, features), BF),
+        pltpu.VMEM(forward[0].shape, BF),
+        pltpu.VMEM(forward[1].shape, BF),
+        pltpu.VMEM((micro_count, depth, PB, features), BF),
+        pltpu.VMEM((micro_count, depth + 1, PB, features), BF),
+        pltpu.VMEM(gain, F32),
+        pltpu.VMEM(gain, F32),
+        pltpu.VMEM((high_count - 1,) + gain, F32),
+        pltpu.VMEM((depth - 1,) + gain, F32),
+        pltpu.VMEM(gain, F32),
+        pltpu.VMEM((rows, features), BF),
     ]
-    shapes += [jax.ShapeDtypeStruct(gain.shape, gain.dtype)]
-    buffers, sems = ScatterAll.scratch(sizes, rows, features, local_count, width)
-    outs = pl.pallas_call(
-        functools.partial(scatter_kernel, sizes, count),
-        out_shape=shapes,
-        in_specs=[hbm] * (count + 3) + [vmem],
-        out_specs=[hbm] * (count + 3) + [vmem],
-        scratch_shapes=buffers + sems,
+    dma = pltpu.SemaphoreType.DMA
+    scratch += DenseScatter.semaphores(len(shapes), depth, high_count)
+    scratch += ExpertScatter.semaphores(depth, local_count)
+    stages = 1 + high_count + depth
+    scratch += [
+        dma((micro_count, depth + 1)),
+        dma((micro_count, depth + 1)),
+        dma((owners, micro_count)),
+        dma((owners, micro_count)),
+        dma((owners, micro_count)),
+        dma((owners, micro_count)),
+        dma((stages,)),
+        dma((stages,)),
+        dma((max(total, 2 + micro_count, 4 * micro_count + micro_count),)),
+        dma((1,)),
+        dma((1,)),
+    ]
+    return pl.pallas_call(
+        functools.partial(backward_kernel, sizes),
+        out_shape=out_shape,
+        in_specs=[hbm] * 2 + [vmem] * 5 + [hbm] * 2 + [vmem] + [hbm] * 17,
+        out_specs=[hbm] * len(out_shape),
+        scratch_shapes=scratch,
         compiler_params=pltpu.CompilerParams(
             collective_id=1, has_side_effects=True, vmem_limit_bytes=60 * MIB
         ),
-        name="scatter_gradients",
-    )(*dense, *experts, gain)
-    return outs[:count], outs[count : count + 3], outs[count + 3]
+        name="backward_and_sum",
+    )(tokens, cot, gates, routes, gate_rows, cosine, sine_part, *forward)
 
 
 def on_device_plain(
@@ -1804,188 +2158,43 @@
     expert_up,
     expert_down,
 ):
-    micro_count = tokens.shape[2]
-    row_count = tokens.shape[4]
-    feature_count = tokens.shape[5]
     owners = lax.axis_size(EXPERTS)
-    local_experts = expert_gate.shape[0]
-    total_experts = owners * local_experts
-    capacity = row_count * 8 // (3 * total_experts)
-    blocks = lax.axis_size(CONTEXT)
-    prompt = blocks * PB
-    scaling = HD ** (-0.5)
-    sizes = (blocks, owners // 2)
+    sizes = (lax.axis_size(CONTEXT), owners // 2)
     own_at = lax.axis_index(CONTEXT) * owners + lax.axis_index(EXPERTS)
-    gain_width = gains.shape[1]
+    gain_width, features = gains.shape[1], tokens.shape[5]
     gain_rows = lax.dynamic_update_slice(
-        jnp.zeros((16, feature_count), jnp.bfloat16), gains, (0, own_at * gain_width)
-    )
-    (
-        w_qkv, w_out, w_gains, _, _, _, _, _, _,
-        n1_all, k_all, v_all, q_all, att_all, hid_all, lse_all, side_all, dn2_all,
-        gsg, gsu, gsd, geg, geu, ged, outs, dins,
-    ) = run_forward(
+        jnp.zeros((16, features), jnp.bfloat16), gains, (0, own_at * gain_width)
+    )
+    rows, cot = tokens[0, 0, :, 0], cotangent[0, 0, :, 0]
+    gate_rows, route_rows = gates[0, 0, :, 0], routes[0, 0, :, 0]
+    gate_columns, route_columns = gate_rows.transpose(0, 2, 1), route_rows.transpose(0, 2, 1)
+    forward = run_forward(
         sizes,
-        tokens[0, 0, :, 0],
-        cotangent[0, 0, :, 0],
-        gates[0, 0, :, 0].transpose(0, 2, 1),
-        routes[0, 0, :, 0].transpose(0, 2, 1),
+        rows,
+        cot,
+        gate_columns,
+        route_columns,
         (qkv_weight.T, out_weight, gain_rows, shared_gate, shared_up, shared_down),
         (expert_gate, expert_up, expert_down),
     )
-    gain_one, gain_two = w_gains[0], w_gains[1]
-    here_index = lax.axis_index(CONTEXT)
-    row_ids = jnp.arange(row_count, dtype=jnp.int32)
-    query_pos = jnp.where(row_ids < PB, here_index * PB + row_ids, prompt + row_ids - PB)
-    key_pos = jnp.arange(prompt + CONT, dtype=jnp.int32)
-    allowed = key_pos[None, None, :] <= query_pos[None, :, None]
-    half_size = HD // 2
-    frequency = 10000.0 ** (-2.0 * jnp.arange(half_size, dtype=jnp.float32) / HD)
-    angles = query_pos.astype(jnp.float32)[:, None] * frequency
-    cosine = jnp.cos(angles)[:, None, :]
-    sine_part = jnp.sin(angles)[:, None, :]
-    acc_qkv = jnp.zeros(w_qkv.shape, jnp.float32)
-    acc_out = jnp.zeros(w_out.shape, jnp.float32)
-    acc_gain_one = jnp.zeros((feature_count,), jnp.float32)
-    acc_gain_two = jnp.zeros((feature_count,), jnp.float32)
-    mixed_list = []
-    input_list = []
-    for step_index in range(micro_count):
-        inputs = tokens[0, 0, step_index, 0].astype(jnp.float32)
-        root_one = lax.rsqrt(jnp.mean(inputs * inputs, -1, keepdims=True) + EPSILON)
-        hidden = hid_all[step_index]
-        root_two = lax.rsqrt(jnp.mean(hidden * hidden, -1, keepdims=True) + EPSILON)
-        grad_rows = cotangent[0, 0, step_index, 0].astype(jnp.float32)
-        rows_here = slice(step_index * row_count, (step_index + 1) * row_count)
-        side, d_normed_two = side_all[rows_here], dn2_all[rows_here]
-        route_rows = routes[0, 0, step_index, 0]
-        slots = slot_table(route_rows, total_experts)
-        flat_dest = (route_rows * capacity + slots).reshape(-1)
-        gate_rows = gates[0, 0, step_index, 0]
-
-        def come_back(item):
-            item = item.reshape(local_experts, micro_count, owners, capacity, feature_count)
-            item = item[:, step_index].transpose(1, 0, 2, 3)
-            item = item.reshape(total_experts, capacity, feature_count)
-            return lax.all_to_all(item, EXPERTS, split_axis=0, concat_axis=0, tiled=True).reshape(-1, feature_count)
-
-        returned, back = come_back(outs), come_back(dins)
-        picked = returned[flat_dest].reshape(row_count, 2, feature_count).astype(jnp.float32)
-        routed = jnp.sum(gate_rows[:, :, None] * picked, 1)
-        mixed_list.append((hidden + routed + side).astype(jnp.bfloat16))
-        d_normed_two = d_normed_two + jnp.sum(
-            back[flat_dest].reshape(row_count, 2, feature_count).astype(jnp.float32), 1
-        )
-        query, key_rows, value_rows = q_all[step_index], k_all[step_index], v_all[step_index]
-        attended = att_all[step_index]
-        log_total = lse_all[step_index][:, :H].T[:, :, None]
-        normed_one = jnp.concatenate(
-            [
-                lax.dynamic_slice(n1_all[step_index], (here_index * PB, 0), (PB, feature_count)),
-                n1_all[step_index][prompt:],
-            ],
-            0,
-        )
-        scaled_two = gain_two * d_normed_two
-        d_hidden = (
-            grad_rows
-            + root_two * scaled_two
-            - hidden * root_two**3 * jnp.mean(hidden * scaled_two, -1, keepdims=True)
-        )
-        acc_gain_two = acc_gain_two + jnp.sum(d_normed_two * hidden * root_two, 0)
-        d_attn = d_hidden.astype(jnp.bfloat16)
-        acc_out = acc_out + tdot(attended, d_attn)
-        d_attended = ndot(d_attn, w_out).astype(jnp.bfloat16)
-        key_heads = key_rows.reshape(prompt + CONT, H, HD)
-        value_heads = value_rows.reshape(prompt + CONT, H, HD)
-        query_heads = query.reshape(row_count, H, HD)
-        scores = (
-            jnp.einsum("qhd,khd->hqk", query_heads, key_heads, preferred_element_type=jnp.float32)
-        )
-        scores = jnp.where(allowed, scores, -1000000000.0)
-        probs = jnp.exp(scores - log_total)
-        d_heads = d_attended.reshape(row_count, H, HD)
-        d_probs = jnp.einsum(
-            "qhd,khd->hqk", d_heads, value_heads, preferred_element_type=jnp.float32
-        )
-        centre = jnp.sum(probs * d_probs, -1, keepdims=True)
-        d_scores = (probs * (d_probs - centre)).astype(jnp.bfloat16)
-        d_query = (
-            jnp.einsum(
-                "hqk,khd->qhd", d_scores, key_heads, preferred_element_type=jnp.float32
-            ).reshape(row_count, feature_count)
-            * scaling
-        )
-        d_keys = (
-            jnp.einsum(
-                "hqk,qhd->khd", d_scores, query_heads, preferred_element_type=jnp.float32
-            ).reshape(prompt + CONT, feature_count)
-        )
-        d_values = jnp.einsum(
-            "hqk,qhd->khd", probs.astype(jnp.bfloat16), d_heads, preferred_element_type=jnp.float32
-        ).reshape(prompt + CONT, feature_count)
-        own_dkey, own_dvalue = (
-            lax.psum_scatter(
-                d_keys[:prompt].astype(jnp.bfloat16), CONTEXT, scatter_dimension=0, tiled=True
-            ).astype(jnp.float32),
-            lax.psum_scatter(
-                d_values[:prompt].astype(jnp.bfloat16), CONTEXT, scatter_dimension=0, tiled=True
-            ).astype(jnp.float32),
-        )
-        d_key_rows = jnp.concatenate([own_dkey, d_keys[prompt:]], 0)
-        d_value_rows = jnp.concatenate([own_dvalue, d_values[prompt:]], 0)
-        d_projected = jnp.concatenate(
-            [
-                rotate(d_query, cosine, -sine_part).astype(jnp.bfloat16),
-                rotate(d_key_rows, cosine, -sine_part).astype(jnp.bfloat16),
-                d_value_rows.astype(jnp.bfloat16),
-            ],
-            1,
-        )
-        acc_qkv = acc_qkv + tdot(d_projected, normed_one)
-        d_normed_one = mdot(d_projected, w_qkv)
-        scaled_one = gain_one * d_normed_one
-        d_inputs = (
-            d_hidden
-            + root_one * scaled_one
-            - inputs * root_one**3 * jnp.mean(inputs * scaled_one, -1, keepdims=True)
-        )
-        acc_gain_one = acc_gain_one + jnp.sum(d_normed_one * inputs * root_one, 0)
-        input_list.append(d_inputs.astype(jnp.bfloat16))
-    acc_gains = jnp.concatenate(
-        [acc_gain_one[None], acc_gain_two[None], jnp.zeros((6, feature_count), jnp.float32)], 0
-    )
-    dense_sums, expert_sums, gain_sum = scatter_gradients(
-        sizes,
-        tuple(
-            item.astype(jnp.bfloat16).reshape(blocks, owners // 2, 2, -1, feature_count)
-            for item in (acc_qkv, acc_out, gsg.T, gsu.T, gsd)
-        ),
-        (geg, geu, ged),
-        acc_gains,
-    )
-    grad_qkv, grad_out, grad_sgate, grad_sup, grad_sdown = (
-        item.astype(jnp.float32) for item in dense_sums
-    )
-    grad_qkv, grad_sgate, grad_sup = grad_qkv.T, grad_sgate.T, grad_sup.T
-    grad_gains = lax.dynamic_slice(gain_sum, (0, own_at * gain_width), (2, gain_width))
-    sharded_expert_gate, sharded_expert_up, sharded_expert_down = (
-        item.astype(jnp.float32) for item in expert_sums
-    )
-    mixed = jnp.stack(mixed_list, 0).reshape(tokens.shape)
-    input_grad = jnp.stack(input_list, 0).reshape(tokens.shape)
+    (
+        mixed, input_grad, grad_qkv, grad_out, grad_sgate, grad_sup, grad_sdown,
+        grad_egate, grad_eup, grad_edown, gain_sum, *_,
+    ) = run_backward(
+        sizes, rows, cot, gate_columns, route_columns, gate_rows, forward[:3] + forward[9:]
+    )
     return (
-        mixed,
-        input_grad,
-        grad_qkv,
-        grad_out,
-        grad_sgate,
-        grad_sup,
-        grad_sdown,
-        grad_gains,
-        sharded_expert_gate,
-        sharded_expert_up,
-        sharded_expert_down,
+        mixed.reshape(tokens.shape),
+        input_grad.reshape(tokens.shape),
+        grad_qkv.T.astype(F32),
+        grad_out.astype(F32),
+        grad_sgate.astype(F32),
+        grad_sup.astype(F32),
+        grad_sdown.astype(F32),
+        lax.dynamic_slice(gain_sum, (0, own_at * gain_width), (2, gain_width)),
+        grad_egate.astype(F32),
+        grad_eup.astype(F32),
+        grad_edown.astype(F32),
     )
 
 
@@ -1996,6 +2205,7 @@
         mesh_shape[DP] == 2
         and mesh_shape[EXPERTS] % 2 == 0
         and all(count % 16 == 0 for count in rows)
+        and shared_gate.shape[1] % 128 == 0
         and arrays[10].shape[2] % 128 == 0
     )
 

time: 1040 us -> 763 us (0.73)
  local copies, waits for them, and re-layouts: 124 us -> 6.64 us
  matrix products: 84.1 us -> 0 us
  other arithmetic: 72.1 us -> 12.2 us
  Pallas kernels: 689 us -> 735 us
  waiting for transfers between devices: 31.6 us -> 0 us
  starting transfers between devices: 16.8 us -> 0 us
  between operations: 15.3 us -> 1.18 us
    dot_general x18 -> x0, matrix products: 84.1 us -> none  [the longest x2 18.5 us: on_device(): jnp.einsum('qhd,khd->hqk', query_heads, key_heads, preferred_element_type...]
    pallas_call x1, Pallas kernels: 315 us -> 361 us  [run_backward(): pl.pallas_call(functools.partial(backward_kernel, sizes), out_shape=out_s...]
    slice x27 -> x0, local copies, waits for them, and re-layouts: 38.6 us -> none  [the longest x3 7.99 us: on_device(): k_all[step_index]]
    unnamed x170 -> x17, local copies, waits for them, and re-layouts: 33.9 us -> 2.93 us
    reduce_sum x8 -> x0, other arithmetic: 22.5 us -> none  [the longest x2 8.94 us: on_device(): jnp.sum(back[flat_dest].reshape(row_count, 2, feature_count).astype(jnp.f...]
    convert_element_type x9 -> x8, other arithmetic: 30 us -> 12.2 us  [the longest x1 1.77 us: on_device(): grad_sup.astype(F32)]
    all_to_all x4 -> x0, waiting for transfers between devices: 16.9 us -> none  [come_back(): lax.all_to_all(item, EXPERTS, split_axis=0, concat_axis=0, tiled=True)]
    gather x4 -> x0, local copies, waits for them, and re-layouts: 16.6 us -> none  [the longest x2 10.3 us: on_device(): returned[flat_dest].reshape(row_count, 2, feature_count).astype(jnp.float32)]
  transfers between devices with their start and end apart: 8 -> 0, of which waited for: 3 -> 0; matrix products, arithmetic and copies ran while one was open for 17% -> 0% of each run, Pallas kernels for 0% -> 0%
where the time goes in v2:
time: 763 us; the launch traced here: 755 us
  Pallas kernels  735 us (96%)
  other arithmetic  12.2 us (2%)
    pallas_call x1, Pallas kernels, run_forward(): pl.pallas_call(functools.partial(forward_kernel, sizes), out_shape=out_sh...  375 us
    pallas_call x1, Pallas kernels, run_backward(): pl.pallas_call(functools.partial(backward_kernel, sizes), out_shape=out_s...  361 us

profile of v2, /device:TPU:0, one launch (start us, length us, event | category | flops | bytes accessed | tf_op | source)
XLA Modules:
  0.0 755.1 jit_solution(385185606113727639)
XLA Ops:
  0.7 1.5 dynamic_update_slice.3.refs_8_
  2.2 0.0 copy-start.6
  2.2 0.9 copy.28
  3.1 0.0 copy-start
  3.1 0.7 copy.30.refs_2_
  3.8 0.0 copy-done.6
  3.8 374.6 %gather_and_forward.1 = (bf16[2304,768]{1,0:T(8,128)(2,1)}, bf16[768,768]{1,0:T(8,128)(2,1)}, f32[8,768]{1,0:T(8,128)}, bf16[768,2048]{1,0:T(8,128)(2,1)}, bf16[...) custom-call(bf16[2,384,768]{2,1,0:T(8,128)(2,1)} %bitcast.17, ...), custom_call_target="tpu_custom_call" | custom-call | tf_op jit(solution)/shard_map/gather_and_forward/pallas_call | solution.py:935
  378.4 0.0 copy-done
  378.4 360.5 %backward_and_sum.1 = (bf16[2,384,768]{2,1,0:T(8,128)(2,1)}, bf16[2,384,768]{2,1,0:T(8,128)(2,1)}, bf16[144,768]{1,0:T(8,128)(2,1)}, bf16[48,768]{1,0:T(8,128)(2...) custom-call(bf16[2,384,768]{2,1,0:T(8,128)(2,1)} %bitcast.18, ...), custom_call_target="tpu_custom_call" | custom-call | tf_op jit(solution)/shard_map/backward_and_sum/pallas_call | solution.py:1773
  738.9 0.0 copy-start.5
  739.0 0.0 copy-start.4
  739.0 1.5 constant_dynamic-slice_fusion
  740.4 1.6 convert_element_type.29
  742.0 1.7 convert_element_type.30
  743.7 1.8 convert_element_type.31
  745.4 1.7 convert_element_type.32
  747.1 1.7 convert_bitcast_fusion
  748.9 0.0 copy-done.5
  748.9 1.3 convert_element_type.33
  750.1 1.3 convert_element_type.34
  751.4 1.3 convert_element_type.35
  752.7 0.0 copy-done.2
  752.7 1.0 copy.36
  753.7 1.0 copy.37
  (7 shorter events, 0.0 us)
Async XLA Ops:
  2.2 1.7 copy-start.6
  3.1 375.3 %copy-start = (f32[1,1,2,1,384,2]{5,4,2,3,1,0:T(8,128)}, f32[1,1,2,1,384,2]{5,4,2,3,1,0:T(8,128)S(1)}, u32[]{:S(2)}) copy-start(f32[1,1,2,1,384,2]{5,4,2,3,1,0:T(8,128)S(1)} %copy.28) | copy-start | bytes 18436
  738.9 9.9 %copy-start.5 = (bf16[2,768,256]{2,1,0:T(8,128)(2,1)S(1)}, bf16[2,768,256]{2,1,0:T(8,128)(2,1)}, u32[]{:S(2)}) copy-start(bf16[2,768,256]{2,1,0:T(8,128)(2,1)} %get-tuple-element.70) | copy-start | bytes 2359300
  739.0 11.2 %copy-start.4 = (bf16[2,768,256]{2,1,0:T(8,128)(2,1)S(1)}, bf16[2,768,256]{2,1,0:T(8,128)(2,1)}, u32[]{:S(2)}) copy-start(bf16[2,768,256]{2,1,0:T(8,128)(2,1)} %get-tuple-element.71) | copy-start | bytes 2359300
  743.7 7.7 %copy-start.3 = (bf16[2,256,768]{2,1,0:T(8,128)(2,1)S(1)}, bf16[2,256,768]{2,1,0:T(8,128)(2,1)}, u32[]{:S(2)}) copy-start(bf16[2,256,768]{2,1,0:T(8,128)(2,1)} %get-tuple-element.72) | copy-start | bytes 2359300
  748.9 3.8 copy-start.2
  750.1 3.5 copy-start.1

commit v3 on v2

--- a/solution.py
+++ b/solution.py
@@ -230,11 +230,10 @@
             arrived(self.slot(z, high, place.low), self.h_recv.at[high, z])
             self._to_low(z, high, False).start()
 
-    def finish(self):
+    def finish(self, z):
         place = self.place
-        for z in range(place.depth):
-            for high in range(place.high_count):
-                arrived(self.slot(z, high, 1 - place.low), self.l_recv.at[high, z])
+        for high in range(place.high_count):
+            arrived(self.slot(z, high, 1 - place.low), self.l_recv.at[high, z])
 
     def drain(self):
         place = self.place
@@ -452,13 +451,16 @@
     ]
     experts = ExpertGather(place, (eg_in, eu_in, ed_in), (eg_o, eu_o, ed_o), expert_sems)
     own_prompt = pl.ds(pl.multiple_of(place.z * PB, PB), PB)
-    prompts = Line(
-        place,
-        tokens.at[:, pl.ds(0, PB)],
-        lambda z: xk.at[:, pl.ds(pl.multiple_of(z * PB, PB), PB)],
-        line_send,
-        line_recv,
-    )
+    prompts = [
+        Line(
+            place,
+            tokens.at[m, pl.ds(0, PB)],
+            lambda z, m=m: xk.at[m, pl.ds(pl.multiple_of(z * PB, PB), PB)],
+            line_send.at[m],
+            line_recv.at[m],
+        )
+        for m in range(micro_count)
+    ]
     own_at = (place.z * high_count + place.high) * 2 + place.low
     loads = [
         (tokens.at[:, pl.ds(0, PB)], xk.at[:, own_prompt]),
@@ -483,7 +485,6 @@
     for copy in load_copies:
         copy.start()
     place.greet()
-    prompts.start()
     for d in early:
         d.start()
     experts.start_x()
@@ -520,31 +521,40 @@
         else:
             buffer[i // local_count - 1, m, i % local_count] = value
 
-    for m in range(micro_count):
+    def expert_gradients(m):
         g_rows = g_all[pl.ds(m * rows, rows), :]
         for i, hit, weight in one_hots(routes.at[m], gates.at[m], me, local_count, total):
             gate = jnp.sum(jnp.where(hit, weight, 0.0), -1, keepdims=True)
             value = mdot(hit.astype(F32).astype(BF), g_rows)
             put(send_do, do_s, m, i, (gate * value).astype(BF))
-    prompts.hop(0)
-    for step in range(depth - 1):
+
+    def early_hop(step):
         for d in early:
             d.hop(step)
-        if step + 1 < depth - 1:
-            prompts.hop(step + 1)
-    for copy in bounce_copies:
-        copy.wait()
-    for d in late:
-        d.start()
-    experts.start_z()
+
+    for step in range(depth - 2):
+        if step < micro_count:
+            expert_gradients(step)
+        early_hop(step)
+    for m in range(max(depth - 2, 0), micro_count):
+        expert_gradients(m)
+    prompts[0].start()
+    early_hop(depth - 2)
+    for m in range(micro_count):
+        for step in range(1, owners):
+            exchange(send_do, do_s, ad_send, ad_recv, m, step).start()
+    prompts[0].hop(0)
     for z in range(depth):
         for d in early:
             d.cross(z)
-    for d in early:
-        d.finish()
-    for m in range(micro_count):
-        for step in range(1, owners):
-            exchange(send_do, do_s, ad_send, ad_recv, m, step).start()
+    for step in range(1, depth - 1):
+        prompts[0].hop(step)
+        if step == 1:
+            for prompt_line in prompts[1:]:
+                prompt_line.start()
+    for z in range(depth):
+        for d in early:
+            d.finish(z)
     store(wq, qkv_o)
     store(wo, out_o)
     shards = depth * owners
@@ -561,8 +571,15 @@
 
     def front(n1, k, v, q, att, hid, lse):
         lse[...] = jnp.zeros_like(lse)
-        for m in range(micro_count):
-
+        pairs = features // (2 * HD)
+
+        def prompt_hop(step):
+            for prompt_line in prompts[1:]:
+                prompt_line.hop(step)
+            if step == depth - 2:
+                experts.start_z()
+
+        def project_all(m):
             def project(here):
                 normed = norm_rows(xk[m, here, :].astype(F32), gain_v[0:1, :])
                 n1[m, here, :] = normed
@@ -576,23 +593,22 @@
                 query = ndot(n1[m, here, :], wq[pl.ds(0, features), :])
                 query = rope(query, cosine[here, :], sine_part[here, :]).astype(BF)
                 q[m, pl.ds(i * PB, PB), :] = query * jnp.asarray(HD**-0.5, BF)
-            for d in late:
-                d.hop(m)
-        store(n1, n1_o)
-        store(k, k_o)
-        store(v, v_o)
-        store(q, q_o)
         lane = lax.broadcasted_iota(jnp.int32, (PB, 2 * HD), 1)
-        column = lax.broadcasted_iota(jnp.int32, (PB, length), 1)
-        row = lax.broadcasted_iota(jnp.int32, (PB, length), 0)
         for m in range(micro_count):
+            project_all(m)
 
             def pair(index, carry):
+                if m == 0:
+                    for step in range(depth - 1):
+                        pl.when(index == min(step, pairs - 1))(lambda step=step: prompt_hop(step))
                 lanes = pl.ds(pl.multiple_of(index * 2 * HD, 2 * HD), 2 * HD)
-                keys, values = k[m, :, lanes], v[m, :, lanes]
                 for i in range(rows // PB):
                     here = pl.ds(i * PB, PB)
                     query = q[m, here, lanes]
+                    seen = prompt + i * PB
+                    keys, values = k[m, pl.ds(0, seen), lanes], v[m, pl.ds(0, seen), lanes]
+                    column = lax.broadcasted_iota(jnp.int32, (PB, seen), 1)
+                    row = lax.broadcasted_iota(jnp.int32, (PB, seen), 0)
                     allowed = column <= row + own_rows(i)[0]
                     parts = []
                     logs = lse[m, here, :]
@@ -608,7 +624,16 @@
                     att[m, here, lanes] = jnp.where(lane < HD, parts[0], parts[1]).astype(BF)
                 return carry
 
-            lax.fori_loop(0, features // (2 * HD), pair, 0)
+            lax.fori_loop(0, pairs, pair, 0)
+            if m == 0:
+                for copy in bounce_copies:
+                    copy.wait()
+                for d in late:
+                    d.start()
+            if m == micro_count - 1:
+                experts.hop(0, 0)
+                for d in late:
+                    d.cross(place.z)
             for i in range(rows // PB):
                 here = pl.ds(i * PB, PB)
                 hidden = xk[m, own_rows(i)[1], :].astype(F32) + mdot(att[m, here, :], wo[...])
@@ -620,18 +645,13 @@
                 put(send_in, in_s, m, i, value.astype(BF))
             for step in range(1, owners):
                 exchange(send_in, in_s, ai_send, ai_recv, m, step).start()
-            if m == 0:
-                for step in range(micro_count, depth - 1):
-                    for d in late:
-                        d.hop(step)
+        store(n1, n1_o)
+        store(k, k_o)
+        store(v, v_o)
+        store(q, q_o)
         store(att, att_o)
         store(hid, hid_o)
         store(lse, lse_o)
-        for z in range(depth):
-            for d in late:
-                d.cross(z)
-        for d in late:
-            d.finish()
         for copy in stores:
             copy.wait()
 
@@ -660,157 +680,168 @@
             for kind, (target, buffer) in enumerate(zip(targets, staged))
         ]
 
-    def shared(out_sum, in_sum):
+    def wait_rows():
+        for m in range(micro_count):
+            for step in range(1, owners):
+                exchanged(in_s, ai_recv, m, step)
+                exchanged(do_s, ad_recv, m, step)
+
+    def returns(local):
+        return [
+            pltpu.make_async_copy(source.at[local], target.at[local], out_sem.at[2 + 2 * local + i])
+            for i, (source, target) in enumerate(((in_s, outs_o), (do_s, dins_o)))
+        ]
+
+    def both(out_sum, in_sum, side_sum, normed_sum):
         out_sum[...] = jnp.zeros_like(out_sum)
         in_sum[...] = jnp.zeros_like(in_sum)
-        count = sg_o.shape[1] // width
-
-        def part(refs, c):
-            here = pl.ds(pl.multiple_of(c * width, 128), width)
-            return [refs[0].at[:, here], refs[1].at[:, here], refs[2].at[here]]
-
-        for copy in chunk_loads(part((sg_o, su_o, sd_o), 0), 0):
-            copy.start()
-
-        def run(c, carry):
-            slot = lax.rem(c, 2)
-
-            def prefetch():
-                for copy in chunk_loads(part((sg_o, su_o, sd_o), c + 1), 1 - slot):
-                    copy.start()
-
-            pl.when(c + 1 < count)(prefetch)
-            for copy in chunk_loads(part((sg_o, su_o, sd_o), c), slot):
-                copy.wait()
-            targets = part((gsg_o, gsu_o, gsd_o), c)
-
+        side_sum[...] = jnp.zeros_like(side_sum)
+        normed_sum[...] = jnp.zeros_like(normed_sum)
+        group = late[0].own.shape[1] * owners // width
+
+        def store_grads(targets, slot, stored):
             def previous():
                 for copy in chunk_stores(targets, slot):
                     copy.wait()
 
-            pl.when(c >= 2)(previous)
+            pl.when(stored)(previous)
+            return lambda: [copy.start() for copy in chunk_stores(targets, slot)]
+
+        def shared_part(refs, c):
+            here = pl.ds(pl.multiple_of(c * width, 128), width)
+            return [refs[0].at[:, here], refs[1].at[:, here], refs[2].at[here]]
+
+        def shared_item(w, z):
+            for d in late:
+                d.finish(z)
+
+            def one(i, carry):
+                c = z * group + i
+                loads = chunk_loads(shared_part((sg_o, su_o, sd_o), c), 2 * local_count + i)
+                for copy in loads:
+                    copy.wait()
+                send = store_grads(shared_part((gsg_o, gsu_o, gsd_o), c), i, w > 0)
+                ffn_chunk(
+                    n2,
+                    g_all,
+                    [buffer.at[2 * local_count + i] for buffer in (wg, wu, wd)],
+                    saved,
+                    (side_sum, normed_sum),
+                    [buffer.at[i] for buffer in staged],
+                    micro_count * rows,
+                )
+                send()
+                return carry
+
+            for i in range(group):
+                for copy in chunk_loads(
+                    shared_part((sg_o, su_o, sd_o), z * group + i), 2 * local_count + i
+                ):
+                    copy.start()
+            lax.fori_loop(0, group, one, 0)
+
+        def expert_item(w, z, crossed, local, side, ahead):
+            shard = jnp.where(crossed, place.other_shard(z), place.shard(z))
+
+            def load(n):
+                sources = [
+                    expert_slab(ref, k, n, shard, width) for k, ref in enumerate((eg_o, eu_o, ed_o))
+                ]
+                return chunk_loads(sources, side * local_count + n)
+
+            def begin(n):
+                def own():
+                    mine = [ref.at[n] for ref in (eg_in, eu_in, ed_in)]
+                    for copy in chunk_loads(mine, side * local_count + n):
+                        copy.start()
+
+                def landed():
+                    pl.when(crossed)(lambda: experts.wait_x(n, z))
+                    for copy in load(n):
+                        copy.start()
+
+                pl.when(w == 1)(own)
+                pl.when(w > 1)(landed)
+
+            def begin_rest():
+                for n in range(1, local_count):
+                    begin(n)
+
+            pl.when(w == 1)(wait_rows)
+            pl.when(local == 0)(lambda: begin(0))
+            pl.when(ahead & (local == 0))(begin_rest)
+            pl.when(jnp.logical_not(ahead) & (local > 0))(lambda: begin(local))
+            for copy in load(local):
+                copy.wait()
+            targets = [
+                expert_slab(ref, k, local, shard, width) for k, ref in enumerate((geg_o, geu_o, ged_o))
+            ]
+            send = store_grads(targets, local, True)
             ffn_chunk(
-                n2,
-                g_all,
-                (wg.at[slot], wu.at[slot], wd.at[slot]),
+                in_s.at[local],
+                do_s.at[local],
+                [buffer.at[side * local_count + local] for buffer in (wg, wu, wd)],
                 saved,
-                (out_sum, in_sum),
-                [buffer.at[slot] for buffer in staged],
-                384,
+                (out_sum.at[local], in_sum.at[local]),
+                [buffer.at[local] for buffer in staged],
+                slots,
             )
-            for copy in chunk_stores(targets, slot):
-                copy.start()
+            send()
+
+        def crossing(step):
+            for d in late:
+                for z in (place.z - 1 - step, place.z + 1 + step):
+                    pl.when(place.on_line(z))(lambda d=d, z=z: d.cross(z))
+
+        def late_hop(step):
+            for d in late:
+                d.hop(step)
+
+        heads = 2 * local_count + 1
+        in_step = 2 * heads
+        after_item = [(local, lambda local=local: experts.hop(local, 0)) for local in range(1, local_count)]
+        after_item = [(local - 1, run) for local, run in after_item]
+        after_item += [(local_count, lambda: late_hop(0)), (heads - 1, lambda: crossing(0))]
+        for step in range(1, depth - 1):
+            here = heads + in_step * step
+            first = here - in_step + 3
+            spots = [first, here - 1] if step == 1 else [here - 1, here + 1]
             for local in range(local_count):
-                pl.when(c == count // 2 + local)(lambda local=local: experts.hop(local, 0))
+                at = spots[min(local, 1)]
+                after_item.append((at, lambda local=local, step=step: experts.hop(local, step)))
+            after_item.append((here + 3, lambda step=step: late_hop(step)))
+            after_item.append((here + 5, lambda step=step: crossing(step)))
+
+        def item(w, carry):
+            head = w < heads
+            after = jnp.maximum(w - heads, 0)
+            step, spot = after // in_step, lax.rem(after, in_step)
+            kind = jnp.where(head, w - 1, spot // 2)
+            turn = jnp.where(head, kind, jnp.where(kind > local_count, kind - 1, kind))
+            is_shared = kind == jnp.where(head, -1, local_count + 1)
+            crossed = turn >= local_count
+            local = jnp.clip(jnp.where(crossed, turn - local_count, turn), 0, local_count - 1)
+            z = jnp.where(head, place.z, place.z + (2 * lax.rem(spot, 2) - 1) * (1 + step))
+            valid = place.on_line(z)
+            pl.when(valid & is_shared)(lambda: shared_item(w, z))
+            ahead = head | (step < depth - 2)
+            side = jnp.where(head, 0, lax.rem(spot, 2))
+            pl.when(valid & jnp.logical_not(is_shared))(
+                lambda: expert_item(w, z, crossed, local, side, ahead)
+            )
+            for at, run in after_item:
+                pl.when(w == at)(run)
             return carry
 
-        lax.fori_loop(0, count, run, 0)
-        for slot in range(2):
-            for copy in chunk_stores(part((gsg_o, gsu_o, gsd_o), slot), slot):
-                copy.wait()
-        ends = [
-            pltpu.make_async_copy(out_sum, side_o, out_sem.at[0]),
-            pltpu.make_async_copy(in_sum, dn2_o, out_sem.at[1]),
+        lax.fori_loop(0, heads + in_step * (depth - 1), item, 0)
+        sums = [
+            pltpu.make_async_copy(side_sum, side_o, out_sem.at[0]),
+            pltpu.make_async_copy(normed_sum, dn2_o, out_sem.at[1]),
         ]
-        for copy in ends:
+        for copy in sums:
             copy.start()
-        for copy in ends:
-            copy.wait()
-
-    pl.run_scoped(
-        shared,
-        pltpu.VMEM((micro_count * rows, features), F32),
-        pltpu.VMEM((micro_count * rows, features), F32),
-    )
-    for m in range(micro_count):
-        for step in range(1, owners):
-            exchanged(in_s, ai_recv, m, step)
-            exchanged(do_s, ad_recv, m, step)
-
-    def routed(out_sum, in_sum):
-        out_sum[...] = jnp.zeros_like(out_sum)
-        in_sum[...] = jnp.zeros_like(in_sum)
-
-        def item(w, carry):
-            after = jnp.maximum(w - 2, 0)
-            step, kind = after // 4, lax.rem(after, 4)
-            side = lax.rem(kind, 2)
-            z = jnp.where(w < 2, place.z, place.z + (2 * side - 1) * (1 + step))
-            crossed = jnp.where(w < 2, w, kind // 2)
-            valid = place.on_line(z)
-            shard = jnp.where(crossed == 1, place.other_shard(z), place.shard(z))
-
-            def load(local):
-                sources = [
-                    expert_slab(ref, kind, local, shard, width)
-                    for kind, ref in enumerate((eg_o, eu_o, ed_o))
-                ]
-                return chunk_loads(sources, local)
-
-            def begin():
-                def own():
-                    for local in range(local_count):
-                        mine = [ref.at[local] for ref in (eg_in, eu_in, ed_in)]
-                        for copy in chunk_loads(mine, local):
-                            copy.start()
-
-                def landed():
-                    def wait_x():
-                        for local in range(local_count):
-                            experts.wait_x(local, z)
-
-                    pl.when(crossed == 1)(wait_x)
-                    for local in range(local_count):
-                        for copy in load(local):
-                            copy.start()
-
-                pl.when(w == 0)(own)
-                pl.when(w > 0)(landed)
-
-            pl.when(valid)(begin)
-
-            def one(local, carry):
-                targets = [
-                    expert_slab(ref, kind, local, shard, width)
-                    for kind, ref in enumerate((geg_o, geu_o, ged_o))
-                ]
-
-                def compute():
-                    for copy in load(local):
-                        copy.wait()
-
-                    def previous():
-                        for copy in chunk_stores(targets, local):
-                            copy.wait()
-
-                    pl.when(w > 0)(previous)
-                    ffn_chunk(
-                        in_s.at[local],
-                        do_s.at[local],
-                        (wg.at[local], wu.at[local], wd.at[local]),
-                        saved,
-                        (out_sum.at[local], in_sum.at[local]),
-                        [buffer.at[local] for buffer in staged],
-                        512,
-                    )
-                    for copy in chunk_stores(targets, local):
-                        copy.start()
-
-                pl.when(valid)(compute)
-                for later in range(1, depth - 1):
-                    at = 0 if later == 1 else 2 + 4 * (later - 2)
-                    pl.when(w == at)(lambda later=later: experts.hop(local, later))
-                return carry
-
-            lax.fori_loop(0, local_count, one, 0)
-            return carry
-
-        lax.fori_loop(0, 2 + 4 * (depth - 1), item, 0)
         for local in range(local_count):
-            targets = [
-                expert_slab(ref, kind, local, 0, width)
-                for kind, ref in enumerate((geg_o, geu_o, ged_o))
-            ]
+            targets = [expert_slab(ref, k, local, 0, width) for k, ref in enumerate((geg_o, geu_o, ged_o))]
             for copy in chunk_stores(targets, local):
                 copy.wait()
 
@@ -819,21 +850,23 @@
                 do_s[local, here, :] = in_sum[local, here, :].astype(BF)
 
             tiles(slots, 256, finish)
+            for copy in returns(local):
+                copy.start()
+        for copy in sums:
+            copy.wait()
 
     pl.run_scoped(
-        routed,
+        both,
         pltpu.VMEM((local_count, slots, features), F32),
         pltpu.VMEM((local_count, slots, features), F32),
-    )
-    ends = [
-        pltpu.make_async_copy(in_s, outs_o, out_sem.at[0]),
-        pltpu.make_async_copy(do_s, dins_o, out_sem.at[1]),
-    ]
-    for copy in ends:
-        copy.start()
-    for copy in ends:
-        copy.wait()
-    prompts.drain()
+        pltpu.VMEM((micro_count * rows, features), F32),
+        pltpu.VMEM((micro_count * rows, features), F32),
+    )
+    for local in range(local_count):
+        for copy in returns(local):
+            copy.wait()
+    for line in prompts:
+        line.drain()
     for d in early + late:
         d.drain()
     experts.drain()
@@ -895,6 +928,7 @@
     ]
     dma = pltpu.SemaphoreType.DMA
     buffers = max(2, local_count)
+    loads = 2 * local_count + 2
     send = pltpu.VMEM((owners - 1, micro_count, local_count, capacity, features), BF)
     scratch = [
         pltpu.VMEM((micro_count, length, features), BF),
@@ -908,9 +942,9 @@
         pltpu.VMEM((local_count, slots, features), BF),
         send,
         send,
-        pltpu.VMEM((buffers, features, width), BF),
-        pltpu.VMEM((buffers, features, width), BF),
-        pltpu.VMEM((buffers, width, features), BF),
+        pltpu.VMEM((loads, features, width), BF),
+        pltpu.VMEM((loads, features, width), BF),
+        pltpu.VMEM((loads, width, features), BF),
         pltpu.VMEM((max(slots, token_rows), width), BF),
         pltpu.VMEM((max(slots, token_rows), width), BF),
         pltpu.VMEM((max(slots, token_rows), width), BF),
@@ -921,16 +955,16 @@
     scratch += DenseGather.semaphores(len(dense), depth, high_count)
     scratch += ExpertGather.semaphores(depth, local_count)
     scratch += [
-        dma((2, depth)),
-        dma((depth,)),
+        dma((micro_count, 2, depth)),
+        dma((micro_count, depth)),
         dma((10 + micro_count,)),
         dma((owners - 1, micro_count)),
         dma((owners - 1, micro_count)),
         dma((owners - 1, micro_count)),
         dma((owners - 1, micro_count)),
+        dma((loads, 3)),
         dma((buffers, 3)),
-        dma((buffers, 3)),
-        dma((12,)),
+        dma((12 + 2 * local_count,)),
     ]
     return pl.pallas_call(
         functools.partial(forward_kernel, sizes),
@@ -1198,12 +1232,11 @@
             self.land[kind].at[slot, local], self.more[kind].at[which], self.load_sem.at[1 + which, kind]
         )
 
-    def pass_on(self, direction, step, local):
+    def pass_on(self, direction, step, local, kinds=(0, 1, 2)):
         def body(z):
-            line = self._line(local, 0)
-            for kind in range(3):
+            for kind in kinds:
                 self._own_load(local, kind, z).start()
-            for kind in range(3):
+            for kind in kinds:
                 line = self._line(local, kind)
                 target = self.cross[kind].at[z, local]
 
@@ -1373,9 +1406,6 @@
     for d in early:
         d.start()
     experts.start()
-    for m in range(micro_count):
-        for step in range(1, owners):
-            hand_back(*returns[1], m, step).start()
 
     def fetch(pairs):
         copies = [
@@ -1401,21 +1431,29 @@
                 pairs.append((piece, target.at[at]))
         fetch(pairs)
 
-    for d in early:
+    for kind, d in enumerate(early):
+        for direction in (1, -1):
+            experts.pass_on(direction, depth - 1, 0, (kind,))
         d.add_low()
+    for m in range(micro_count):
+        for step in range(1, owners):
+            hand_back(*returns[1], m, step).start()
     gain_own[...] = jnp.zeros_like(gain_own)
+
+    def mark_pairs(first, second, m):
+        for i, hit, _ in one_hots(routes.at[m], gates.at[m], me, local_count, total):
+            here = pl.ds(i * capacity, capacity)
+            expert = lax.rem(me * local_count + i, total)
+            hit_first = either(hit, routes[m, 0:1, :] == expert)
+            hit_second = either(hit, routes[m, 1:2, :] == expert)
+            first[here, :] = hit_first.astype(F32).astype(BF)
+            second[here, :] = hit_second.astype(F32).astype(BF)
 
     def after_experts(hidden, extra, back, first, second, g_rows, att, d_attn, wo):
         fetch([(out_w, wo)] + [(att_i.at[m], att.at[pl.ds(m * rows, rows)]) for m in range(micro_count)])
         for m in range(micro_count):
             fetch([(hid_i.at[m], hidden), (cot.at[m], g_rows), (dn2_i.at[pl.ds(m * rows, rows)], extra)])
-            for i, hit, _ in one_hots(routes.at[m], gates.at[m], me, local_count, total):
-                here = pl.ds(i * capacity, capacity)
-                expert = lax.rem(me * local_count + i, total)
-                hit_first = either(hit, routes[m, 0:1, :] == expert)
-                hit_second = either(hit, routes[m, 1:2, :] == expert)
-                first[here, :] = hit_first.astype(F32).astype(BF)
-                second[here, :] = hit_second.astype(F32).astype(BF)
+            mark_pairs(first, second, m)
             fetch_returned(dins_i, ret_in, ri_recv, back, m)
             gain = gain_v[1:2, :]
             for i in range(rows // PB):
@@ -1437,17 +1475,9 @@
                 d_attn[there, :] = low_part
                 d_att[there, :] = ndot(low_part, wo[...]).astype(BF)
             fetch([(extra, d_hidden_o.at[m])])
-            fetch([(side_i.at[pl.ds(m * rows, rows)], extra)])
-            fetch_returned(outs_i, ret_out, ro_recv, back, m)
-            for i in range(rows // PB):
-                here = pl.ds(i * PB, PB)
-                routed = gate_rows[m, here, 0:1] * tdot(first[:, here], back[...])
-                routed += gate_rows[m, here, 1:2] * tdot(second[:, here], back[...])
-                out_rows[here, :] = (hidden[here, :] + extra[here, :] + routed).astype(BF)
-            fetch([(out_rows, mixed_o.at[m])])
-            if m < local_count:
-                experts.pass_on(1, depth - 1, m)
-                experts.pass_on(-1, depth - 1, m)
+            for kind in ((0,), (1, 2))[m] if m < 2 else ():
+                for direction in (1, -1):
+                    experts.pass_on(direction, depth - 1, 1, (kind,))
 
         def out_grad(here):
             g_out[here, :] = tdot(att[:, here], d_attn[...]).astype(BF)
@@ -1466,16 +1496,19 @@
         pltpu.VMEM((micro_count * rows, features), BF),
         pltpu.VMEM((features, features), BF),
     )
-    for local in range(micro_count, local_count):
-        experts.pass_on(1, depth - 1, local)
-        experts.pass_on(-1, depth - 1, local)
-    for d in early:
-        d.add_high()
-    for step in range(depth - 1, 0, -1):
+
+    def both_ways(items, step):
         for direction in (1, -1):
-            for d in early:
-                if step == depth - 1:
-                    d.pass_on(direction, step)
+            for item in items:
+                item.pass_on(direction, step)
+
+    def prompts_on(m, step):
+        for direction in (1, -1):
+            prompts[m].pass_on(direction, step, lambda t, s: add_into(t, [s], 64))
+
+    def experts_on(step, local):
+        for direction in (1, -1):
+            experts.pass_on(direction, step, local)
 
     def own_rows(i):
         start = place.z * PB if i == 0 else prompt + (i - 1) * PB
@@ -1486,20 +1519,23 @@
         load_wq.start()
         lane = lax.broadcasted_iota(jnp.int32, (PB, 2 * HD), 1)
         wide_lane = lax.broadcasted_iota(jnp.int32, (rows, 2 * HD), 1)
-        column = lax.broadcasted_iota(jnp.int32, (PB, length), 1)
-        row = lax.broadcasted_iota(jnp.int32, (PB, length), 0)
+        ds_s[...] = jnp.zeros_like(ds_s)
+        p_s[...] = jnp.zeros_like(p_s)
         for m in range(micro_count):
             fetch([(k_i.at[m], k), (v_i.at[m], v), (q_i.at[m], q), (lse_i.at[m], lse)])
             whole = pl.ds(m * rows, rows)
 
             def pair(index, carry):
                 lanes = pl.ds(pl.multiple_of(index * 2 * HD, 2 * HD), 2 * HD)
-                keys, values = k[:, lanes], v[:, lanes]
                 for i in range(rows // PB):
                     here = pl.ds(i * PB, PB)
                     there = pl.ds(m * rows + i * PB, PB)
                     query, d_out, logs = q[here, lanes], d_att[there, lanes], lse[here, :]
                     start, table = own_rows(i)
+                    seen = prompt + i * PB
+                    keys, values = k[pl.ds(0, seen), lanes], v[pl.ds(0, seen), lanes]
+                    column = lax.broadcasted_iota(jnp.int32, (PB, seen), 1)
+                    row = lax.broadcasted_iota(jnp.int32, (PB, seen), 0)
                     allowed = column <= row + start
                     parts = []
                     for sub in range(2):
@@ -1512,8 +1548,8 @@
                         d_probs = ndot(jnp.where(mine, d_out, jnp.zeros_like(d_out)), values)
                         centre = jnp.sum(probs * d_probs, -1, keepdims=True)
                         d_scores = (probs * (d_probs - centre)).astype(BF)
-                        ds_s[sub, here, :] = d_scores
-                        p_s[sub, here, :] = probs.astype(BF)
+                        ds_s[sub, here, pl.ds(0, seen)] = d_scores
+                        p_s[sub, here, pl.ds(0, seen)] = probs.astype(BF)
                         parts.append(mdot(d_scores, keys))
                     d_query = jnp.where(lane < HD, parts[0], parts[1]) * HD**-0.5
                     d_query = rope(d_query, cosine[table, :], -sine_part[table, :])
@@ -1538,10 +1574,7 @@
             for z in range(depth):
                 here = pl.ds(m * length + z * PB, PB)
                 part[m, z] = (mdot(dpk[here, :], key_w) + mdot(dpv[here, :], value_w)).astype(BF)
-            for step in range(depth - 1, 0, -1):
-                if step == depth - 1:
-                    for direction in (1, -1):
-                        prompts[m].pass_on(direction, step, lambda t, s: add_into(t, [s], 64))
+            prompts_on(m, depth - 1)
             for i in range(rows // PB):
                 _, table = own_rows(i)
                 start = own_rows(i)[0] + m * length
@@ -1553,18 +1586,11 @@
                     + mdot(dpv[here, :], value_w)
                 )
             fetch([(dn1, dn1_o.at[m])])
-            for local in range(local_count):
-                for direction in (1, -1):
-                    if depth > 2 and m == 0:
-                        experts.pass_on(direction, depth - 2, local)
-            for step in range(depth - 2, 0, -1):
-                for direction in (1, -1):
-                    prompts[m].pass_on(direction, step, lambda t, s: add_into(t, [s], 64))
+            experts_on(depth - 2, m)
             if m == 0:
-                for step in range(depth - 2, 0, -1):
-                    for direction in (1, -1):
-                        for d in early:
-                            d.pass_on(direction, step)
+                for d in early:
+                    d.add_high()
+                both_ways(early, depth - 1)
 
     pl.run_scoped(
         attention,
@@ -1609,14 +1635,54 @@
     )
     for d in late:
         d.start()
-    for local in range(local_count):
-        for step in range(depth - 3, 0, -1):
-            for direction in (1, -1):
-                experts.pass_on(direction, step, local)
+
+    for step in range(depth - 2, 1, -1):
+        for m in range(micro_count):
+            prompts_on(m, step)
     for d in late:
         d.add_low()
-    for d in early:
-        d.end()
+
+    def outputs(hidden, side, back, first, second):
+        for m in range(micro_count):
+            fetch([(hid_i.at[m], hidden), (side_i.at[pl.ds(m * rows, rows)], side)])
+            mark_pairs(first, second, m)
+            fetch_returned(outs_i, ret_out, ro_recv, back, m)
+            for i in range(rows // PB):
+                here = pl.ds(i * PB, PB)
+                routed = gate_rows[m, here, 0:1] * tdot(first[:, here], back[...])
+                routed += gate_rows[m, here, 1:2] * tdot(second[:, here], back[...])
+                out_rows[here, :] = (hidden[here, :] + side[here, :] + routed).astype(BF)
+            fetch([(out_rows, mixed_o.at[m])])
+            if m == 0:
+                for step in range(depth - 2, 1, -1):
+                    both_ways(early, step)
+                for d in late:
+                    d.add_high()
+                both_ways(late, depth - 1)
+                for step in range(depth - 3, 0, -1):
+                    experts_on(step, 0)
+
+    pl.run_scoped(
+        outputs,
+        pltpu.VMEM((rows, features), F32),
+        pltpu.VMEM((rows, features), F32),
+        pltpu.VMEM((total * capacity, features), BF),
+        pltpu.VMEM((total * capacity, rows), BF),
+        pltpu.VMEM((total * capacity, rows), BF),
+    )
+
+    def last_on(kind):
+        for step in range(depth - 3, 0, -1):
+            for local in range(1, local_count):
+                for direction in (1, -1):
+                    experts.pass_on(direction, step, local, (kind,))
+
+    for m in range(micro_count):
+        prompts_on(m, 1)
+    both_ways(early, 1)
+    last_on(0)
+    for step in range(depth - 2, 1, -1):
+        both_ways(late, step)
 
     def inputs(x_rows, d_hidden, dn1):
         for m in range(micro_count):
@@ -1649,20 +1715,19 @@
         pltpu.VMEM((rows, features), F32),
         pltpu.VMEM((rows, features), F32),
     )
-    for d in late:
-        d.add_high()
-    for step in range(depth - 1, 0, -1):
-        for direction in (1, -1):
-            for d in late:
-                d.pass_on(direction, step)
-
-    def stage(first, targets, lands):
-        copies = [
+    last_on(1)
+    both_ways(late, 1)
+    last_on(2)
+    for d in early:
+        d.end()
+
+    def gain_copies(first, targets, lands):
+        return [
             remote(gain_own, land, gain_send.at[first + i], gain_recv.at[first + i], **target)
             for i, (target, land) in enumerate(zip(targets, lands))
         ]
-        for copy in copies:
-            copy.start()
+
+    def gain_add(copies, lands):
         for copy in copies:
             copy.wait()
         total_gain = gain_own[...]
@@ -1670,24 +1735,44 @@
             total_gain = total_gain + land[...]
         gain_own[...] = total_gain
 
-    stage(0, [dict(experts=place.e + 1 - 2 * place.low)], [gain_low])
-    stage(
-        1,
-        [dict(experts=place.peer_high(s) * 2 + place.low) for s in range(1, high_count)],
-        [gain_high.at[s - 1] for s in range(1, high_count)],
-    )
-    stage(
-        high_count,
-        [dict(context=lax.rem(place.z + s, depth)) for s in range(1, depth)],
-        [gain_line.at[s - 1] for s in range(1, depth)],
-    )
-    stage(high_count + depth - 1, [dict(dp=1 - place.x)], [gain_cross])
-    for local in range(local_count):
-        experts.end(local)
+    peers = range(1, high_count)
+    places = range(1, depth)
+    stages = [
+        (0, [dict(experts=place.e + 1 - 2 * place.low)], [gain_low]),
+        (
+            1,
+            [dict(experts=place.peer_high(s) * 2 + place.low) for s in peers],
+            [gain_high.at[s - 1] for s in peers],
+        ),
+        (
+            high_count,
+            [dict(context=lax.rem(place.z + s, depth)) for s in places],
+            [gain_line.at[s - 1] for s in places],
+        ),
+        (high_count + depth - 1, [dict(dp=1 - place.x)], [gain_cross]),
+    ]
+
+    def gain_start(i):
+        copies = gain_copies(*stages[i])
+        for copy in copies:
+            copy.start()
+        return copies
+
+    for i in range(2):
+        gain_add(gain_start(i), stages[i][2])
+    line_copies = gain_start(2)
+    experts.end(0)
     for d in late:
         d.end()
-    for d in dense:
+    gain_add(line_copies, stages[2][2])
+    cross_copies = gain_start(3)
+    for d in early:
         d.finish()
+    for d in late:
+        d.finish()
+    for local in range(1, local_count):
+        experts.end(local)
+    gain_add(cross_copies, stages[3][2])
     fetch([(gain_own, gain_o)])
     for d in dense:
         d.drain()

time: 763 us -> 597 us (0.78)
  Pallas kernels: 735 us -> 566 us
    pallas_call x1, Pallas kernels: 361 us -> 275 us  [run_backward(): pl.pallas_call(functools.partial(backward_kernel, sizes), out_shape=out_s...]
    pallas_call x1, Pallas kernels: 375 us -> 292 us  [run_forward(): pl.pallas_call(functools.partial(forward_kernel, sizes), out_shape=out_sh...]
where the time goes in v3:
time: 597 us; the launch traced here: 586 us
  Pallas kernels  566 us (95%)
  other arithmetic  12.2 us (2%)
  local copies, waits for them, and re-layouts  6.64 us (1%)
    pallas_call x1, Pallas kernels, run_forward(): pl.pallas_call(functools.partial(forward_kernel, sizes), out_shape=out_sh...  292 us
    pallas_call x1, Pallas kernels, run_backward(): pl.pallas_call(functools.partial(backward_kernel, sizes), out_shape=out_s...  275 us

profile of v3, /device:TPU:0, one launch (start us, length us, event | category | flops | bytes accessed | tf_op | source)
XLA Modules:
  0.0 586.5 jit_solution(14138338692424038706)
XLA Ops:
  0.7 1.5 dynamic_update_slice.3.refs_8_
  2.2 0.0 copy-start.6
  2.2 0.9 copy.28
  3.1 0.0 copy-start
  3.1 0.7 copy.30.refs_2_
  3.8 0.0 copy-done.6
  3.8 291.9 %gather_and_forward.1 = (bf16[2304,768]{1,0:T(8,128)(2,1)}, bf16[768,768]{1,0:T(8,128)(2,1)}, f32[8,768]{1,0:T(8,128)}, bf16[768,2048]{1,0:T(8,128)(2,1)}, bf16[...) custom-call(bf16[2,384,768]{2,1,0:T(8,128)(2,1)} %bitcast.17, ...), custom_call_target="tpu_custom_call" | custom-call | tf_op jit(solution)/shard_map/gather_and_forward/pallas_call | solution.py:969
  295.7 0.0 copy-done
  295.8 274.5 %backward_and_sum.1 = (bf16[2,384,768]{2,1,0:T(8,128)(2,1)}, bf16[2,384,768]{2,1,0:T(8,128)(2,1)}, bf16[144,768]{1,0:T(8,128)(2,1)}, bf16[48,768]{1,0:T(8,128)(2...) custom-call(bf16[2,384,768]{2,1,0:T(8,128)(2,1)} %bitcast.18, ...), custom_call_target="tpu_custom_call" | custom-call | tf_op jit(solution)/shard_map/backward_and_sum/pallas_call | solution.py:1858
  570.3 0.0 copy-start.5
  570.3 0.0 copy-start.4
  570.3 1.5 constant_dynamic-slice_fusion
  571.8 1.6 convert_element_type.29
  573.3 1.7 convert_element_type.30
  575.0 1.8 convert_element_type.31
  576.8 1.7 convert_element_type.32
  578.5 1.7 convert_bitcast_fusion
  580.2 0.0 copy-done.5
  580.2 1.3 convert_element_type.33
  581.5 1.3 convert_element_type.34
  582.8 1.3 convert_element_type.35
  584.0 0.0 copy-done.2
  584.0 1.0 copy.36
  585.0 1.0 copy.37
  (7 shorter events, 0.0 us)
Async XLA Ops:
  2.2 1.7 copy-start.6
  3.1 292.7 %copy-start = (f32[1,1,2,1,384,2]{5,4,2,3,1,0:T(8,128)}, f32[1,1,2,1,384,2]{5,4,2,3,1,0:T(8,128)S(1)}, u32[]{:S(2)}) copy-start(f32[1,1,2,1,384,2]{5,4,2,3,1,0:T(8,128)S(1)} %copy.28) | copy-start | bytes 18436
  570.3 9.9 %copy-start.5 = (bf16[2,768,256]{2,1,0:T(8,128)(2,1)S(1)}, bf16[2,768,256]{2,1,0:T(8,128)(2,1)}, u32[]{:S(2)}) copy-start(bf16[2,768,256]{2,1,0:T(8,128)(2,1)} %get-tuple-element.70) | copy-start | bytes 2359300
  570.3 11.2 %copy-start.4 = (bf16[2,768,256]{2,1,0:T(8,128)(2,1)S(1)}, bf16[2,768,256]{2,1,0:T(8,128)(2,1)}, u32[]{:S(2)}) copy-start(bf16[2,768,256]{2,1,0:T(8,128)(2,1)} %get-tuple-element.71) | copy-start | bytes 2359300
  575.0 7.7 %copy-start.3 = (bf16[2,256,768]{2,1,0:T(8,128)(2,1)S(1)}, bf16[2,256,768]{2,1,0:T(8,128)(2,1)}, u32[]{:S(2)}) copy-start(bf16[2,256,768]{2,1,0:T(8,128)(2,1)} %get-tuple-element.72) | copy-start | bytes 2359300
  580.2 3.8 copy-start.2
  581.5 3.5 copy-start.1

commit v4 on v3

--- a/solution.py
+++ b/solution.py
@@ -410,7 +410,7 @@
         qkv_in, out_in, gain_in, sg_in, su_in, sd_in, eg_in, eu_in, ed_in,
         qkv_o, out_o, gain_o, sg_o, su_o, sd_o, eg_o, eu_o, ed_o,
         n1_o, k_o, v_o, q_o, att_o, hid_o, lse_o, side_o, dn2_o,
-        gsg_o, gsu_o, gsd_o, geg_o, geu_o, ged_o, outs_o, dins_o,
+        gsg_o, gsu_o, gsd_o, geg_o, geu_o, ged_o, outs_o, dins_o, pre_g, pre_u, pre_d,
         xk, wq, wo, gain_land, gain_v, g_all, n2, in_s, do_s, send_in, send_do,
         wg, wu, wd, act_s, dg_s, du_s, stage_g, stage_u, stage_d,
         *sems,
@@ -419,7 +419,7 @@
     expert_sems, sems = sems[:4], sems[4:]
     (
         line_send, line_recv, load_sem, ai_send, ai_recv, ad_send, ad_recv,
-        chunk_sem, store_sem, out_sem,
+        chunk_sem, store_sem, out_sem, pre_send, pre_recv,
     ) = sems
     micro_count, rows, features = tokens.shape
     prompt = depth * PB
@@ -686,6 +686,45 @@
                 exchanged(in_s, ai_recv, m, step)
                 exchanged(do_s, ad_recv, m, step)
 
+    at_end = (place.z == 0) | (place.z == depth - 1)
+    beside_end = (place.z == 1) | (place.z == depth - 2)
+
+    def sums_to_neighbour(which):
+        z = jnp.where(place.z == 0, 1, depth - 2)
+        return [
+            remote(
+                expert_slab(
+                    ref, kind, local, (place.other_shard if crossed else place.shard)(z), width
+                ),
+                land.at[crossed, local],
+                pre_send.at[crossed, local, kind],
+                pre_recv.at[crossed, local, kind],
+                context=z,
+            )
+            for crossed in which
+            for local in range(local_count)
+            for kind, (ref, land) in enumerate(
+                ((geg_o, pre_g), (geu_o, pre_u), (ged_o, pre_d))
+            )
+        ]
+
+    def send_sums(crossed):
+        def body():
+            for copy in sums_to_neighbour((crossed,)):
+                copy.start()
+
+        pl.when(at_end)(body)
+
+    def sums_sent():
+        for copy in sums_to_neighbour((0, 1)):
+            copy.wait_send()
+
+    def sums_arrived():
+        for crossed in (1, 0):
+            for local in range(local_count):
+                for kind, land in enumerate((pre_g, pre_u, pre_d)):
+                    arrived(land.at[crossed, local], pre_recv.at[crossed, local, kind])
+
     def returns(local):
         return [
             pltpu.make_async_copy(source.at[local], target.at[local], out_sem.at[2 + 2 * local + i])
@@ -804,21 +843,53 @@
         after_item += [(local_count, lambda: late_hop(0)), (heads - 1, lambda: crossing(0))]
         for step in range(1, depth - 1):
             here = heads + in_step * step
-            first = here - in_step + 3
-            spots = [first, here - 1] if step == 1 else [here - 1, here + 1]
+            if step == 1:
+                spots = [heads + 3, jnp.where(at_end, here - 1, heads + 5)]
+                late_spot = jnp.where(at_end, here + 3, heads + 7)
+            else:
+                spots = [here - 3, here + 1 if step == depth - 2 else here - 1]
+                late_spot = here + 3
             for local in range(local_count):
                 at = spots[min(local, 1)]
                 after_item.append((at, lambda local=local, step=step: experts.hop(local, step)))
-            after_item.append((here + 3, lambda step=step: late_hop(step)))
+            after_item.append((late_spot, lambda step=step: late_hop(step)))
             after_item.append((here + 5, lambda step=step: crossing(step)))
+        after_item.append((heads + in_step - 3, lambda: send_sums(0)))
+        after_item.append((heads + in_step - 1, lambda: send_sums(1)))
+        count = heads + in_step * (depth - 1)
+
+        def finish(local):
+            def convert(here):
+                in_s[local, here, :] = out_sum[local, here, :].astype(BF)
+                do_s[local, here, :] = in_sum[local, here, :].astype(BF)
+
+            tiles(slots, 256, convert)
+            for copy in returns(local):
+                copy.start()
+
+        def side_sums():
+            return [
+                pltpu.make_async_copy(side_sum, side_o, out_sem.at[0]),
+                pltpu.make_async_copy(normed_sum, dn2_o, out_sem.at[1]),
+            ]
+
+        def finish_first():
+            for copy in side_sums():
+                copy.start()
+            finish(0)
+
+        after_item.append((count - 2 * (local_count - 1) - 1, finish_first))
 
         def item(w, carry):
             head = w < heads
             after = jnp.maximum(w - heads, 0)
             step, spot = after // in_step, lax.rem(after, in_step)
             kind = jnp.where(head, w - 1, spot // 2)
-            turn = jnp.where(head, kind, jnp.where(kind > local_count, kind - 1, kind))
-            is_shared = kind == jnp.where(head, -1, local_count + 1)
+            last = jnp.logical_not(head) & (step == depth - 2)
+            turn = jnp.where(last & (kind > local_count), kind - 1, kind)
+            is_shared = kind == jnp.where(
+                head, -1, jnp.where(last, local_count + 1, 2 * local_count)
+            )
             crossed = turn >= local_count
             local = jnp.clip(jnp.where(crossed, turn - local_count, turn), 0, local_count - 1)
             z = jnp.where(head, place.z, place.z + (2 * lax.rem(spot, 2) - 1) * (1 + step))
@@ -833,26 +904,14 @@
                 pl.when(w == at)(run)
             return carry
 
-        lax.fori_loop(0, heads + in_step * (depth - 1), item, 0)
-        sums = [
-            pltpu.make_async_copy(side_sum, side_o, out_sem.at[0]),
-            pltpu.make_async_copy(normed_sum, dn2_o, out_sem.at[1]),
-        ]
-        for copy in sums:
-            copy.start()
+        lax.fori_loop(0, count, item, 0)
         for local in range(local_count):
             targets = [expert_slab(ref, k, local, 0, width) for k, ref in enumerate((geg_o, geu_o, ged_o))]
             for copy in chunk_stores(targets, local):
                 copy.wait()
-
-            def finish(here, local=local):
-                in_s[local, here, :] = out_sum[local, here, :].astype(BF)
-                do_s[local, here, :] = in_sum[local, here, :].astype(BF)
-
-            tiles(slots, 256, finish)
-            for copy in returns(local):
-                copy.start()
-        for copy in sums:
+        for local in range(1, local_count):
+            finish(local)
+        for copy in side_sums():
             copy.wait()
 
     pl.run_scoped(
@@ -865,6 +924,8 @@
     for local in range(local_count):
         for copy in returns(local):
             copy.wait()
+    pl.when(beside_end)(sums_arrived)
+    pl.when(at_end)(sums_sent)
     for line in prompts:
         line.drain()
     for d in early + late:
@@ -925,6 +986,9 @@
         shape(BF, local_count, *wide), shape(BF, local_count, *wide), shape(BF, local_count, *tall),
         shape(BF, local_count, slots, features),
         shape(BF, local_count, slots, features),
+        shape(BF, 2, local_count, features, width),
+        shape(BF, 2, local_count, features, width),
+        shape(BF, 2, local_count, width, features),
     ]
     dma = pltpu.SemaphoreType.DMA
     buffers = max(2, local_count)
@@ -965,6 +1029,8 @@
         dma((loads, 3)),
         dma((buffers, 3)),
         dma((12 + 2 * local_count,)),
+        dma((2, local_count, 3)),
+        dma((2, local_count, 3)),
     ]
     return pl.pallas_call(
         functools.partial(forward_kernel, sizes),
@@ -1168,7 +1234,10 @@
 
 
 class ExpertScatter:
-    def __init__(self, place, sums, cross, land, own, more, outs, sems):
+    def __init__(self, place, sums, cross, land, own, more, early, absorbed, outs, sems):
+        self.early, self.absorbed = early, absorbed
+        self.at_end = (place.z == 0) | (place.z == place.depth - 1)
+        self.beside_end = (place.z == 1) | (place.z == place.depth - 2)
         self.place, self.sums, self.cross, self.land = place, sums, cross, land
         self.own, self.more, self.outs = own, more, outs
         self.x_send, self.x_recv, self.z_send, self.z_recv, self.load_sem, self.out_sem = sems
@@ -1209,8 +1278,10 @@
         for step in range(place.depth - 1, 0, -1):
             for direction in (1, -1):
                 z = place.z + direction * step
-                pl.when(place.on_line(z))(lambda z=z: body(z))
-        body(place.z)
+                here = place.on_line(z)
+                if step == 1:
+                    here = here & jnp.logical_not(self.at_end)
+                pl.when(here)(lambda z=z: body(z))
 
     def start(self):
         def body(z):
@@ -1219,6 +1290,52 @@
                     self._across(local, kind, z).start()
 
         self._order(body)
+        pl.when(jnp.logical_not(self.beside_end))(lambda: body(self.place.z))
+
+    def absorb(self):
+        z = self.place.z
+
+        def body():
+            for local in range(self.local_count):
+                loads = []
+                for kind in range(3):
+                    source = expert_slab(
+                        self.sums[kind], kind, local, self.place.other_shard(z), self.width
+                    )
+                    early = self.early[kind].at[1, local]
+                    loads.append(
+                        [
+                            pltpu.make_async_copy(source, self.own[kind], self.load_sem.at[0, kind]),
+                            pltpu.make_async_copy(
+                                early, self.more[kind].at[0], self.load_sem.at[1, kind]
+                            ),
+                        ]
+                    )
+                stores = [
+                    pltpu.make_async_copy(
+                        self.own[kind], self.absorbed[kind].at[local], self.load_sem.at[0, kind]
+                    )
+                    for kind in range(3)
+                ]
+                for pair in loads:
+                    for copy in pair:
+                        copy.start()
+                for kind in range(3):
+                    for copy in loads[kind]:
+                        copy.wait()
+                    add_into(self.own[kind], [self.more[kind].at[0]], 64)
+                    stores[kind].start()
+                for kind in range(3):
+                    stores[kind].wait()
+                    remote(
+                        self.absorbed[kind].at[local],
+                        self.cross[kind].at[z, local],
+                        self.x_send.at[local, kind, z],
+                        self.x_recv.at[local, kind, z],
+                        dp=1 - self.place.x,
+                    ).start()
+
+        pl.when(self.beside_end)(body)
 
     def _own_load(self, local, kind, z):
         return pltpu.make_async_copy(
@@ -1259,7 +1376,18 @@
                 pl.when(jnp.logical_not(line.upstream(direction)))(single)
                 line.copy(z, direction).start()
 
-        self._line(local, 0).at(direction, step, body)
+        def there(z):
+            if step == 1:
+                pl.when(jnp.logical_not(self.at_end))(lambda: body(z))
+            else:
+                body(z)
+
+        self._line(local, 0).at(direction, step, there)
+
+    def _early_load(self, local, kind, which):
+        return pltpu.make_async_copy(
+            self.early[kind].at[0, local], self.more[kind].at[which], self.load_sem.at[1 + which, kind]
+        )
 
     def end(self, local):
         place = self.place
@@ -1275,7 +1403,12 @@
                     line.arrive(slot)
                     self._more_load(local, kind, slot, which).start()
 
-                pl.when(line.upstream(direction))(come)
+                def came(which=which, kind=kind):
+                    self._early_load(local, kind, which).start()
+
+                from_end = z - direction == (0 if direction > 0 else place.depth - 1)
+                pl.when(line.upstream(direction) & jnp.logical_not(from_end))(come)
+                pl.when(from_end)(came)
             self._across(local, kind, z).wait_recv()
             self._own_load(local, kind, z).wait()
             add_into(target, [self.own[kind]], 64)
@@ -1298,9 +1431,22 @@
     def drain(self):
         for local in range(self.local_count):
             for kind in range(3):
-                for z in range(self.place.depth):
-                    self._across(local, kind, z).wait_send()
-                self._line(local, kind).drain()
+                self._order(lambda z, p=(local, kind): self._across(*p, z).wait_send())
+                self._across(local, kind, self.place.z).wait_send()
+                line = self._line(local, kind)
+                for step in range(1, self.place.depth):
+                    for direction in (1, -1):
+
+                        def sent(z, line=line, direction=direction):
+                            line.copy(z, direction).wait_send()
+
+                        def there(z, step=step, sent=sent):
+                            if step == 1:
+                                pl.when(jnp.logical_not(self.at_end))(lambda: sent(z))
+                            else:
+                                sent(z)
+
+                        line.at(direction, step, there)
                 self._store(local, kind).wait()
 
 
@@ -1311,9 +1457,9 @@
     (
         tokens, cot, gates, routes, gate_rows, cosine, sine_part,
         qkv_w, out_w, gain_v, n1_i, k_i, v_i, q_i, att_i, hid_i, lse_i, side_i, dn2_i,
-        gsg, gsu, gsd, geg, geu, ged, outs_i, dins_i,
+        gsg, gsu, gsd, geg, geu, ged, outs_i, dins_i, pre_g, pre_u, pre_d,
         mixed_o, input_o, gqkv_o, gout_o, gsg_o, gsu_o, gsd_o, geg_o, geu_o, ged_o, gain_o,
-        eland_g, eland_u, eland_d, ret_in, ret_out, d_hidden_o, dn1_o,
+        eland_g, eland_u, eland_d, ret_in, ret_out, d_hidden_o, dn1_o, abs_g, abs_u, abs_d,
         *rest,
     ) = refs
     count = 5
@@ -1371,6 +1517,8 @@
         (eland_g, eland_u, eland_d),
         (eown_g, eown_u, eown_d),
         (emore_g, emore_u, emore_d),
+        (pre_g, pre_u, pre_d),
+        (abs_g, abs_u, abs_d),
         (geg_o, geu_o, ged_o),
         expert_sems,
     )
@@ -1438,6 +1586,7 @@
     for m in range(micro_count):
         for step in range(1, owners):
             hand_back(*returns[1], m, step).start()
+    experts.absorb()
     gain_own[...] = jnp.zeros_like(gain_own)
 
     def mark_pairs(first, second, m):
@@ -1506,9 +1655,15 @@
         for direction in (1, -1):
             prompts[m].pass_on(direction, step, lambda t, s: add_into(t, [s], 64))
 
-    def experts_on(step, local):
-        for direction in (1, -1):
-            experts.pass_on(direction, step, local)
+    def experts_on(step, local, where=True):
+        def body():
+            for direction in (1, -1):
+                experts.pass_on(direction, step, local)
+
+        pl.when(where)(body)
+
+    inside = jnp.logical_not(experts.at_end)
+    experts_on(depth - 2, 0, inside)
 
     def own_rows(i):
         start = place.z * PB if i == 0 else prompt + (i - 1) * PB
@@ -1586,8 +1741,9 @@
                     + mdot(dpv[here, :], value_w)
                 )
             fetch([(dn1, dn1_o.at[m])])
-            experts_on(depth - 2, m)
+            experts_on(depth - 2, m, experts.at_end)
             if m == 0:
+                experts_on(depth - 2, 1, inside)
                 for d in early:
                     d.add_high()
                 both_ways(early, depth - 1)
@@ -1656,11 +1812,11 @@
             if m == 0:
                 for step in range(depth - 2, 1, -1):
                     both_ways(early, step)
-                for d in late:
-                    d.add_high()
-                both_ways(late, depth - 1)
                 for step in range(depth - 3, 0, -1):
                     experts_on(step, 0)
+                for n in range(micro_count):
+                    prompts_on(n, 1)
+                both_ways(early, 1)
 
     pl.run_scoped(
         outputs,
@@ -1677,10 +1833,11 @@
                 for direction in (1, -1):
                     experts.pass_on(direction, step, local, (kind,))
 
-    for m in range(micro_count):
-        prompts_on(m, 1)
-    both_ways(early, 1)
+    for d in late:
+        d.add_high()
+    both_ways(late, depth - 1)
     last_on(0)
+    last_on(1)
     for step in range(depth - 2, 1, -1):
         both_ways(late, step)
 
@@ -1715,11 +1872,10 @@
         pltpu.VMEM((rows, features), F32),
         pltpu.VMEM((rows, features), F32),
     )
-    last_on(1)
-    both_ways(late, 1)
     last_on(2)
     for d in early:
         d.end()
+    both_ways(late, 1)
 
     def gain_copies(first, targets, lands):
         return [
@@ -1812,6 +1968,7 @@
     out_shape += [jax.ShapeDtypeStruct((depth + 1, local_count) + s, BF) for s in expert_shapes]
     out_shape += [jax.ShapeDtypeStruct(returned, BF)] * 2
     out_shape += [jax.ShapeDtypeStruct((micro_count, rows, features), F32)] * 2
+    out_shape += [jax.ShapeDtypeStruct((local_count,) + s, BF) for s in expert_shapes]
     scratch = [pltpu.VMEM((depth, high_count) + s, BF) for s in shapes]
     scratch += [pltpu.VMEM((high_count - 1, depth) + s, BF) for s in shapes]
     scratch += [pltpu.VMEM((depth + 1,) + s, BF) for s in shapes]
@@ -1858,7 +2015,7 @@
     return pl.pallas_call(
         functools.partial(backward_kernel, sizes),
         out_shape=out_shape,
-        in_specs=[hbm] * 2 + [vmem] * 5 + [hbm] * 2 + [vmem] + [hbm] * 17,
+        in_specs=[hbm] * 2 + [vmem] * 5 + [hbm] * 2 + [vmem] + [hbm] * 20,
         out_specs=[hbm] * len(out_shape),
         scratch_shapes=scratch,
         compiler_params=pltpu.CompilerParams(
@@ -1866,6 +2023,62 @@
         ),
         name="backward_and_sum",
     )(tokens, cot, gates, routes, gate_rows, cosine, sine_part, *forward)
+
+
+def finish_kernel(count, gain_width, *refs):
+    low, refs = refs[:count], refs[count:]
+    rows, refs = refs[:2], refs[2:]
+    gain, refs = refs[0], refs[1:]
+    rows_o, refs = refs[:2], refs[2:]
+    wide_o, refs = refs[:count], refs[count:]
+    gain_o, refs = refs[0], refs[1:]
+    low_s, refs = refs[:count], refs[count:]
+    wide_s, refs = refs[:count], refs[count:]
+    rows_s, sem_in, sem_out = refs[:2], refs[2], refs[3]
+    loads = [
+        pltpu.make_async_copy(source, target, sem_in.at[i])
+        for i, (source, target) in enumerate(zip(low + rows, low_s + rows_s))
+    ]
+    for copy in loads:
+        copy.start()
+    stores = [
+        pltpu.make_async_copy(source, target, sem_out.at[i])
+        for i, (source, target) in enumerate(zip(wide_s + rows_s, wide_o + rows_o))
+    ]
+    place = (lax.axis_index(CONTEXT) * lax.axis_size(EXPERTS) + lax.axis_index(EXPERTS)) * gain_width
+    features = gain.shape[1]
+    gain_o[...] = pltpu.roll(gain[...], lax.rem(features - place, features), 1)[:2, :gain_width]
+    for i in range(count):
+        loads[i].wait()
+        wide_s[i][...] = low_s[i][...].astype(F32)
+        stores[i].start()
+    for i in range(count, count + 2):
+        loads[i].wait()
+        stores[i].start()
+    for copy in stores:
+        copy.wait()
+
+
+def finish_outputs(low, rows, gain, gain_width):
+    count = len(low)
+    hbm, vmem = pl.BlockSpec(memory_space=pltpu.HBM), pl.BlockSpec(memory_space=pltpu.VMEM)
+    wide = [item.shape for item in low]
+    out_shape = [jax.ShapeDtypeStruct(item.shape, BF) for item in rows]
+    out_shape += [jax.ShapeDtypeStruct(dims, F32) for dims in wide]
+    out_shape += [jax.ShapeDtypeStruct((2, gain_width), F32)]
+    dma = pltpu.SemaphoreType.DMA
+    return pl.pallas_call(
+        functools.partial(finish_kernel, count, gain_width),
+        out_shape=out_shape,
+        in_specs=[hbm] * (count + 2) + [vmem],
+        out_specs=[hbm] * (count + 2) + [vmem],
+        scratch_shapes=[pltpu.VMEM(item.shape, BF) for item in low]
+        + [pltpu.VMEM(dims, F32) for dims in wide]
+        + [pltpu.VMEM(item.shape, BF) for item in rows]
+        + [dma((count + 2,)), dma((count + 2,))],
+        compiler_params=pltpu.CompilerParams(vmem_limit_bytes=60 * MIB),
+        name="finish_outputs",
+    )(*low, *rows, gain)
 
 
 def on_device_plain(
@@ -2268,18 +2481,25 @@
     ) = run_backward(
         sizes, rows, cot, gate_columns, route_columns, gate_rows, forward[:3] + forward[9:]
     )
+    mixed, input_grad, grad_qkv, *rest = finish_outputs(
+        (grad_qkv, grad_out, grad_sgate, grad_sup, grad_sdown, grad_egate, grad_eup, grad_edown),
+        (mixed, input_grad),
+        gain_sum,
+        gain_width,
+    )
+    grad_out, grad_sgate, grad_sup, grad_sdown, grad_egate, grad_eup, grad_edown, grad_gains = rest
     return (
         mixed.reshape(tokens.shape),
         input_grad.reshape(tokens.shape),
-        grad_qkv.T.astype(F32),
-        grad_out.astype(F32),
-        grad_sgate.astype(F32),
-        grad_sup.astype(F32),
-        grad_sdown.astype(F32),
-        lax.dynamic_slice(gain_sum, (0, own_at * gain_width), (2, gain_width)),
-        grad_egate.astype(F32),
-        grad_eup.astype(F32),
-        grad_edown.astype(F32),
+        grad_qkv.T,
+        grad_out,
+        grad_sgate,
+        grad_sup,
+        grad_sdown,
+        grad_gains,
+        grad_egate,
+        grad_eup,
+        grad_edown,
     )
 
 
@@ -2288,10 +2508,12 @@
     rows = (qkv_weight.shape[1], out_weight.shape[0], shared_gate.shape[1], shared_down.shape[0])
     return (
         mesh_shape[DP] == 2
+        and mesh_shape[CONTEXT] >= 4
         and mesh_shape[EXPERTS] % 2 == 0
         and all(count % 16 == 0 for count in rows)
         and shared_gate.shape[1] % 128 == 0
         and arrays[10].shape[2] % 128 == 0
+        and shared_gate.shape[1] * mesh_shape[EXPERTS] == 2 * arrays[10].shape[2]
     )
 
 

time: 597 us -> 549 us (0.920)
  the two profiles are of different devices: /device:TPU:0 before, /device:TPU:15 now
where the time goes in v4:
time: 549 us; the launch traced here: 539 us
  Pallas kernels  535 us (97%)
    pallas_call x1, Pallas kernels, run_backward(): pl.pallas_call(functools.partial(backward_kernel, sizes), out_shape=out_s...  264 us
    pallas_call x1, Pallas kernels, run_forward(): pl.pallas_call(functools.partial(forward_kernel, sizes), out_shape=out_sh...  263 us

profile of v4, /device:TPU:15, one launch (start us, length us, event | category | flops | bytes accessed | tf_op | source)
XLA Modules:
  0.0 539.0 jit_solution(3540720051459239625)
XLA Ops:
  0.7 1.7 dynamic_update_slice.3.refs_8_
  2.4 0.0 copy-start.1
  2.4 0.9 copy.28
  3.2 0.0 copy-start
  3.3 0.7 copy.30.refs_2_
  4.0 0.0 copy-done.1
  4.0 263.3 %gather_and_forward.1 = (bf16[2304,768]{1,0:T(8,128)(2,1)}, bf16[768,768]{1,0:T(8,128)(2,1)}, f32[8,768]{1,0:T(8,128)}, bf16[768,2048]{1,0:T(8,128)(2,1)}, bf16[...) custom-call(bf16[2,384,768]{2,1,0:T(8,128)(2,1)} %bitcast.16, ...), custom_call_target="tpu_custom_call" | custom-call | tf_op jit(solution)/shard_map/gather_and_forward/pallas_call | solution.py:1035
  267.4 0.0 copy-done
  267.4 263.9 %backward_and_sum.1 = (bf16[2,384,768]{2,1,0:T(8,128)(2,1)}, bf16[2,384,768]{2,1,0:T(8,128)(2,1)}, bf16[144,768]{1,0:T(8,128)(2,1)}, bf16[48,768]{1,0:T(8,128)(2...) custom-call(bf16[2,384,768]{2,1,0:T(8,128)(2,1)} %bitcast.17, ...), custom_call_target="tpu_custom_call" | custom-call | tf_op jit(solution)/shard_map/backward_and_sum/pallas_call | solution.py:2015
  531.3 7.3 %finish_outputs.1 = (bf16[2,384,768]{2,1,0:T(8,128)(2,1)}, bf16[2,384,768]{2,1,0:T(8,128)(2,1)}, f32[144,768]{1,0:T(8,128)}, f32[48,768]{1,0:T(8,128)}, f32[768,...) custom-call(bf16[144,768]{1,0:T(8,128)(2,1)} %get-tuple-element.79.r, ...), custom_call_target="tpu_custom_call" | custom-call | tf_op jit(solution)/shard_map/finish_outputs/pallas_call | solution.py:2070
  (1 shorter events, 0.0 us)
Async XLA Ops:
  2.4 1.7 copy-start.1
  3.2 264.1 %copy-start = (f32[1,1,2,1,384,2]{5,4,2,3,1,0:T(8,128)}, f32[1,1,2,1,384,2]{5,4,2,3,1,0:T(8,128)S(1)}, u32[]{:S(2)}) copy-start(f32[1,1,2,1,384,2]{5,4,2,3,1,0:T(8,128)S(1)} %copy.28) | copy-start | bytes 18436

commit v5 on v4

--- a/solution.py
+++ b/solution.py
@@ -300,8 +300,8 @@
             for kind in range(3):
                 self._line(local, kind).start()
 
-    def hop(self, local, step):
-        for kind in range(3):
+    def hop(self, local, step, kinds=(0, 1, 2)):
+        for kind in kinds:
             self._line(local, kind).hop(
                 step, lambda z, kind=kind: self._across(local, kind, z).start()
             )
@@ -843,17 +843,31 @@
         after_item += [(local_count, lambda: late_hop(0)), (heads - 1, lambda: crossing(0))]
         for step in range(1, depth - 1):
             here = heads + in_step * step
-            if step == 1:
-                spots = [heads + 3, jnp.where(at_end, here - 1, heads + 5)]
-                late_spot = jnp.where(at_end, here + 3, heads + 7)
+            late_spot, cross_spot = here + 3, here + 5
+            if step == depth - 2:
+                before = here - in_step
+                spots = [(0, before + 3), (0, before + 5), (0, before + 7)]
+                spots += [(local, here - 1) for local in range(1, local_count)]
+                spots += [(local, here + 1) for local in range(1, local_count)] * 2
+                late_spot, cross_spot = here + 5, here + 7
+                kinds = {}
+                for local, at in spots:
+                    kind = kinds.get(local, 0)
+                    kinds[local] = kind + 1
+                    after_item.append(
+                        (at, lambda p=(local, step, (kind,)): experts.hop(*p))
+                    )
             else:
-                spots = [here - 3, here + 1 if step == depth - 2 else here - 1]
-                late_spot = here + 3
-            for local in range(local_count):
-                at = spots[min(local, 1)]
-                after_item.append((at, lambda local=local, step=step: experts.hop(local, step)))
+                if step == 1:
+                    spots = [heads + 3, jnp.where(at_end, here - 1, heads + 5)]
+                    late_spot = jnp.where(at_end, here + 3, heads + 7)
+                else:
+                    spots = [here - 3, here - 1]
+                for local in range(local_count):
+                    at = spots[min(local, 1)]
+                    after_item.append((at, lambda p=(local, step): experts.hop(*p)))
             after_item.append((late_spot, lambda step=step: late_hop(step)))
-            after_item.append((here + 5, lambda step=step: crossing(step)))
+            after_item.append((cross_spot, lambda step=step: crossing(step)))
         after_item.append((heads + in_step - 3, lambda: send_sums(0)))
         after_item.append((heads + in_step - 1, lambda: send_sums(1)))
         count = heads + in_step * (depth - 1)
@@ -873,25 +887,31 @@
                 pltpu.make_async_copy(normed_sum, dn2_o, out_sem.at[1]),
             ]
 
-        def finish_first():
-            for copy in side_sums():
-                copy.start()
-            finish(0)
-
-        after_item.append((count - 2 * (local_count - 1) - 1, finish_first))
+        def finish_routed():
+            for local in range(local_count):
+                finish(local)
+
+        def early_drain():
+            for line in prompts:
+                line.drain()
+            for d in early:
+                d.drain()
+            for m in range(micro_count):
+                for step in range(1, owners):
+                    exchange(send_do, do_s, ad_send, ad_recv, m, step).wait_send()
+                    exchange(send_in, in_s, ai_send, ai_recv, m, step).wait_send()
+
+        after_item.append((count - in_step, early_drain))
+        after_item.append((count - 3, finish_routed))
 
         def item(w, carry):
             head = w < heads
             after = jnp.maximum(w - heads, 0)
             step, spot = after // in_step, lax.rem(after, in_step)
             kind = jnp.where(head, w - 1, spot // 2)
-            last = jnp.logical_not(head) & (step == depth - 2)
-            turn = jnp.where(last & (kind > local_count), kind - 1, kind)
-            is_shared = kind == jnp.where(
-                head, -1, jnp.where(last, local_count + 1, 2 * local_count)
-            )
-            crossed = turn >= local_count
-            local = jnp.clip(jnp.where(crossed, turn - local_count, turn), 0, local_count - 1)
+            is_shared = kind == jnp.where(head, -1, 2 * local_count)
+            crossed = kind >= local_count
+            local = jnp.clip(jnp.where(crossed, kind - local_count, kind), 0, local_count - 1)
             z = jnp.where(head, place.z, place.z + (2 * lax.rem(spot, 2) - 1) * (1 + step))
             valid = place.on_line(z)
             pl.when(valid & is_shared)(lambda: shared_item(w, z))
@@ -905,12 +925,12 @@
             return carry
 
         lax.fori_loop(0, count, item, 0)
+        for copy in side_sums():
+            copy.start()
         for local in range(local_count):
             targets = [expert_slab(ref, k, local, 0, width) for k, ref in enumerate((geg_o, geu_o, ged_o))]
             for copy in chunk_stores(targets, local):
                 copy.wait()
-        for local in range(1, local_count):
-            finish(local)
         for copy in side_sums():
             copy.wait()
 
@@ -926,15 +946,9 @@
             copy.wait()
     pl.when(beside_end)(sums_arrived)
     pl.when(at_end)(sums_sent)
-    for line in prompts:
-        line.drain()
-    for d in early + late:
+    for d in late:
         d.drain()
     experts.drain()
-    for m in range(micro_count):
-        for step in range(1, owners):
-            exchange(send_do, do_s, ad_send, ad_recv, m, step).wait_send()
-            exchange(send_in, in_s, ai_send, ai_recv, m, step).wait_send()
 
 
 def rope_tables(prompt):
@@ -1224,10 +1238,12 @@
         self._add(self.cross, self.low.at[self.place.z, self.place.high])
         self._store().start()
 
-    def drain(self):
+    def drain_first(self):
         self._each(lambda z, high: self._to_low(z, high).wait_send())
         for step in range(1, self.place.high_count):
             self._to_high(step).wait_send()
+
+    def drain(self):
         self.line.drain()
         self._across().wait_send()
         self._store().wait()
@@ -1810,13 +1826,8 @@
                 out_rows[here, :] = (hidden[here, :] + side[here, :] + routed).astype(BF)
             fetch([(out_rows, mixed_o.at[m])])
             if m == 0:
-                for step in range(depth - 2, 1, -1):
-                    both_ways(early, step)
                 for step in range(depth - 3, 0, -1):
                     experts_on(step, 0)
-                for n in range(micro_count):
-                    prompts_on(n, 1)
-                both_ways(early, 1)
 
     pl.run_scoped(
         outputs,
@@ -1836,10 +1847,14 @@
     for d in late:
         d.add_high()
     both_ways(late, depth - 1)
+    for m in range(micro_count):
+        prompts_on(m, 1)
+    for step in range(depth - 2, 1, -1):
+        both_ways(early, step)
+        both_ways(late, step)
+    both_ways(early, 1)
     last_on(0)
     last_on(1)
-    for step in range(depth - 2, 1, -1):
-        both_ways(late, step)
 
     def inputs(x_rows, d_hidden, dn1):
         for m in range(micro_count):
@@ -1872,10 +1887,10 @@
         pltpu.VMEM((rows, features), F32),
         pltpu.VMEM((rows, features), F32),
     )
+    both_ways(late, 1)
     last_on(2)
     for d in early:
         d.end()
-    both_ways(late, 1)
 
     def gain_copies(first, targets, lands):
         return [
@@ -1918,6 +1933,12 @@
         gain_add(gain_start(i), stages[i][2])
     line_copies = gain_start(2)
     experts.end(0)
+    for d in dense:
+        d.drain_first()
+    for m in range(micro_count):
+        for step in range(1, owners):
+            for entry in returns:
+                hand_back(*entry, m, step).wait_send()
     for d in late:
         d.end()
     gain_add(line_copies, stages[2][2])
@@ -1935,10 +1956,6 @@
     experts.drain()
     for p in prompts:
         p.drain()
-    for m in range(micro_count):
-        for step in range(1, owners):
-            for entry in returns:
-                hand_back(*entry, m, step).wait_send()
 
 
 def run_backward(sizes, tokens, cot, gates, routes, gate_rows, forward):

time: 549 us -> 548 us (level)
  the two profiles are of different devices: /device:TPU:15 before, /device:TPU:0 now
where the time goes in v5:
time: 548 us; the launch traced here: 538 us
  Pallas kernels  533 us (97%)
    pallas_call x1, Pallas kernels, run_forward(): pl.pallas_call(functools.partial(forward_kernel, sizes), out_shape=out_sh...  277 us
    pallas_call x1, Pallas kernels, run_backward(): pl.pallas_call(functools.partial(backward_kernel, sizes), out_shape=out_s...  249 us

profile of v5, /device:TPU:0, one launch (start us, length us, event | category | flops | bytes accessed | tf_op | source)
XLA Modules:
  0.0 537.5 jit_solution(2037988011918267835)
XLA Ops:
  0.7 1.5 dynamic_update_slice.3.refs_8_
  2.2 0.0 copy-start.1
  2.2 0.9 copy.28
  3.1 0.0 copy-start
  3.1 0.7 copy.30.refs_2_
  3.8 0.0 copy-done.1
  3.8 277.3 %gather_and_forward.1 = (bf16[2304,768]{1,0:T(8,128)(2,1)}, bf16[768,768]{1,0:T(8,128)(2,1)}, f32[8,768]{1,0:T(8,128)}, bf16[768,2048]{1,0:T(8,128)(2,1)}, bf16[...) custom-call(bf16[2,384,768]{2,1,0:T(8,128)(2,1)} %bitcast.16, ...), custom_call_target="tpu_custom_call" | custom-call | tf_op jit(solution)/shard_map/gather_and_forward/pallas_call | solution.py:1049
  281.1 0.0 copy-done
  281.1 248.7 %backward_and_sum.1 = (bf16[2,384,768]{2,1,0:T(8,128)(2,1)}, bf16[2,384,768]{2,1,0:T(8,128)(2,1)}, bf16[144,768]{1,0:T(8,128)(2,1)}, bf16[48,768]{1,0:T(8,128)(2...) custom-call(bf16[2,384,768]{2,1,0:T(8,128)(2,1)} %bitcast.17, ...), custom_call_target="tpu_custom_call" | custom-call | tf_op jit(solution)/shard_map/backward_and_sum/pallas_call | solution.py:2032
  529.8 7.3 %finish_outputs.1 = (bf16[2,384,768]{2,1,0:T(8,128)(2,1)}, bf16[2,384,768]{2,1,0:T(8,128)(2,1)}, f32[144,768]{1,0:T(8,128)}, f32[48,768]{1,0:T(8,128)}, f32[768,...) custom-call(bf16[144,768]{1,0:T(8,128)(2,1)} %get-tuple-element.79.r, ...), custom_call_target="tpu_custom_call" | custom-call | tf_op jit(solution)/shard_map/finish_outputs/pallas_call | solution.py:2087
  (1 shorter events, 0.0 us)
Async XLA Ops:
  2.2 1.7 copy-start.1
  3.1 278.0 %copy-start = (f32[1,1,2,1,384,2]{5,4,2,3,1,0:T(8,128)}, f32[1,1,2,1,384,2]{5,4,2,3,1,0:T(8,128)S(1)}, u32[]{:S(2)}) copy-start(f32[1,1,2,1,384,2]{5,4,2,3,1,0:T(8,128)S(1)} %copy.28) | copy-start | bytes 18436

commit v6 on v5

--- a/solution.py
+++ b/solution.py
@@ -832,8 +832,8 @@
                 for z in (place.z - 1 - step, place.z + 1 + step):
                     pl.when(place.on_line(z))(lambda d=d, z=z: d.cross(z))
 
-        def late_hop(step):
-            for d in late:
+        def late_hop(step, which=late):
+            for d in which:
                 d.hop(step)
 
         heads = 2 * local_count + 1
@@ -850,6 +850,7 @@
                 spots += [(local, here - 1) for local in range(1, local_count)]
                 spots += [(local, here + 1) for local in range(1, local_count)] * 2
                 late_spot, cross_spot = here + 5, here + 7
+                after_item.append((here + 3, lambda step=step: late_hop(step, late[:1])))
                 kinds = {}
                 for local, at in spots:
                     kind = kinds.get(local, 0)
@@ -866,7 +867,8 @@
                 for local in range(local_count):
                     at = spots[min(local, 1)]
                     after_item.append((at, lambda p=(local, step): experts.hop(*p)))
-            after_item.append((late_spot, lambda step=step: late_hop(step)))
+            rest = late[1:] if step == depth - 2 else late
+            after_item.append((late_spot, lambda p=(step, rest): late_hop(*p)))
             after_item.append((cross_spot, lambda step=step: crossing(step)))
         after_item.append((heads + in_step - 3, lambda: send_sums(0)))
         after_item.append((heads + in_step - 1, lambda: send_sums(1)))
@@ -927,6 +929,9 @@
         lax.fori_loop(0, count, item, 0)
         for copy in side_sums():
             copy.start()
+        for d in late:
+            d.drain()
+        experts.drain()
         for local in range(local_count):
             targets = [expert_slab(ref, k, local, 0, width) for k, ref in enumerate((geg_o, geu_o, ged_o))]
             for copy in chunk_stores(targets, local):
@@ -946,9 +951,6 @@
             copy.wait()
     pl.when(beside_end)(sums_arrived)
     pl.when(at_end)(sums_sent)
-    for d in late:
-        d.drain()
-    experts.drain()
 
 
 def rope_tables(prompt):
@@ -1471,7 +1473,7 @@
     depth, high_count = sizes
     owners = place.owners
     (
-        tokens, cot, gates, routes, gate_rows, cosine, sine_part,
+        tokens, cot, gates, routes, cosine, sine_part,
         qkv_w, out_w, gain_v, n1_i, k_i, v_i, q_i, att_i, hid_i, lse_i, side_i, dn2_i,
         gsg, gsu, gsd, geg, geu, ged, outs_i, dins_i, pre_g, pre_u, pre_d,
         mixed_o, input_o, gqkv_o, gout_o, gsg_o, gsu_o, gsd_o, geg_o, geu_o, ged_o, gain_o,
@@ -1671,10 +1673,10 @@
         for direction in (1, -1):
             prompts[m].pass_on(direction, step, lambda t, s: add_into(t, [s], 64))
 
-    def experts_on(step, local, where=True):
+    def experts_on(step, local, where=True, kinds=(0, 1, 2)):
         def body():
             for direction in (1, -1):
-                experts.pass_on(direction, step, local)
+                experts.pass_on(direction, step, local, kinds)
 
         pl.when(where)(body)
 
@@ -1690,6 +1692,7 @@
         load_wq.start()
         lane = lax.broadcasted_iota(jnp.int32, (PB, 2 * HD), 1)
         wide_lane = lax.broadcasted_iota(jnp.int32, (rows, 2 * HD), 1)
+        pairs = features // (2 * HD)
         ds_s[...] = jnp.zeros_like(ds_s)
         p_s[...] = jnp.zeros_like(p_s)
         for m in range(micro_count):
@@ -1697,6 +1700,14 @@
             whole = pl.ds(m * rows, rows)
 
             def pair(index, carry):
+                for kind in range(3):
+
+                    def pass_some(kind=kind):
+                        experts_on(depth - 2, m, experts.at_end, (kind,))
+                        if m == 0:
+                            experts_on(depth - 2, 1, inside, (kind,))
+
+                    pl.when(index == min(2 * kind + 1, pairs - 1))(pass_some)
                 lanes = pl.ds(pl.multiple_of(index * 2 * HD, 2 * HD), 2 * HD)
                 for i in range(rows // PB):
                     here = pl.ds(i * PB, PB)
@@ -1738,7 +1749,7 @@
                 dpv[keys_here, lanes] = d_value.astype(BF)
                 return carry
 
-            lax.fori_loop(0, features // (2 * HD), pair, 0)
+            lax.fori_loop(0, pairs, pair, 0)
             if m == 0:
                 load_wq.wait()
             key_w, value_w = wq[pl.ds(features, features), :], wq[pl.ds(2 * features, features), :]
@@ -1757,9 +1768,7 @@
                     + mdot(dpv[here, :], value_w)
                 )
             fetch([(dn1, dn1_o.at[m])])
-            experts_on(depth - 2, m, experts.at_end)
             if m == 0:
-                experts_on(depth - 2, 1, inside)
                 for d in early:
                     d.add_high()
                 both_ways(early, depth - 1)
@@ -1808,11 +1817,14 @@
     for d in late:
         d.start()
 
-    for step in range(depth - 2, 1, -1):
-        for m in range(micro_count):
-            prompts_on(m, step)
     for d in late:
         d.add_low()
+
+    def column_of(values):
+        dims = (values.shape[1], values.shape[1])
+        across = lax.broadcasted_iota(jnp.int32, dims, 1)
+        diagonal = lax.broadcasted_iota(jnp.int32, dims, 0) == across
+        return jnp.sum(jnp.where(diagonal, values, 0.0), -1, keepdims=True)
 
     def outputs(hidden, side, back, first, second):
         for m in range(micro_count):
@@ -1821,11 +1833,15 @@
             fetch_returned(outs_i, ret_out, ro_recv, back, m)
             for i in range(rows // PB):
                 here = pl.ds(i * PB, PB)
-                routed = gate_rows[m, here, 0:1] * tdot(first[:, here], back[...])
-                routed += gate_rows[m, here, 1:2] * tdot(second[:, here], back[...])
+                routed = column_of(gates[m, 0:1, here]) * tdot(first[:, here], back[...])
+                routed += column_of(gates[m, 1:2, here]) * tdot(second[:, here], back[...])
                 out_rows[here, :] = (hidden[here, :] + side[here, :] + routed).astype(BF)
             fetch([(out_rows, mixed_o.at[m])])
             if m == 0:
+                for step in range(depth - 2, 1, -1):
+                    for n in range(micro_count):
+                        prompts_on(n, step)
+                    both_ways(early, step)
                 for step in range(depth - 3, 0, -1):
                     experts_on(step, 0)
 
@@ -1850,7 +1866,6 @@
     for m in range(micro_count):
         prompts_on(m, 1)
     for step in range(depth - 2, 1, -1):
-        both_ways(early, step)
         both_ways(late, step)
     both_ways(early, 1)
     last_on(0)
@@ -1887,11 +1902,6 @@
         pltpu.VMEM((rows, features), F32),
         pltpu.VMEM((rows, features), F32),
     )
-    both_ways(late, 1)
-    last_on(2)
-    for d in early:
-        d.end()
-
     def gain_copies(first, targets, lands):
         return [
             remote(gain_own, land, gain_send.at[first + i], gain_recv.at[first + i], **target)
@@ -1929,9 +1939,16 @@
             copy.start()
         return copies
 
-    for i in range(2):
-        gain_add(gain_start(i), stages[i][2])
-    line_copies = gain_start(2)
+    copies = gain_start(0)
+    both_ways(late, 1)
+    gain_add(copies, stages[0][2])
+    copies = gain_start(1)
+    last_on(2)
+    gain_add(copies, stages[1][2])
+    copies = gain_start(3)
+    for d in early:
+        d.end()
+
     experts.end(0)
     for d in dense:
         d.drain_first()
@@ -1939,17 +1956,17 @@
         for step in range(1, owners):
             for entry in returns:
                 hand_back(*entry, m, step).wait_send()
+    gain_add(copies, stages[3][2])
+    copies = gain_start(2)
     for d in late:
         d.end()
-    gain_add(line_copies, stages[2][2])
-    cross_copies = gain_start(3)
+    for local in range(1, local_count):
+        experts.end(local)
     for d in early:
         d.finish()
     for d in late:
         d.finish()
-    for local in range(1, local_count):
-        experts.end(local)
-    gain_add(cross_copies, stages[3][2])
+    gain_add(copies, stages[2][2])
     fetch([(gain_own, gain_o)])
     for d in dense:
         d.drain()
@@ -1958,7 +1975,7 @@
         p.drain()
 
 
-def run_backward(sizes, tokens, cot, gates, routes, gate_rows, forward):
+def run_backward(sizes, tokens, cot, gates, routes, forward):
     depth, high_count = sizes
     micro_count, rows, features = tokens.shape
     owners = high_count * 2
@@ -2032,14 +2049,14 @@
     return pl.pallas_call(
         functools.partial(backward_kernel, sizes),
         out_shape=out_shape,
-        in_specs=[hbm] * 2 + [vmem] * 5 + [hbm] * 2 + [vmem] + [hbm] * 20,
+        in_specs=[hbm] * 2 + [vmem] * 4 + [hbm] * 2 + [vmem] + [hbm] * 20,
         out_specs=[hbm] * len(out_shape),
         scratch_shapes=scratch,
         compiler_params=pltpu.CompilerParams(
             collective_id=1, has_side_effects=True, vmem_limit_bytes=60 * MIB
         ),
         name="backward_and_sum",
-    )(tokens, cot, gates, routes, gate_rows, cosine, sine_part, *forward)
+    )(tokens, cot, gates, routes, cosine, sine_part, *forward)
 
 
 def finish_kernel(count, gain_width, *refs):
@@ -2481,8 +2498,8 @@
         jnp.zeros((16, features), jnp.bfloat16), gains, (0, own_at * gain_width)
     )
     rows, cot = tokens[0, 0, :, 0], cotangent[0, 0, :, 0]
-    gate_rows, route_rows = gates[0, 0, :, 0], routes[0, 0, :, 0]
-    gate_columns, route_columns = gate_rows.transpose(0, 2, 1), route_rows.transpose(0, 2, 1)
+    gate_columns = gates[0, 0, :, 0].transpose(0, 2, 1)
+    route_columns = routes[0, 0, :, 0].transpose(0, 2, 1)
     forward = run_forward(
         sizes,
         rows,
@@ -2496,7 +2513,7 @@
         mixed, input_grad, grad_qkv, grad_out, grad_sgate, grad_sup, grad_sdown,
         grad_egate, grad_eup, grad_edown, gain_sum, *_,
     ) = run_backward(
-        sizes, rows, cot, gate_columns, route_columns, gate_rows, forward[:3] + forward[9:]
+        sizes, rows, cot, gate_columns, route_columns, forward[:3] + forward[9:]
     )
     mixed, input_grad, grad_qkv, *rest = finish_outputs(
         (grad_qkv, grad_out, grad_sgate, grad_sup, grad_sdown, grad_egate, grad_eup, grad_edown),

time: 548 us -> 544 us (level)
  no operation moved by 1% of the time
where the time goes in v6:
time: 544 us; the launch traced here: 533 us
  Pallas kernels  530 us (97%)
    pallas_call x1, Pallas kernels, run_forward(): pl.pallas_call(functools.partial(forward_kernel, sizes), out_shape=out_sh...  273 us
    pallas_call x1, Pallas kernels, run_backward(): pl.pallas_call(functools.partial(backward_kernel, sizes), out_shape=out_s...  250 us

profile of v6, /device:TPU:0, one launch (start us, length us, event | category | flops | bytes accessed | tf_op | source)
XLA Modules:
  0.0 533.3 jit_solution(4800008377249605098)
XLA Ops:
  0.7 1.5 dynamic_update_slice.3.refs_8_
  2.2 0.0 copy-start
  2.2 0.6 copy-done
  2.8 273.1 %gather_and_forward.1 = (bf16[2304,768]{1,0:T(8,128)(2,1)}, bf16[768,768]{1,0:T(8,128)(2,1)}, f32[8,768]{1,0:T(8,128)}, bf16[768,2048]{1,0:T(8,128)(2,1)}, bf16[...) custom-call(bf16[2,384,768]{2,1,0:T(8,128)(2,1)} %bitcast.16, ...), custom_call_target="tpu_custom_call" | custom-call | tf_op jit(solution)/shard_map/gather_and_forward/pallas_call | solution.py:1051
  275.9 249.8 %backward_and_sum.1 = (bf16[2,384,768]{2,1,0:T(8,128)(2,1)}, bf16[2,384,768]{2,1,0:T(8,128)(2,1)}, bf16[144,768]{1,0:T(8,128)(2,1)}, bf16[48,768]{1,0:T(8,128)(2...) custom-call(bf16[2,384,768]{2,1,0:T(8,128)(2,1)} %bitcast.17, ...), custom_call_target="tpu_custom_call" | custom-call | tf_op jit(solution)/shard_map/backward_and_sum/pallas_call | solution.py:2049
  525.7 7.3 %finish_outputs.1 = (bf16[2,384,768]{2,1,0:T(8,128)(2,1)}, bf16[2,384,768]{2,1,0:T(8,128)(2,1)}, f32[144,768]{1,0:T(8,128)}, f32[48,768]{1,0:T(8,128)}, f32[768,...) custom-call(bf16[144,768]{1,0:T(8,128)(2,1)} %get-tuple-element.79.r, ...), custom_call_target="tpu_custom_call" | custom-call | tf_op jit(solution)/shard_map/finish_outputs/pallas_call | solution.py:2104
  (1 shorter events, 0.0 us)
Async XLA Ops:
  2.2 0.6 copy-start

commit v7 on v6

--- a/solution.py
+++ b/solution.py
@@ -1958,10 +1958,10 @@
                 hand_back(*entry, m, step).wait_send()
     gain_add(copies, stages[3][2])
     copies = gain_start(2)
+    for local in range(1, local_count):
+        experts.end(local)
     for d in late:
         d.end()
-    for local in range(1, local_count):
-        experts.end(local)
     for d in early:
         d.finish()
     for d in late:

time: 544 us -> 549 us (level)
  the two profiles are of different devices: /device:TPU:0 before, /device:TPU:18 now
where the time goes in v7:
time: 549 us; the launch traced here: 539 us
  Pallas kernels  536 us (98%)
    pallas_call x1, Pallas kernels, run_forward(): pl.pallas_call(functools.partial(forward_kernel, sizes), out_shape=out_sh...  264 us
    pallas_call x1, Pallas kernels, run_backward(): pl.pallas_call(functools.partial(backward_kernel, sizes), out_shape=out_s...  264 us

profile of v7, /device:TPU:18, one launch (start us, length us, event | category | flops | bytes accessed | tf_op | source)
XLA Modules:
  0.0 538.8 jit_solution(15835783816536206039)
XLA Ops:
  0.7 1.5 dynamic_update_slice.3.refs_8_
  2.2 0.0 copy-start
  2.2 0.6 copy-done
  2.8 264.4 %gather_and_forward.1 = (bf16[2304,768]{1,0:T(8,128)(2,1)}, bf16[768,768]{1,0:T(8,128)(2,1)}, f32[8,768]{1,0:T(8,128)}, bf16[768,2048]{1,0:T(8,128)(2,1)}, bf16[...) custom-call(bf16[2,384,768]{2,1,0:T(8,128)(2,1)} %bitcast.16, ...), custom_call_target="tpu_custom_call" | custom-call | tf_op jit(solution)/shard_map/gather_and_forward/pallas_call | solution.py:1051
  267.2 263.9 %backward_and_sum.1 = (bf16[2,384,768]{2,1,0:T(8,128)(2,1)}, bf16[2,384,768]{2,1,0:T(8,128)(2,1)}, bf16[144,768]{1,0:T(8,128)(2,1)}, bf16[48,768]{1,0:T(8,128)(2...) custom-call(bf16[2,384,768]{2,1,0:T(8,128)(2,1)} %bitcast.17, ...), custom_call_target="tpu_custom_call" | custom-call | tf_op jit(solution)/shard_map/backward_and_sum/pallas_call | solution.py:2049
  531.1 7.3 %finish_outputs.1 = (bf16[2,384,768]{2,1,0:T(8,128)(2,1)}, bf16[2,384,768]{2,1,0:T(8,128)(2,1)}, f32[144,768]{1,0:T(8,128)}, f32[48,768]{1,0:T(8,128)}, f32[768,...) custom-call(bf16[144,768]{1,0:T(8,128)(2,1)} %get-tuple-element.79.r, ...), custom_call_target="tpu_custom_call" | custom-call | tf_op jit(solution)/shard_map/finish_outputs/pallas_call | solution.py:2104
  (1 shorter events, 0.0 us)
Async XLA Ops:
  2.2 0.6 copy-start
